TPU v7x, 256 devices: a whole 4x4x8 slice. The times are simulated.
256 devices in a mesh: ctx: 64 (over x, y, z_lo, core), tp: 4 (over z_hi).
Axes of the slice: x: 4, y: 4, z: 8 (z_hi: 4, z_lo: 2; z = z_hi * 2 + z_lo), core: 2. Of those that a mesh axis runs over, the one named last changes fastest.
Arguments:
- hidden: bfloat16 [1, 16384, 8192], P(None, 'ctx', 'tp'), may hold values from -6 to 6
- doc_lengths: int32 [1, 128], replicated, may hold values from 1 to 512, 16384 in all within a row
- gain_se: float32 [8192], P('tp'), may hold values from 0.5 to 1.5
- gain_mr: float32 [8192], P('tp'), may hold values from 0.5 to 1.5
- feat_se: float32 [3, 3, 8192], P(None, None, 'tp'), may hold values from -4 to 4
- feat_mr: float32 [3, 3, 8192], P(None, None, 'tp'), may hold values from -4 to 4
- filter_se: float32 [512, 7], P('tp'), may hold values from -3 to 3
- filter_mr: bfloat16 [512, 128], P('tp'), may hold values from -0.5 to 0.5
Outputs:
- output: bfloat16 [1, 16384, 8192], P(None, 'ctx', 'tp')
Inputs may be any that keep to these rules, and one draw needn't show every extreme that they name: `doc_lengths`: each row lists document lengths that sum to 16384; the longest is exactly 512.
All inputs are finite; a program needn't handle non-finite values.
Results may differ from a plain program's by a relative error of at most 0.03.
Values may be sent and summed in bfloat16 or wider, within the bound.
No kernel may reach another device: no remote copies, remote signals or barrier semaphores. Data moves between devices by JAX's collectives and lax.ppermute only.
A program may use at most 128 MiB of HBM per device.

v0:
```python
import jax
import jax.numpy as jnp
from jax import lax
from jax.sharding import PartitionSpec as P

D = 8192
FEAT_TAPS = 3
SHORT_TAPS = 7
MEDIUM_TAPS = 128


norm_epsilon = 1e-06


def shifted(x, axis, by):
    peers = lax.axis_size(axis)
    pairs = [(i, i + by) for i in range(peers) if 0 <= i + by < peers]
    return lax.ppermute(x, axis, pairs)


def doc_offsets(doc_lengths, positions):
    doc_ends = jnp.cumsum(doc_lengths, axis=-1, dtype=jnp.int32)
    doc_starts = doc_ends - doc_lengths
    starts_before = doc_starts[:, None, :] <= positions[None, :, None]
    doc_first = jnp.max(jnp.where(starts_before, doc_starts[:, None, :], 0), axis=-1)
    return positions[None, :] - doc_first


def delayed(inputs, shift_by):
    if shift_by == 0:
        return inputs
    zero_rows = jnp.zeros(inputs.shape[:1] + (shift_by,) + inputs.shape[2:], inputs.dtype)
    return jnp.concatenate([zero_rows, inputs[:, : inputs.shape[1] - shift_by]], axis=1)


def scaled(inputs, square_sums, gain):
    return (inputs * lax.rsqrt(square_sums / D + norm_epsilon)[..., None] * gain).astype(
        jnp.bfloat16
    )


def featurize(normed, taps, offsets):
    inputs = normed.astype(jnp.float32)
    streams = []
    for stream_index in range(3):
        running = jnp.zeros(inputs.shape, jnp.float32)
        for tap_lag in range(FEAT_TAPS):
            keep_mask = (offsets >= tap_lag).astype(jnp.float32)[:, :, None]
            running = running + taps[stream_index, tap_lag] * delayed(inputs, tap_lag) * keep_mask
        streams.append(running)
    return streams


def short_conv(product, filters, offsets):
    group_count, tap_count = filters.shape
    group_size = product.shape[2] // group_count
    per_channel = jnp.broadcast_to(
        filters[:, None, :], (group_count, group_size, tap_count)
    ).reshape(group_count * group_size, tap_count)
    running = jnp.zeros(product.shape, jnp.float32)
    for tap_lag in range(SHORT_TAPS):
        keep_mask = (offsets >= tap_lag).astype(jnp.float32)[:, :, None]
        running = running + per_channel[:, tap_lag] * delayed(product, tap_lag) * keep_mask
    return running


def band_table(filters, tap_lag):
    in_range = (tap_lag >= 0) & (tap_lag < MEDIUM_TAPS)
    table = filters[:, jnp.clip(tap_lag, 0, MEDIUM_TAPS - 1)]
    return jnp.where(in_range[None], table, jnp.zeros((), filters.dtype))


def long_conv(mixed, filters, offsets):
    seq_count, padded_rows, local_width = mixed.shape
    seq_length = padded_rows - MEDIUM_TAPS
    group_count = filters.shape[0]
    group_size = local_width // group_count
    block_rows = 128
    tap_lag = (
        jnp.arange(block_rows, dtype=jnp.int32)[:, None]
        + MEDIUM_TAPS
        - jnp.arange(block_rows + MEDIUM_TAPS, dtype=jnp.int32)[None, :]
    )
    toeplitz = band_table(filters, tap_lag)
    block_count = seq_length // block_rows

    def one_block(item_index):
        seq_index = item_index // block_count
        block_index = item_index % block_count
        window_rows = lax.dynamic_slice(
            mixed,
            (seq_index, block_index * block_rows, jnp.int32(0)),
            (1, block_rows + MEDIUM_TAPS, local_width),
        )[0]
        window_rows = window_rows.reshape(block_rows + MEDIUM_TAPS, group_count, group_size)
        block_offsets = lax.dynamic_slice(
            offsets, (seq_index, block_index * block_rows), (1, block_rows)
        )[0]
        keep_mask = (tap_lag <= block_offsets[:, None]).astype(filters.dtype)
        masked_toep = toeplitz * keep_mask[None]
        convolved = jnp.einsum(
            "gts,sgc->tgc", masked_toep, window_rows, preferred_element_type=jnp.float32
        )
        return convolved.reshape(block_rows, local_width)

    blocks = lax.map(one_block, jnp.arange(seq_count * block_count, dtype=jnp.int32))
    return blocks.reshape(seq_count, seq_length, local_width)


def shards(hidden, doc_lengths, gain_se, gain_mr, feat_se, feat_mr, filter_se, filter_mr):
    local_rows = hidden.shape[1]
    first_position = lax.axis_index("ctx") * local_rows
    stream_in = hidden.astype(jnp.float32)
    offsets = doc_offsets(doc_lengths, first_position + jnp.arange(local_rows, dtype=jnp.int32))
    square_sums = lax.psum(jnp.sum(stream_in * stream_in, axis=-1), "tp")
    normed_one = scaled(stream_in, square_sums, gain_se)
    se_reach = FEAT_TAPS - 1 + SHORT_TAPS - 1
    earlier = shifted(normed_one[:, local_rows - se_reach :], "ctx", 1)
    joined_one = jnp.concatenate([earlier, normed_one], axis=1)
    offsets_one = doc_offsets(
        doc_lengths, first_position - se_reach + jnp.arange(local_rows + se_reach, dtype=jnp.int32)
    )
    query_one, key_one, value_one = featurize(joined_one, feat_se, offsets_one)
    branch_one = query_one * short_conv(key_one * value_one, filter_se, offsets_one)
    middle = (stream_in + branch_one[:, se_reach:]).astype(jnp.bfloat16)
    middle_f = middle.astype(jnp.float32)
    second_sums = lax.psum(jnp.sum(middle_f * middle_f, axis=-1), "tp")
    normed_two = scaled(middle_f, second_sums, gain_mr)
    mr_reach = FEAT_TAPS - 1 + MEDIUM_TAPS - 1
    earlier_two = shifted(normed_two[:, local_rows - mr_reach :], "ctx", 1)
    joined_two = jnp.concatenate([earlier_two, normed_two], axis=1)
    offsets_two = doc_offsets(
        doc_lengths, first_position - mr_reach + jnp.arange(local_rows + mr_reach, dtype=jnp.int32)
    )
    query_two, key_two, value_two = featurize(joined_two, feat_mr, offsets_two)
    mixed = (key_two * value_two).astype(jnp.bfloat16)[:, mr_reach - MEDIUM_TAPS :]
    medium = long_conv(mixed, filter_mr, offsets)
    output_f = middle_f + query_two[:, mr_reach:] * medium
    return output_f.astype(jnp.bfloat16)


def solution(mesh):
    in_specs = (
        P(None, "ctx", "tp"),
        P(),
        P("tp"),
        P("tp"),
        P(None, None, "tp"),
        P(None, None, "tp"),
        P("tp", None),
        P("tp", None),
    )
    out_specs = P(None, "ctx", "tp")
    return jax.shard_map(shards, mesh=mesh, in_specs=in_specs, out_specs=out_specs, check_vma=False)
```

profile of v0, /device:TPU:2, one launch (start us, length us, event | category | flops | bytes accessed | tf_op | source)
XLA Modules:
  0.0 234.1 jit_solution(636093015890537372)
XLA Ops:
  0.0 1.5 fusion.7
  1.6 14.9 %psum.14 = f32[1,256]{1,0:T(1,128)S(1)} all-reduce(f32[1,256]{1,0:T(1,128)S(1)} %bitcast.113), channel_id=1, replica_groups=mesh['ctx'=64,'tp'=4] {'tp'}, use_global_device_ids=true, to_apply=%region_1.2 | all-reduce | flops 256 | bytes 2048 | tf_op jit(solution)/shard_map/psum | solution.py:115
  16.5 1.5 fusion.9
  18.1 1.9 collective-permute-start
  20.0 0.1 fusion.35
  20.1 0.1 fusion.38
  20.3 0.3 reduce_window_sum.13
  20.6 0.2 select_reduce_fusion
  20.8 0.1 fusion.43
  20.9 0.2 broadcast_in_dim.45
  21.1 0.3 reshape.1020
  21.4 8.4 %fusion.34 = s32[385]{0:T(512)S(1)} fusion(s32[128]{0:T(128)S(1)} %subtract_bitcast_fusion, s32[385]{0:T(512)S(1)} %iota_add_fusion), kind=kLoop, calls=%fused_computation.65 | loop fusion | flops 147455 | bytes 3592 | tf_op jit(solution)/shard_map/reduce_max | solution.py:25
  29.8 0.1 copy.41
  30.0 0.1 copy.22
  30.1 114.1 %gather_fusion = bf16[32768,128]{1,0:T(8,128)(2,1)} fusion(bf16[128,128]{0,1:T(8,128)(2,1)S(1)} %copy.22, s32[32768]{0:T(1024)S(1)} %broadcast_clamp_fusion), kind=kCustom, calls=%fused_computation | custom fusion | bytes 16908288 | tf_op jit(solution)/shard_map/gather | solution.py:69
  144.2 12.3 %copy.23 = bf16[128,256,128]{1,0,2:T(8,128)(2,1)} copy(bf16[128,256,128]{2,1,0:T(8,128)(2,1)} %bitcast.82) | data formatting | bytes 16777216 | tf_op jit(solution)/shard_map/gather | solution.py:69
  156.5 7.3 %select_bitcast_fusion = bf16[128,128,256]{2,1,0:T(8,128)(2,1)} fusion(bf16[128,256,128]{1,0,2:T(8,128)(2,1)} %copy.23, pred[128,256]{1,0:T(8,128)(4,1)S(1)} %fusion.38), kind=kLoop, calls=%fused_computation.11 | loop fusion | flops 4194304 | bytes 16809984 | tf_op jit(solution)/shard_map/jit(_where)/select_n | solution.py:70
  163.8 0.2 select_reduce_fusion.1
  164.0 0.1 slice.192
  164.0 0.1 slice.193
  164.1 0.1 slice.195
  164.2 0.1 slice.189
  164.3 0.1 slice.191
  164.3 0.1 slice.194
  164.4 0.1 slice.196
  164.5 0.2 maximum_convert_fusion.1
  164.7 1.8 add_multiply_fusion
  166.5 0.3 pad_multiply_fusion
  166.9 0.9 multiply_multiply_fusion
  167.8 0.3 copy-done.3
  168.1 4.3 %fusion.11 = (f32[256]{0:T(256)S(1)}, bf16[1,256,2048]{2,1,0:T(8,128)(2,1)S(1)}) fusion(f32[256]{0:T(256)S(1)} %slice.196, f32[1,258,2048]{2,1,0:T(8,128)S(1)} %bitcast.73, f32[2048]{0:T(1024)S(1)} %bitcast.85, f32[256]{0:T(256)S(1)} %slice.194, f32[1,259,2048]{2,1,0:T(8,128)S(1)} %bitcast.74, f32[2048]{0:T(1024)S(1)} %bitcast.86, f32[256]{0:T(256)S(1)} %slice.191, ...), kind=kLoop, calls=%fused_computation.27 | loop fusion | flops 14155520 | bytes 21209088 | tf_op jit(solution)/shard_map/reduce_sum | solution.py:127
  172.4 10.3 %psum.15 = f32[1,256]{1,0:T(1,128)S(1)} all-reduce(f32[1,256]{1,0:T(1,128)S(1)} %bitcast.110), channel_id=1, replica_groups=mesh['ctx'=64,'tp'=4] {'tp'}, use_global_device_ids=true, to_apply=%region_5.6 | all-reduce | flops 256 | bytes 2048 | tf_op jit(solution)/shard_map/psum | solution.py:127
  182.7 0.3 fusion.13
  183.0 0.9 slice.197
  183.9 1.9 collective-permute-start.1
  185.9 0.1 slice.205
  185.9 0.1 slice.201
  186.0 0.1 slice.206
  186.1 0.1 slice.202
  186.2 0.1 slice.207
  186.2 0.1 slice.203
  186.4 11.6 %collective-permute-done.1 = bf16[1,129,2048]{2,1,0:T(8,128)(2,1)S(1)} collective-permute-done((bf16[1,129,2048]{2,1,0:T(8,128)(2,1)}, bf16[1,129,2048]{2,1,0:T(8,128)(2,1)S(1)}, u32[]{:S(2)}, u32[]{:S(2)}) %collective-permute-start.1) | collective-permute-done | bytes 528416 | tf_op jit(solution)/shard_map/ppermute | solution.py:18
  198.0 0.3 maximum_convert_fusion
  198.4 0.3 slice.198
  198.7 0.3 slice.199
  199.1 1.0 copy-done
  200.1 1.0 copy-done.1
  201.1 4.0 %multiply_convert_fusion = bf16[1,384,2048]{2,1,0:T(8,128)(2,1)} fusion(f32[1,383,2048]{2,1,0:T(8,128)S(1)} %slice.199, f32[1,384,2048]{2,1,0:T(8,128)S(1)} %slice.198, f32[1,385,2048]{2,1,0:T(8,128)S(1)} %maximum_convert_fusion, f32[384]{0:T(512)S(1)} %slice.207, f32[2048]{0:T(1024)S(1)} %bitcast.108, f32[2048]{0:T(1024)S(1)} %bitcast.105, ...), kind=kLoop, calls=%fused_computation.12 | loop fusion | flops 14155776 | bytes 11055616 | tf_op jit(solution)/shard_map/convert_element_type | solution.py:136
  205.1 23.3 %while.13 = (s32[]{:T(128)}, f32[2,128,2048]{2,1,0:T(8,128)}, s32[2]{0:T(128)S(1)}, bf16[1,384,2048]{2,1,0:T(8,128)(2,1)}, s32[1,256]{1,0:T(1,128)S(1)}, /*index...) while((s32[]{:T(128)}, f32[2,128,2048]{2,1,0:T(8,128)}, ...), condition=%wide.region_9.10_spmd.clone, body=%wide.region_8.9_spmd.clone.sunk | while | flops 138510352 | bytes 19008324 | solution.py:106
  205.1 0.6 dynamic_slice.33
  207.7 1.3 constant_dynamic-slice_fusion.3
  209.0 0.5 copy.44
  209.5 0.1 fusion.54
  209.6 5.7 %fusion.55 = f32[128,16,128]{2,1,0:T(8,128)S(1)} fusion(bf16[256,128,16]{0,2,1:T(8,128)(2,1)S(1)} %bitcast.76, bf16[128,128,256]{2,1,0:T(8,128)(2,1)} %get-tuple-element.268, bf16[128,256]{1,0:T(8,128)(2,1)S(1)} %fusion.54), kind=kOutput, calls=%fused_computation.2.clone.1 | convolution fusion | flops 138412032 | bytes 10551296 | tf_op jit(solution)/shard_map/while/body/eval_jaxpr/gts,sgc->tgc/dot_general | solution.py:101
  215.3 0.3 copy.45
  215.7 1.1 constant_dynamic-update-slice_fusion.2
  216.7 0.6 dynamic_slice.33
  219.3 1.3 constant_dynamic-slice_fusion.3
  220.6 0.5 copy.44
  221.1 0.1 fusion.54
  221.3 5.7 %fusion.55 = f32[128,16,128]{2,1,0:T(8,128)S(1)} fusion(bf16[256,128,16]{0,2,1:T(8,128)(2,1)S(1)} %bitcast.76, bf16[128,128,256]{2,1,0:T(8,128)(2,1)} %get-tuple-element.268, bf16[128,256]{1,0:T(8,128)(2,1)S(1)} %fusion.54), kind=kOutput, calls=%fused_computation.2.clone.1 | convolution fusion | flops 138412032 | bytes 10551296 | tf_op jit(solution)/shard_map/while/body/eval_jaxpr/gts,sgc->tgc/dot_general | solution.py:101
  226.9 0.3 copy.45
  227.3 1.1 constant_dynamic-update-slice_fusion.2
  228.4 5.7 %fusion.14 = bf16[1,256,2048]{2,1,0:T(8,128)(2,1)} fusion(bf16[1,256,2048]{2,1,0:T(8,128)(2,1)S(1)} %get-tuple-element.156, f32[1,383,2048]{2,1,0:T(8,128)} %copy-done.2, f32[1,384,2048]{2,1,0:T(8,128)} %copy-done.1, f32[1,385,2048]{2,1,0:T(8,128)} %copy-done, f32[256]{0:T(256)S(1)} %slice.203, f32[2048]{0:T(1024)S(1)} %bitcast.93, f32[256]{0:T(256)S(1)} %slice.202, ...), kind=kLoop, calls=%fused_computation.30 | loop fusion | flops 6291456 | bytes 12602368 | tf_op jit(solution)/shard_map/convert_element_type | solution.py:139
  (36 shorter events, 0.2 us)
Async XLA Ops:
  0.0 20.2 %copy-start.9 = (s32[1,128]{1,0:T(1,128)S(1)}, s32[1,128]{1,0:T(1,128)}, u32[]{:S(2)}) copy-start(s32[1,128]{1,0:T(1,128)} %param.11) | copy-start | bytes 1540
  0.0 20.8 %copy-start.4 = (f32[3,3,2048]{2,1,0:T(4,128)S(1)}, f32[3,3,2048]{2,1,0:T(4,128)}, u32[]{:S(2)}) copy-start(f32[3,3,2048]{2,1,0:T(4,128)} %param.14) | copy-start | bytes 221188
  0.0 20.9 %copy-start.8 = (f32[128,7]{0,1:T(8,128)S(1)}, f32[128,7]{0,1:T(8,128)}, u32[]{:S(2)}) copy-start(f32[128,7]{0,1:T(8,128)} %param.16) | copy-start | bytes 10756
  1.6 28.4 %copy-start.6 = (bf16[128,128]{1,0:T(8,128)(2,1)S(1)}, bf16[128,128]{1,0:T(8,128)(2,1)}, u32[]{:S(2)}) copy-start(bf16[128,128]{1,0:T(8,128)(2,1)} %param.17) | copy-start | bytes 98308
  18.1 146.4 %collective-permute-start = (bf16[1,8,2048]{2,1,0:T(8,128)(2,1)S(1)}, bf16[1,8,2048]{2,1,0:T(8,128)(2,1)S(1)}, u32[]{:S(2)}, u32[]{:S(2)}) collective-permute-start(bf16[1,8,2048]{2,1,0:T(8,128)(2,1)S(1)} %slice.170), channel_id=1, source_target_pairs={{0,4},{4,8},{8,12},{12,16},{16,20},{20,24},{24,28},{28,32},{32,36}... | collective-permute-start | bytes 98312 | tf_op jit(solution)/shard_map/ppermute | solution.py:18
  166.9 1.2 copy-start.3
  168.1 14.6 %copy-start.7 = (f32[2048]{0:T(1024)S(1)}, f32[2048]{0:T(1024)}, u32[]{:S(2)}) copy-start(f32[2048]{0:T(1024)} %param.13) | copy-start | bytes 24580
  172.4 13.9 %copy-start.5 = (f32[3,3,2048]{2,1,0:T(4,128)S(1)}, f32[3,3,2048]{2,1,0:T(4,128)}, u32[]{:S(2)}) copy-start(f32[3,3,2048]{2,1,0:T(4,128)} %param.15) | copy-start | bytes 221188
  183.9 14.1 %collective-permute-start.1 = (bf16[1,129,2048]{2,1,0:T(8,128)(2,1)}, bf16[1,129,2048]{2,1,0:T(8,128)(2,1)S(1)}, u32[]{:S(2)}, u32[]{:S(2)}) collective-permute-start(bf16[1,129,2048]{2,1,0:T(8,128)(2,1)} %slice.197), channel_id=1, source_target_pairs={{0,4},{4,8},{8,12},{12,16},{16,20},{20,24},{24,28},{28,32},{32,36}... | collective-permute-start | bytes 1585160 | tf_op jit(solution)/shard_map/ppermute | solution.py:18
  198.4 1.8 copy-start
  198.7 2.4 %copy-start.1 = (f32[1,384,2048]{2,1,0:T(8,128)}, f32[1,384,2048]{2,1,0:T(8,128)S(1)}, u32[]{:S(2)}) copy-start(f32[1,384,2048]{2,1,0:T(8,128)S(1)} %slice.198) | copy-start | bytes 9437188
  199.1 6.1 %copy-start.2 = (f32[1,383,2048]{2,1,0:T(8,128)}, f32[1,383,2048]{2,1,0:T(8,128)S(1)}, u32[]{:S(2)}) copy-start(f32[1,383,2048]{2,1,0:T(8,128)S(1)} %slice.199) | copy-start | bytes 9412612
where the time goes:
time: 235 us; the launch traced here: 234 us
  local copies, waits for them, and re-layouts  140 us (60%)
  other arithmetic  37.9 us (16%)
  blocking collectives  25.2 us (11%)
  waiting for transfers between devices  11.6 us (5%)
  matrix products  11.3 us (5%)
  loops' own time  4.01 us (2%)
  starting transfers between devices  3.83 us (2%)
    gather x2, local copies, waits for them, and re-layouts, band_table(): table = filters[:, jnp.clip(tap_lag, 0, MEDIUM_TAPS - 1)]  126 us
    psum x1, blocking collectives, shards(): square_sums = lax.psum(jnp.sum(stream_in * stream_in, axis=-1), 'tp')  14.9 us
    ppermute x2, waiting for transfers between devices, shifted(): return lax.ppermute(x, axis, pairs)  11.6 us
    dot_general x2, matrix products, one_block(): jnp.einsum('gts,sgc->tgc', masked_toep, window_rows, preferred_element_ty...  11.3 us
    psum x1, blocking collectives, shards(): second_sums = lax.psum(jnp.sum(middle_f * middle_f, axis=-1), 'tp')  10.3 us
    reduce_max x3, other arithmetic, doc_offsets(): jnp.max(jnp.where(starts_before, doc_starts[:, None, :], 0), axis=-1)  8.83 us
    select_n x1, other arithmetic, band_table(): return jnp.where(in_range[None], table, jnp.zeros((), filters.dtype))  7.29 us
    convert_element_type x1, other arithmetic, shards(): return output_f.astype(jnp.bfloat16)  5.69 us
  transfers between devices with their start and end apart: 2, of which 1 were waited for; matrix products, arithmetic and copies ran while one was open for 62% of the time, Pallas kernels for 0%

commit v1 on v0

v1 whole, which is shorter than its diff:
```python
import jax
import jax.numpy as jnp
from jax import lax
from jax.experimental import pallas as pl
from jax.experimental.pallas import tpu as pltpu
from jax.sharding import PartitionSpec as P

D = 8192
FEAT_TAPS = 3
SHORT_TAPS = 7
MEDIUM_TAPS = 128
HALO = 144
LANES = 128
GROUP = 16
CHUNK = 16
PAD = 8

norm_epsilon = 1e-06
VMEM_LIMIT = 48 * 1024 * 1024


def shifted(x, axis, by):
    peers = lax.axis_size(axis)
    pairs = [(i, i + by) for i in range(peers) if 0 <= i + by < peers]
    return lax.ppermute(x, axis, pairs)


def as_row(column):
    rows = column.shape[0]
    return jnp.broadcast_to(column, (rows, LANES)).T[0:1]


def as_column(row):
    return jnp.broadcast_to(row, (LANES, row.shape[1])).T


def sums_kernel(x_ref, s_ref):
    rows, width = x_ref.shape
    for r in range(0, rows, 64):
        total = jnp.zeros((64, LANES), jnp.float32)
        for c in range(0, width, LANES):
            x = x_ref[r : r + 64, c : c + LANES].astype(jnp.float32)
            total = total + x * x
        col = jnp.sum(total, axis=1, keepdims=True)
        if r % 128 == 0:
            held = col
        else:
            s_ref[0:1, r - 64 : r + 64] = as_row(jnp.concatenate([held, col], axis=0))


def prep_kernel(first_ref, len_ref, fse_ref, fmr_ref, off_ref, fexp_ref, base_ref, rev_ref):
    ext = off_ref.shape[0]
    width = fexp_ref.shape[1]
    groups = fmr_ref.shape[0]
    lens = jnp.broadcast_to(len_ref[0:1, :].astype(jnp.float32), (8, LANES))
    lane = lax.broadcasted_iota(jnp.int32, (8, LANES), 1)
    ends = lens
    step = 1
    while step < LANES:
        ends = ends + jnp.where(lane >= step, pltpu.roll(ends, step, 1), 0.0)
        step *= 2
    starts = (ends - lens)[0:1]
    first = first_ref[0] - HALO
    for r in range(0, ext, CHUNK):
        pos = (lax.broadcasted_iota(jnp.int32, (CHUNK, LANES), 0) + (first + r)).astype(jnp.float32)
        doc_first = jnp.max(jnp.where(starts <= pos, starts, 0.0), axis=1, keepdims=True)
        off_ref[r : r + CHUNK, :] = pos - doc_first
    fse = fse_ref[...]
    for c in range(0, width, LANES):
        row = lax.broadcasted_iota(jnp.int32, (groups, LANES), 0)
        col = lax.broadcasted_iota(jnp.int32, (groups, LANES), 1)
        spread = (row == (c + col) // GROUP).astype(jnp.float32)
        fexp_ref[:, c : c + LANES] = jnp.dot(
            fse, spread, preferred_element_type=jnp.float32, precision=lax.Precision.HIGHEST
        )
    row = lax.broadcasted_iota(jnp.int32, (LANES, LANES), 0)
    col = lax.broadcasted_iota(jnp.int32, (LANES, LANES), 1)
    flip = ((row + col) % MEDIUM_TAPS == 0).astype(jnp.bfloat16)
    rev_ref[...] = jnp.dot(fmr_ref[...], flip, preferred_element_type=jnp.float32)

    def one(g, carry):
        h = jnp.broadcast_to(rev_ref[pl.ds(g, 1), :], (GROUP, LANES))
        base_ref[g] = pltpu.roll(h, 0, 1, stride=1, stride_axis=0)
        return carry

    lax.fori_loop(0, groups, one, 0, unroll=8)


def scale_columns(sums_ref, scale_ref):
    tp = sums_ref.shape[0]
    total = sums_ref[0]
    for i in range(1, tp):
        total = total + sums_ref[i]
    scale = lax.rsqrt(total / D + norm_epsilon)
    own = scale.shape[1]
    scale_ref[0:HALO, :] = as_column(scale[0:1])[own - HALO :, :]
    scale_ref[HALO:, :] = as_column(scale[1:2])


def masks_of(off_ref, mask_ref, taps):
    for r in range(0, off_ref.shape[0], CHUNK):
        off = off_ref[r : r + CHUNK, :]
        for j in range(1, taps):
            mask_ref[j - 1, r : r + CHUNK, :] = (off >= j).astype(jnp.float32)


def se_kernel(
    x_ref, halo_ref, sums_ref, off_ref, gain_ref, feat_ref, fexp_ref, mid_ref, s_ref,
    scale_ref, mask_ref, norm_ref, prod_ref, q_ref, acc_ref,
):
    own, width = x_ref.shape
    ext = HALO + own
    scale_columns(sums_ref, scale_ref)
    masks_of(off_ref, mask_ref, SHORT_TAPS)
    norm_ref[0:PAD, :] = jnp.zeros((PAD, LANES), jnp.float32)
    prod_ref[0:PAD, :] = jnp.zeros((PAD, LANES), jnp.float32)
    acc_ref[...] = jnp.zeros(acc_ref.shape, jnp.float32)

    def raw(e, cols):
        if e < HALO:
            return halo_ref[e : e + CHUNK, cols].astype(jnp.float32)
        return x_ref[e - HALO : e - HALO + CHUNK, cols].astype(jnp.float32)

    def tile(i, carry):
        cols = pl.ds(pl.multiple_of(i * LANES, LANES), LANES)
        gain = gain_ref[0:1, cols]
        for e in range(0, ext, CHUNK):
            n = raw(e, cols) * scale_ref[e : e + CHUNK, :] * gain
            norm_ref[PAD + e : PAD + e + CHUNK, :] = n.astype(jnp.bfloat16).astype(jnp.float32)
        taps = [[feat_ref[s, j : j + 1, cols] for j in range(FEAT_TAPS)] for s in range(3)]
        for e in range(0, ext, CHUNK):
            xs = [norm_ref[PAD + e : PAD + e + CHUNK, :]]
            for j in range(1, FEAT_TAPS):
                xs.append(norm_ref[PAD + e - j : PAD + e - j + CHUNK, :] * mask_ref[j - 1, e : e + CHUNK, :])
            q, k, v = (
                taps[s][0] * xs[0] + taps[s][1] * xs[1] + taps[s][2] * xs[2] for s in range(3)
            )
            prod_ref[PAD + e : PAD + e + CHUNK, :] = k * v
            q_ref[e : e + CHUNK, :] = q
        filt = [fexp_ref[j : j + 1, cols] for j in range(SHORT_TAPS)]
        for e in range(0, ext, CHUNK):
            total = filt[0] * prod_ref[PAD + e : PAD + e + CHUNK, :]
            for j in range(1, SHORT_TAPS):
                total = total + filt[j] * (
                    prod_ref[PAD + e - j : PAD + e - j + CHUNK, :] * mask_ref[j - 1, e : e + CHUNK, :]
                )
            mid = (raw(e, cols) + q_ref[e : e + CHUNK, :] * total).astype(jnp.bfloat16)
            mid_ref[e : e + CHUNK, cols] = mid
            mid = mid.astype(jnp.float32)
            at = slice(own - HALO + e, own - HALO + e + CHUNK)
            acc_ref[at, :] = acc_ref[at, :] + mid * mid
        return carry

    lax.fori_loop(0, width // LANES, tile, 0)
    for part in range(2):
        for r in range(0, own, LANES):
            at = part * own + r
            col = jnp.sum(acc_ref[at : at + LANES, :], axis=1, keepdims=True)
            s_ref[part : part + 1, r : r + LANES] = as_row(col)


def mr_kernel(
    mid_ref, sums_ref, off_ref, gain_ref, feat_ref, base_ref, out_ref,
    scale_ref, mask_ref, norm_ref, mixed_ref, q_ref, keep_ref, toep_ref,
):
    ext, width = mid_ref.shape
    own = ext - HALO
    blocks = own // LANES
    per_tile = LANES // GROUP
    scale_columns(sums_ref, scale_ref)
    masks_of(off_ref, mask_ref, FEAT_TAPS)
    norm_ref[0:PAD, :] = jnp.zeros((PAD, LANES), jnp.float32)
    row = lax.broadcasted_iota(jnp.int32, (LANES, LANES), 0)
    col = lax.broadcasted_iota(jnp.int32, (LANES, LANES), 1)
    for b in range(blocks):
        off = off_ref[HALO + b * LANES : HALO + (b + 1) * LANES, :]
        lag = (row - col).astype(jnp.float32)
        before = (col > row) & (lag + MEDIUM_TAPS <= off)
        within = (row >= col) & (lag <= off)
        keep_ref[b, :, 0:LANES] = before.astype(jnp.float32).astype(jnp.bfloat16)
        keep_ref[b, :, LANES:] = within.astype(jnp.float32).astype(jnp.bfloat16)
    group_of = lax.broadcasted_iota(jnp.int32, (LANES, LANES), 1) // GROUP

    def tile(i, carry):
        cols = pl.ds(pl.multiple_of(i * LANES, LANES), LANES)
        gain = gain_ref[0:1, cols]
        for e in range(0, ext, CHUNK):
            n = mid_ref[e : e + CHUNK, cols].astype(jnp.float32) * scale_ref[e : e + CHUNK, :] * gain
            norm_ref[PAD + e : PAD + e + CHUNK, :] = n.astype(jnp.bfloat16).astype(jnp.float32)
        taps = [[feat_ref[s, j : j + 1, cols] for j in range(FEAT_TAPS)] for s in range(3)]
        for e in range(HALO - LANES, ext, CHUNK):
            xs = [norm_ref[PAD + e : PAD + e + CHUNK, :]]
            for j in range(1, FEAT_TAPS):
                xs.append(norm_ref[PAD + e - j : PAD + e - j + CHUNK, :] * mask_ref[j - 1, e : e + CHUNK, :])
            k, v = (taps[s][0] * xs[0] + taps[s][1] * xs[1] + taps[s][2] * xs[2] for s in (1, 2))
            w = e - (HALO - LANES)
            mixed_ref[w : w + CHUNK, :] = (k * v).astype(jnp.bfloat16)
            if e >= HALO:
                q = taps[0][0] * xs[0] + taps[0][1] * xs[1] + taps[0][2] * xs[2]
                q_ref[e - HALO : e - HALO + CHUNK, :] = q
        for g in range(per_tile):
            base = base_ref[i * per_tile + g]
            for r in range(0, LANES, GROUP):
                turned = (pltpu.roll(base, r, 1) if r else base).astype(jnp.bfloat16)
                for b in range(blocks):
                    at = slice(g * LANES + r, g * LANES + r + GROUP)
                    toep_ref[b, at, 0:LANES] = turned * keep_ref[b, r : r + GROUP, 0:LANES]
                    toep_ref[b, at, LANES:] = turned * keep_ref[b, r : r + GROUP, LANES:]
        for b in range(blocks):
            window = mixed_ref[b * LANES : (b + 2) * LANES, :]
            medium = jnp.zeros((LANES, LANES), jnp.float32)
            for g in range(per_tile):
                y = jnp.dot(
                    toep_ref[b, g * LANES : (g + 1) * LANES, :], window, preferred_element_type=jnp.float32
                )
                medium = y if g == 0 else jnp.where(group_of == g, y, medium)
            rows = slice(b * LANES, (b + 1) * LANES)
            mid = mid_ref[HALO + b * LANES : HALO + (b + 1) * LANES, cols].astype(jnp.float32)
            out_ref[rows, cols] = (mid + q_ref[rows, :] * medium).astype(jnp.bfloat16)
        return carry

    lax.fori_loop(0, width // LANES, tile, 0)


def call(kernel, out_shape, scratch, flops, nbytes, smem=0):
    count = smem
    params = pltpu.CompilerParams(vmem_limit_bytes=VMEM_LIMIT)
    cost = pl.CostEstimate(flops=flops, bytes_accessed=nbytes, transcendentals=0)

    def run(*operands):
        specs = [pl.BlockSpec(memory_space=pltpu.SMEM)] * count
        specs += [pl.BlockSpec(memory_space=pltpu.VMEM)] * (len(operands) - count)
        return pl.pallas_call(
            kernel, out_shape=out_shape, in_specs=specs,
            out_specs=jax.tree.map(lambda _: pl.BlockSpec(memory_space=pltpu.VMEM), out_shape),
            scratch_shapes=scratch, compiler_params=params, cost_estimate=cost,
        )(*operands)

    return run


def shards(hidden, doc_lengths, gain_se, gain_mr, feat_se, feat_mr, filter_se, filter_mr):
    f32, bf16 = jnp.float32, jnp.bfloat16
    shape = jax.ShapeDtypeStruct
    own, width = hidden.shape[1:]
    ext = HALO + own
    groups = filter_se.shape[0]
    x = hidden[0]
    first = (lax.axis_index("ctx") * own).astype(jnp.int32).reshape(1)
    part = call(sums_kernel, shape((1, own), f32), [], 1 << 20, 1 << 20)(x)
    before = shifted(part, "ctx", 1)
    halo = shifted(x[own - HALO :], "ctx", 1)
    off, fexp, base = call(
        prep_kernel,
        (shape((ext, LANES), f32), shape((8, width), f32), shape((groups, GROUP, LANES), f32)),
        [pltpu.VMEM((groups, LANES), f32)], 1 << 24, 1 << 20, smem=1,
    )(first, doc_lengths, jnp.pad(filter_se.T, ((0, 1), (0, 0))), filter_mr)
    sums = lax.all_gather(jnp.concatenate([before, part], axis=0), "tp")
    mid, part_two = call(
        se_kernel,
        (shape((ext, width), bf16), shape((2, own), f32)),
        [
            pltpu.VMEM((ext, LANES), f32),
            pltpu.VMEM((SHORT_TAPS - 1, ext, LANES), f32),
            pltpu.VMEM((PAD + ext, LANES), f32),
            pltpu.VMEM((PAD + ext, LANES), f32),
            pltpu.VMEM((ext, LANES), f32),
            pltpu.VMEM((2 * own, LANES), f32),
        ],
        50 << 20, 4 << 20,
    )(x, halo, sums, off, gain_se.reshape(1, width), feat_se, fexp)
    sums_two = lax.all_gather(part_two, "tp")
    out = call(
        mr_kernel,
        shape((own, width), bf16),
        [
            pltpu.VMEM((ext, LANES), f32),
            pltpu.VMEM((FEAT_TAPS - 1, ext, LANES), f32),
            pltpu.VMEM((PAD + ext, LANES), f32),
            pltpu.VMEM((own + LANES, LANES), bf16),
            pltpu.VMEM((own, LANES), f32),
            pltpu.VMEM((own // LANES, LANES, 2 * LANES), bf16),
            pltpu.VMEM((own // LANES, (LANES // GROUP) * LANES, 2 * LANES), bf16),
        ],
        1 << 30, 4 << 20,
    )(mid, sums_two, off, gain_mr.reshape(1, width), feat_mr, base)
    return out[None]


def solution(mesh):
    in_specs = (
        P(None, "ctx", "tp"),
        P(),
        P("tp"),
        P("tp"),
        P(None, None, "tp"),
        P(None, None, "tp"),
        P("tp", None),
        P("tp", None),
    )
    out_specs = P(None, "ctx", "tp")
    return jax.shard_map(shards, mesh=mesh, in_specs=in_specs, out_specs=out_specs, check_vma=False)
```

time: 235 us -> 63.6 us (0.27)
  local copies, waits for them, and re-layouts: 140 us -> 1.23 us
  other arithmetic: 37.9 us -> 0.01 us
  Pallas kernels: 0 us -> 20.3 us
  matrix products: 11.3 us -> 0 us
  waiting for transfers between devices: 11.6 us -> 5.94 us
  blocking collectives: 25.2 us -> 29.9 us
  loops' own time: 4.01 us -> 0 us
    gather x2 -> x0, local copies, waits for them, and re-layouts: 126 us -> none  [band_table(): table = filters[:, jnp.clip(tap_lag, 0, MEDIUM_TAPS - 1)]]
    all_gather x0 -> x2, blocking collectives: none -> 29.9 us  [the longest x1 17.3 us: shards(): sums = lax.all_gather(jnp.concatenate([before, part], axis=0), 'tp')]
    psum x2 -> x0, blocking collectives: 25.2 us -> none  [the longest x1 14.9 us: shards(): square_sums = lax.psum(jnp.sum(stream_in * stream_in, axis=-1), 'tp')]
    pallas_call x0 -> x4, Pallas kernels: none -> 20.3 us  [run(): pl.pallas_call(kernel, out_shape=out_shape, in_specs=specs, out_specs=jax...]
    convert_element_type x10 -> x0, other arithmetic: 12.3 us -> none  [the longest x1 5.69 us: shards(): return output_f.astype(jnp.bfloat16)]
    dot_general x2 -> x0, matrix products: 11.3 us -> none  [one_block(): jnp.einsum('gts,sgc->tgc', masked_toep, window_rows, preferred_element_ty...]
    reduce_max x3 -> x0, other arithmetic: 8.83 us -> none  [doc_offsets(): jnp.max(jnp.where(starts_before, doc_starts[:, None, :], 0), axis=-1)]
    select_n x1 -> x0, other arithmetic: 7.29 us -> none  [band_table(): return jnp.where(in_range[None], table, jnp.zeros((), filters.dtype))]
  transfers between devices with their start and end apart: 2 -> 2, of which waited for: 1 -> 1; matrix products, arithmetic and copies ran while one was open for 62% -> 0% of each run, Pallas kernels for 0% -> 4%
where the time goes in v1:
time: 63.6 us; the launch traced here: 63.5 us
  blocking collectives  29.9 us (47%)
  Pallas kernels  20.3 us (32%)
  starting transfers between devices  5.99 us (9%)
  waiting for transfers between devices  5.94 us (9%)
  local copies, waits for them, and re-layouts  1.23 us (2%)
    pallas_call x4, Pallas kernels, run(): pl.pallas_call(kernel, out_shape=out_shape, in_specs=specs, out_specs=jax...  20.3 us
    all_gather x1, blocking collectives, shards(): sums = lax.all_gather(jnp.concatenate([before, part], axis=0), 'tp')  17.3 us
    all_gather x1, blocking collectives, shards(): sums_two = lax.all_gather(part_two, 'tp')  12.5 us
    ppermute x2, starting transfers between devices, shifted(): return lax.ppermute(x, axis, pairs)  5.99 us
    ppermute x2, waiting for transfers between devices, shifted(): return lax.ppermute(x, axis, pairs)  5.94 us
  transfers between devices with their start and end apart: 2, of which 1 were waited for; matrix products, arithmetic and copies ran while one was open for 0% of the time, Pallas kernels for 4%

profile of v1, /device:TPU:2, one launch (start us, length us, event | category | flops | bytes accessed | tf_op | source)
XLA Modules:
  0.0 63.5 jit_solution(8588421966798214931)
XLA Ops:
  0.0 0.0 copy-start
  0.0 0.0 copy-start.7
  0.0 0.0 copy-start.5
  0.0 0.0 copy-start.6
  0.0 0.0 copy-start.1
  0.0 0.0 copy-start.3
  0.0 1.2 %slice_bitcast_fusion = bf16[144,2048]{1,0:T(8,128)(2,1)S(1)} fusion(bf16[1,256,2048]{2,1,0:T(8,128)(2,1)} %param.8), kind=kLoop, calls=%fused_computation | loop fusion | bytes 1179648 | tf_op jit(solution)/shard_map/slice | solution.py:252
  1.2 0.0 copy-start.2
  1.2 0.0 copy-start.4
  1.3 2.1 %collective-permute-start = (bf16[144,2048]{1,0:T(8,128)(2,1)S(1)}, bf16[144,2048]{1,0:T(8,128)(2,1)S(1)}, u32[]{:S(2)}, u32[]{:S(2)}) collective-permute-start(bf16[144,2048]{1,0:T(8,128)(2,1)S(1)} %slice_bitcast_fusion), channel_id=1, source_target_pairs={{0,4},{4,8},{8,12},{12,16},{16,20},{20,24},{24,28},{28,32},{32,36}... | collective-permute-start | bytes 1769480 | tf_op jit(solution)/shard_map/ppermute | solution.py:25
  3.3 0.0 copy-done
  3.3 0.4 shard_map.82
  3.7 3.9 %collective-permute-start.1 = (f32[1,256]{1,0:T(1,128)S(1)}, f32[1,256]{1,0:T(1,128)S(1)}, u32[]{:S(2)}, u32[]{:S(2)}) collective-permute-start(f32[1,256]{1,0:T(1,128)S(1)} %shard_map.82), channel_id=1, source_target_pairs={{0,4},{4,8},{8,12},{12,16},{16,20},{20,24},{24,28},{28,32},{32,36}... | collective-permute-start | bytes 3080 | tf_op jit(solution)/shard_map/ppermute | solution.py:25
  7.7 0.0 copy-done.7
  7.7 0.0 copy-done.5
  7.7 0.0 copy-done.6
  7.7 2.0 %shard_map.83 = (f32[400,128]{1,0:T(8,128)S(1)}, f32[8,2048]{1,0:T(8,128)S(1)}, f32[128,16,128]{2,1,0:T(8,128)S(1)}) custom-call(s32[1]{0:T(128)} %bitcast.3.first_ref, s32[1,128]{1,0:T(1,128)S(1)} %copy-done.6, f32[8,128]{1,0:T(8,128)S(1)} %pad.4.fse_ref, bf16[128,128]{1,0:T(8,128)(2,1)S(1)} %copy-done.5), custom_call_target="tpu_custom_call" | custom-call | flops 16777216 | bytes 1048576 | tf_op jit(solution)/shard_map/pallas_call | solution.py:233
  9.7 5.9 %collective-permute-done.1 = f32[1,256]{1,0:T(1,128)S(1)} collective-permute-done((f32[1,256]{1,0:T(1,128)S(1)}, f32[1,256]{1,0:T(1,128)S(1)}, u32[]{:S(2)}, u32[]{:S(2)}) %collective-permute-start.1) | collective-permute-done | bytes 1056 | tf_op jit(solution)/shard_map/ppermute | solution.py:25
  15.7 17.3 %all-gather.2.sums_ref = f32[4,2,256]{2,1,0:T(2,128)S(1)} all-gather(f32[1,2,256]{2,1,0:T(2,128)S(1)} %maximum_bitcast_fusion), channel_id=2, replica_groups=mesh['ctx'=64,'tp'=4] {'tp'}, dimensions={0}, use_global_device_ids=true | all-gather | bytes 10240 | tf_op jit(solution)/shard_map/all_gather | solution.py:258
  33.0 0.0 collective-permute-done.halo_ref
  33.0 0.0 copy-done.1
  33.0 0.0 copy-done.3
  33.0 6.2 %shard_map.84 = (bf16[400,2048]{1,0:T(8,128)(2,1)S(1)}, f32[2,256]{1,0:T(2,128)S(1)}) custom-call(bf16[256,2048]{1,0:T(8,128)(2,1)S(1)} %bitcast.12, bf16[144,2048]{1,0:T(8,128)(2,1)S(1)} %collective-permute-done.halo_ref, f32[4,2,256]{2,1,0:T(2,128)S(1)} %all-gather.2.sums_ref, f32[400,128]{1,0:T(8,128)S(1)} %get-tuple-element.10.off_ref, ...), custom_call_target="tpu_custom_call" | custom-call | flops 52428800 | bytes 4194304 | tf_op jit(solution)/shard_map/pallas_call | solution.py:233
  39.2 12.5 %all-gather.3.sums_ref = f32[4,2,256]{2,1,0:T(2,128)S(1)} all-gather(f32[1,2,256]{2,1,0:T(2,128)S(1)} %bitcast.15), channel_id=3, replica_groups=mesh['ctx'=64,'tp'=4] {'tp'}, dimensions={0}, use_global_device_ids=true | all-gather | bytes 10240 | tf_op jit(solution)/shard_map/all_gather | solution.py:272
  51.8 0.0 copy-done.2
  51.8 0.0 copy-done.4
  51.8 11.7 %shard_map.85 = bf16[256,2048]{1,0:T(8,128)(2,1)} custom-call(bf16[400,2048]{1,0:T(8,128)(2,1)S(1)} %get-tuple-element.12.mid_ref, f32[4,2,256]{2,1,0:T(2,128)S(1)} %all-gather.3.sums_ref, f32[400,128]{1,0:T(8,128)S(1)} %get-tuple-element.10.off_ref, f32[1,2048]{1,0:T(1,128)S(1)} %bitcast.14, f32[3,3,2048]{2,1,0:T(4,128)S(1)} %copy-done.2, ...), custom_call_target="tpu_custom_call" | custom-call | flops 1073741824 | bytes 4194304 | tf_op jit(solution)/shard_map/pallas_call | solution.py:233
  (2 shorter events, 0.0 us)
Async XLA Ops:
  0.0 3.3 %copy-start = (bf16[1,256,2048]{2,1,0:T(8,128)(2,1)S(1)}, bf16[1,256,2048]{2,1,0:T(8,128)(2,1)}, u32[]{:S(2)}) copy-start(bf16[1,256,2048]{2,1,0:T(8,128)(2,1)} %param.8) | copy-start | bytes 3145732
  0.0 7.7 %copy-start.7 = (f32[128,7]{0,1:T(8,128)S(1)}, f32[128,7]{0,1:T(8,128)}, u32[]{:S(2)}) copy-start(f32[128,7]{0,1:T(8,128)} %param.14) | copy-start | bytes 10756
  0.0 7.7 %copy-start.5 = (bf16[128,128]{1,0:T(8,128)(2,1)S(1)}, bf16[128,128]{1,0:T(8,128)(2,1)}, u32[]{:S(2)}) copy-start(bf16[128,128]{1,0:T(8,128)(2,1)} %fmr_ref.1) | copy-start | bytes 98308
  0.0 7.7 %copy-start.6 = (s32[1,128]{1,0:T(1,128)S(1)}, s32[1,128]{1,0:T(1,128)}, u32[]{:S(2)}) copy-start(s32[1,128]{1,0:T(1,128)} %len_ref.1) | copy-start | bytes 1540
  0.0 33.0 %copy-start.1 = (f32[3,3,2048]{2,1,0:T(4,128)S(1)}, f32[3,3,2048]{2,1,0:T(4,128)}, u32[]{:S(2)}) copy-start(f32[3,3,2048]{2,1,0:T(4,128)} %feat_ref.2) | copy-start | bytes 221188
  0.0 33.0 %copy-start.3 = (f32[2048]{0:T(1024)S(1)}, f32[2048]{0:T(1024)}, u32[]{:S(2)}) copy-start(f32[2048]{0:T(1024)} %param.10) | copy-start | bytes 24580
  1.2 50.5 %copy-start.2 = (f32[3,3,2048]{2,1,0:T(4,128)S(1)}, f32[3,3,2048]{2,1,0:T(4,128)}, u32[]{:S(2)}) copy-start(f32[3,3,2048]{2,1,0:T(4,128)} %feat_ref.3) | copy-start | bytes 221188
  1.2 50.5 %copy-start.4 = (f32[2048]{0:T(1024)S(1)}, f32[2048]{0:T(1024)}, u32[]{:S(2)}) copy-start(f32[2048]{0:T(1024)} %param.11) | copy-start | bytes 24580
  1.3 31.7 %collective-permute-start = (bf16[144,2048]{1,0:T(8,128)(2,1)S(1)}, bf16[144,2048]{1,0:T(8,128)(2,1)S(1)}, u32[]{:S(2)}, u32[]{:S(2)}) collective-permute-start(bf16[144,2048]{1,0:T(8,128)(2,1)S(1)} %slice_bitcast_fusion), channel_id=1, source_target_pairs={{0,4},{4,8},{8,12},{12,16},{16,20},{20,24},{24,28},{28,32},{32,36}... | collective-permute-start | bytes 1769480 | tf_op jit(solution)/shard_map/ppermute | solution.py:25
  3.7 11.9 %collective-permute-start.1 = (f32[1,256]{1,0:T(1,128)S(1)}, f32[1,256]{1,0:T(1,128)S(1)}, u32[]{:S(2)}, u32[]{:S(2)}) collective-permute-start(f32[1,256]{1,0:T(1,128)S(1)} %shard_map.82), channel_id=1, source_target_pairs={{0,4},{4,8},{8,12},{12,16},{16,20},{20,24},{24,28},{28,32},{32,36}... | collective-permute-start | bytes 3080 | tf_op jit(solution)/shard_map/ppermute | solution.py:25

commit v2 on v1

--- a/solution.py
+++ b/solution.py
@@ -48,7 +48,8 @@
             s_ref[0:1, r - 64 : r + 64] = as_row(jnp.concatenate([held, col], axis=0))
 
 
-def prep_kernel(first_ref, len_ref, fse_ref, fmr_ref, off_ref, fexp_ref, base_ref, rev_ref):
+def prep_kernel(first_ref, x_ref, len_ref, fse_ref, fmr_ref, off_ref, fexp_ref, base_ref, last_ref, rev_ref):
+    last_ref[...] = x_ref[x_ref.shape[0] - HALO :, :]
     ext = off_ref.shape[0]
     width = fexp_ref.shape[1]
     groups = fmr_ref.shape[0]
@@ -208,12 +209,10 @@
                     toep_ref[b, at, LANES:] = turned * keep_ref[b, r : r + GROUP, LANES:]
         for b in range(blocks):
             window = mixed_ref[b * LANES : (b + 2) * LANES, :]
-            medium = jnp.zeros((LANES, LANES), jnp.float32)
-            for g in range(per_tile):
-                y = jnp.dot(
-                    toep_ref[b, g * LANES : (g + 1) * LANES, :], window, preferred_element_type=jnp.float32
-                )
-                medium = y if g == 0 else jnp.where(group_of == g, y, medium)
+            y = jnp.dot(toep_ref[b], window, preferred_element_type=jnp.float32)
+            medium = y[0:LANES]
+            for g in range(1, per_tile):
+                medium = jnp.where(group_of == g, y[g * LANES : (g + 1) * LANES], medium)
             rows = slice(b * LANES, (b + 1) * LANES)
             mid = mid_ref[HALO + b * LANES : HALO + (b + 1) * LANES, cols].astype(jnp.float32)
             out_ref[rows, cols] = (mid + q_ref[rows, :] * medium).astype(jnp.bfloat16)
@@ -237,6 +236,43 @@
         )(*operands)
 
     return run
+
+
+def se_call(x, halo, sums, off, gain, feat, fexp):
+    own, width = x.shape
+    ext = HALO + own
+    return call(
+        se_kernel,
+        (jax.ShapeDtypeStruct((ext, width), jnp.bfloat16), jax.ShapeDtypeStruct((2, own), jnp.float32)),
+        [
+            pltpu.VMEM((ext, LANES), jnp.float32),
+            pltpu.VMEM((SHORT_TAPS - 1, ext, LANES), jnp.float32),
+            pltpu.VMEM((PAD + ext, LANES), jnp.float32),
+            pltpu.VMEM((PAD + ext, LANES), jnp.float32),
+            pltpu.VMEM((ext, LANES), jnp.float32),
+            pltpu.VMEM((2 * own, LANES), jnp.float32),
+        ],
+        50 << 20, 4 << 20,
+    )(x, halo, sums, off, gain, feat, fexp)
+
+
+def mr_call(mid, sums, off, gain, feat, base):
+    ext, width = mid.shape
+    own = ext - HALO
+    return call(
+        mr_kernel,
+        jax.ShapeDtypeStruct((own, width), jnp.bfloat16),
+        [
+            pltpu.VMEM((ext, LANES), jnp.float32),
+            pltpu.VMEM((FEAT_TAPS - 1, ext, LANES), jnp.float32),
+            pltpu.VMEM((PAD + ext, LANES), jnp.float32),
+            pltpu.VMEM((own + LANES, LANES), jnp.bfloat16),
+            pltpu.VMEM((own, LANES), jnp.float32),
+            pltpu.VMEM((own // LANES, LANES, 2 * LANES), jnp.bfloat16),
+            pltpu.VMEM((own // LANES, (LANES // GROUP) * LANES, 2 * LANES), jnp.bfloat16),
+        ],
+        1 << 30, 4 << 20,
+    )(mid, sums, off, gain, feat, base)
 
 
 def shards(hidden, doc_lengths, gain_se, gain_mr, feat_se, feat_mr, filter_se, filter_mr):
@@ -249,41 +285,21 @@
     first = (lax.axis_index("ctx") * own).astype(jnp.int32).reshape(1)
     part = call(sums_kernel, shape((1, own), f32), [], 1 << 20, 1 << 20)(x)
     before = shifted(part, "ctx", 1)
-    halo = shifted(x[own - HALO :], "ctx", 1)
-    off, fexp, base = call(
+    off, fexp, base, last = call(
         prep_kernel,
-        (shape((ext, LANES), f32), shape((8, width), f32), shape((groups, GROUP, LANES), f32)),
+        (
+            shape((ext, LANES), f32),
+            shape((8, width), f32),
+            shape((groups, GROUP, LANES), f32),
+            shape((HALO, width), bf16),
+        ),
         [pltpu.VMEM((groups, LANES), f32)], 1 << 24, 1 << 20, smem=1,
-    )(first, doc_lengths, jnp.pad(filter_se.T, ((0, 1), (0, 0))), filter_mr)
+    )(first, x, doc_lengths, jnp.pad(filter_se.T, ((0, 1), (0, 0))), filter_mr)
+    halo = shifted(last, "ctx", 1)
     sums = lax.all_gather(jnp.concatenate([before, part], axis=0), "tp")
-    mid, part_two = call(
-        se_kernel,
-        (shape((ext, width), bf16), shape((2, own), f32)),
-        [
-            pltpu.VMEM((ext, LANES), f32),
-            pltpu.VMEM((SHORT_TAPS - 1, ext, LANES), f32),
-            pltpu.VMEM((PAD + ext, LANES), f32),
-            pltpu.VMEM((PAD + ext, LANES), f32),
-            pltpu.VMEM((ext, LANES), f32),
-            pltpu.VMEM((2 * own, LANES), f32),
-        ],
-        50 << 20, 4 << 20,
-    )(x, halo, sums, off, gain_se.reshape(1, width), feat_se, fexp)
+    mid, part_two = se_call(x, halo, sums, off, gain_se.reshape(1, width), feat_se, fexp)
     sums_two = lax.all_gather(part_two, "tp")
-    out = call(
-        mr_kernel,
-        shape((own, width), bf16),
-        [
-            pltpu.VMEM((ext, LANES), f32),
-            pltpu.VMEM((FEAT_TAPS - 1, ext, LANES), f32),
-            pltpu.VMEM((PAD + ext, LANES), f32),
-            pltpu.VMEM((own + LANES, LANES), bf16),
-            pltpu.VMEM((own, LANES), f32),
-            pltpu.VMEM((own // LANES, LANES, 2 * LANES), bf16),
-            pltpu.VMEM((own // LANES, (LANES // GROUP) * LANES, 2 * LANES), bf16),
-        ],
-        1 << 30, 4 << 20,
-    )(mid, sums_two, off, gain_mr.reshape(1, width), feat_mr, base)
+    out = mr_call(mid, sums_two, off, gain_mr.reshape(1, width), feat_mr, base)
     return out[None]
 
 

time: 63.6 us -> 67.2 us (1.057)
  local copies, waits for them, and re-layouts: 1.23 us -> 3.37 us
  waiting for transfers between devices: 5.94 us -> 7.98 us
  Pallas kernels: 20.3 us -> 19.6 us
    unnamed x16, local copies, waits for them, and re-layouts: 0.04 us -> 2.66 us
    ppermute x2, waiting for transfers between devices: 5.94 us -> 7.98 us  [shifted(): return lax.ppermute(x, axis, pairs)]
    slice x1 -> x0, local copies, waits for them, and re-layouts: 1.19 us -> none  [shards(): halo = shifted(x[own - HALO:], 'ctx', 1)]
    pad x1, local copies, waits for them, and re-layouts: 0.01 us -> 0.7 us  [shards(): jnp.pad(filter_se.T, ((0, 1), (0, 0)))]
    pallas_call x4, Pallas kernels: 20.3 us -> 19.6 us  [run(): pl.pallas_call(kernel, out_shape=out_shape, in_specs=specs, out_specs=jax...]
  transfers between devices with their start and end apart: 2 -> 2, of which waited for: 1 -> 1; matrix products, arithmetic and copies ran while one was open for 0% -> 0% of each run, Pallas kernels for 4% -> 1%
where the time goes in v2:
time: 67.2 us; the launch traced here: 66.9 us
  blocking collectives  29.9 us (44%)
  Pallas kernels  19.6 us (29%)
  waiting for transfers between devices  7.98 us (12%)
  starting transfers between devices  5.99 us (9%)
  local copies, waits for them, and re-layouts  3.37 us (5%)
    pallas_call x4, Pallas kernels, run(): pl.pallas_call(kernel, out_shape=out_shape, in_specs=specs, out_specs=jax...  19.6 us
    all_gather x1, blocking collectives, shards(): sums = lax.all_gather(jnp.concatenate([before, part], axis=0), 'tp')  17.3 us
    all_gather x1, blocking collectives, shards(): sums_two = lax.all_gather(part_two, 'tp')  12.5 us
    ppermute x2, waiting for transfers between devices, shifted(): return lax.ppermute(x, axis, pairs)  7.98 us
    ppermute x2, starting transfers between devices, shifted(): return lax.ppermute(x, axis, pairs)  5.99 us
    unnamed x16, local copies, waits for them, and re-layouts  2.66 us
  transfers between devices with their start and end apart: 2, of which 1 were waited for; matrix products, arithmetic and copies ran while one was open for 0% of the time, Pallas kernels for 1%

profile of v2, /device:TPU:2, one launch (start us, length us, event | category | flops | bytes accessed | tf_op | source)
XLA Modules:
  0.0 66.9 jit_solution(5440809084321834600)
XLA Ops:
  0.0 0.0 copy-start.5
  0.0 0.7 %pad.4.fse_ref = f32[8,128]{1,0:T(8,128)S(1)} pad(f32[7,128]{1,0:T(8,128)} %bitcast.15, f32[]{:T(128)} %constant.10.clone.1), padding=0_1x0_0 | pad | bytes 7684 | tf_op jit(solution)/shard_map/jit(_pad)/pad | solution.py:297
  0.7 0.0 copy-start
  0.7 1.2 %copy-done = bf16[1,256,2048]{2,1,0:T(8,128)(2,1)S(1)} copy-done((bf16[1,256,2048]{2,1,0:T(8,128)(2,1)S(1)}, bf16[1,256,2048]{2,1,0:T(8,128)(2,1)}, u32[]{:S(2)}) %copy-start) | copy-done | bytes 1048600
  1.9 0.0 copy-start.4
  1.9 0.8 %copy-done.4 = bf16[128,128]{1,0:T(8,128)(2,1)S(1)} copy-done((bf16[128,128]{1,0:T(8,128)(2,1)S(1)}, bf16[128,128]{1,0:T(8,128)(2,1)}, u32[]{:S(2)}) %copy-start.4) | copy-done | bytes 32792
  2.7 0.0 copy-start.7
  2.7 0.7 copy-done.7
  3.3 0.0 copy-start.1
  3.3 0.0 copy-start.2
  3.4 2.0 %shard_map.82 = (f32[400,128]{1,0:T(8,128)S(1)}, f32[8,2048]{1,0:T(8,128)S(1)}, f32[128,16,128]{2,1,0:T(8,128)S(1)}, bf16[144,2048]{1,0:T(8,128)(2,1)S(1)}) custom-call(s32[1]{0:T(128)} %bitcast.1.first_ref, bf16[256,2048]{1,0:T(8,128)(2,1)S(1)} %bitcast.9, s32[1,128]{1,0:T(1,128)S(1)} %copy-done.7, f32[8,128]{1,0:T(8,128)S(1)} %pad.4.fse_ref, ...), custom_call_target="tpu_custom_call" | custom-call | flops 16777216 | bytes 1048576 | tf_op jit(solution)/shard_map/pallas_call | solution.py:232
  5.4 0.0 copy-start.3
  5.4 0.0 copy-start.6
  5.4 2.1 %collective-permute-start = (bf16[144,2048]{1,0:T(8,128)(2,1)S(1)}, bf16[144,2048]{1,0:T(8,128)(2,1)S(1)}, u32[]{:S(2)}, u32[]{:S(2)}) collective-permute-start(bf16[144,2048]{1,0:T(8,128)(2,1)S(1)} %get-tuple-element.11), channel_id=1, source_target_pairs={{0,4},{4,8},{8,12},{12,16},{16,20},{20,24},{24,28},{28,32},{32,36}... | collective-permute-start | bytes 1769480 | tf_op jit(solution)/shard_map/ppermute | solution.py:25
  7.5 0.0 copy-done.1
  7.5 0.4 shard_map.83
  7.9 3.9 %collective-permute-start.1 = (f32[1,256]{1,0:T(1,128)S(1)}, f32[1,256]{1,0:T(1,128)S(1)}, u32[]{:S(2)}, u32[]{:S(2)}) collective-permute-start(f32[1,256]{1,0:T(1,128)S(1)} %shard_map.83), channel_id=1, source_target_pairs={{0,4},{4,8},{8,12},{12,16},{16,20},{20,24},{24,28},{28,32},{32,36}... | collective-permute-start | bytes 3080 | tf_op jit(solution)/shard_map/ppermute | solution.py:25
  11.8 8.0 %collective-permute-done.1 = f32[1,256]{1,0:T(1,128)S(1)} collective-permute-done((f32[1,256]{1,0:T(1,128)S(1)}, f32[1,256]{1,0:T(1,128)S(1)}, u32[]{:S(2)}, u32[]{:S(2)}) %collective-permute-start.1) | collective-permute-done | bytes 1056 | tf_op jit(solution)/shard_map/ppermute | solution.py:25
  19.8 17.3 %all-gather.2.sums_ref = f32[4,2,256]{2,1,0:T(2,128)S(1)} all-gather(f32[1,2,256]{2,1,0:T(2,128)S(1)} %maximum_bitcast_fusion), channel_id=2, replica_groups=mesh['ctx'=64,'tp'=4] {'tp'}, dimensions={0}, use_global_device_ids=true | all-gather | bytes 10240 | tf_op jit(solution)/shard_map/all_gather | solution.py:299
  37.1 0.0 collective-permute-done.halo_ref
  37.1 0.0 copy-done.5
  37.1 0.0 copy-done.2
  37.1 6.2 %shard_map.84 = (bf16[400,2048]{1,0:T(8,128)(2,1)S(1)}, f32[2,256]{1,0:T(2,128)S(1)}) custom-call(bf16[256,2048]{1,0:T(8,128)(2,1)S(1)} %bitcast.11, bf16[144,2048]{1,0:T(8,128)(2,1)S(1)} %collective-permute-done.halo_ref, f32[4,2,256]{2,1,0:T(2,128)S(1)} %all-gather.2.sums_ref, f32[400,128]{1,0:T(8,128)S(1)} %get-tuple-element.12.off_ref, ...), custom_call_target="tpu_custom_call" | custom-call | flops 52428800 | bytes 4194304 | tf_op jit(solution)/shard_map/pallas_call | solution.py:232
  43.4 12.5 %all-gather.3.sums_ref = f32[4,2,256]{2,1,0:T(2,128)S(1)} all-gather(f32[1,2,256]{2,1,0:T(2,128)S(1)} %bitcast.14), channel_id=3, replica_groups=mesh['ctx'=64,'tp'=4] {'tp'}, dimensions={0}, use_global_device_ids=true | all-gather | bytes 10240 | tf_op jit(solution)/shard_map/all_gather | solution.py:301
  55.9 0.0 copy-done.3
  55.9 0.0 copy-done.6
  55.9 11.0 %shard_map.85 = bf16[256,2048]{1,0:T(8,128)(2,1)} custom-call(bf16[400,2048]{1,0:T(8,128)(2,1)S(1)} %get-tuple-element.14.mid_ref, f32[4,2,256]{2,1,0:T(2,128)S(1)} %all-gather.3.sums_ref, f32[400,128]{1,0:T(8,128)S(1)} %get-tuple-element.12.off_ref, f32[1,2048]{1,0:T(1,128)S(1)} %bitcast.13, f32[3,3,2048]{2,1,0:T(4,128)S(1)} %copy-done.3, ...), custom_call_target="tpu_custom_call" | custom-call | flops 1073741824 | bytes 4194304 | tf_op jit(solution)/shard_map/pallas_call | solution.py:232
  (1 shorter events, 0.0 us)
Async XLA Ops:
  0.0 37.1 %copy-start.5 = (f32[2048]{0:T(1024)S(1)}, f32[2048]{0:T(1024)}, u32[]{:S(2)}) copy-start(f32[2048]{0:T(1024)} %param.10) | copy-start | bytes 24580
  0.7 1.2 %copy-start = (bf16[1,256,2048]{2,1,0:T(8,128)(2,1)S(1)}, bf16[1,256,2048]{2,1,0:T(8,128)(2,1)}, u32[]{:S(2)}) copy-start(bf16[1,256,2048]{2,1,0:T(8,128)(2,1)} %param.8) | copy-start | bytes 3145732
  1.9 0.8 %copy-start.4 = (bf16[128,128]{1,0:T(8,128)(2,1)S(1)}, bf16[128,128]{1,0:T(8,128)(2,1)}, u32[]{:S(2)}) copy-start(bf16[128,128]{1,0:T(8,128)(2,1)} %fmr_ref.1) | copy-start | bytes 98308
  2.7 0.7 copy-start.7
  3.3 4.1 %copy-start.1 = (bf16[1,256,2048]{2,1,0:T(8,128)(2,1)S(1)}, bf16[1,256,2048]{2,1,0:T(8,128)(2,1)}, u32[]{:S(2)}) copy-start(bf16[1,256,2048]{2,1,0:T(8,128)(2,1)} %param.8) | copy-start | bytes 3145732
  3.3 33.8 %copy-start.2 = (f32[3,3,2048]{2,1,0:T(4,128)S(1)}, f32[3,3,2048]{2,1,0:T(4,128)}, u32[]{:S(2)}) copy-start(f32[3,3,2048]{2,1,0:T(4,128)} %feat_ref.2) | copy-start | bytes 221188
  5.4 50.5 %copy-start.3 = (f32[3,3,2048]{2,1,0:T(4,128)S(1)}, f32[3,3,2048]{2,1,0:T(4,128)}, u32[]{:S(2)}) copy-start(f32[3,3,2048]{2,1,0:T(4,128)} %feat_ref.3) | copy-start | bytes 221188
  5.4 50.5 %copy-start.6 = (f32[2048]{0:T(1024)S(1)}, f32[2048]{0:T(1024)}, u32[]{:S(2)}) copy-start(f32[2048]{0:T(1024)} %param.11) | copy-start | bytes 24580
  5.4 31.7 %collective-permute-start = (bf16[144,2048]{1,0:T(8,128)(2,1)S(1)}, bf16[144,2048]{1,0:T(8,128)(2,1)S(1)}, u32[]{:S(2)}, u32[]{:S(2)}) collective-permute-start(bf16[144,2048]{1,0:T(8,128)(2,1)S(1)} %get-tuple-element.11), channel_id=1, source_target_pairs={{0,4},{4,8},{8,12},{12,16},{16,20},{20,24},{24,28},{28,32},{32,36}... | collective-permute-start | bytes 1769480 | tf_op jit(solution)/shard_map/ppermute | solution.py:25
  7.9 11.9 %collective-permute-start.1 = (f32[1,256]{1,0:T(1,128)S(1)}, f32[1,256]{1,0:T(1,128)S(1)}, u32[]{:S(2)}, u32[]{:S(2)}) collective-permute-start(f32[1,256]{1,0:T(1,128)S(1)} %shard_map.83), channel_id=1, source_target_pairs={{0,4},{4,8},{8,12},{12,16},{16,20},{20,24},{24,28},{28,32},{32,36}... | collective-permute-start | bytes 3080 | tf_op jit(solution)/shard_map/ppermute | solution.py:25

commit v3 on v1

--- a/solution.py
+++ b/solution.py
@@ -48,10 +48,10 @@
             s_ref[0:1, r - 64 : r + 64] = as_row(jnp.concatenate([held, col], axis=0))
 
 
-def prep_kernel(first_ref, len_ref, fse_ref, fmr_ref, off_ref, fexp_ref, base_ref, rev_ref):
+def place_kernel(first_ref, after_ref, len_ref, fse_ref, off_ref, fexp_ref):
     ext = off_ref.shape[0]
     width = fexp_ref.shape[1]
-    groups = fmr_ref.shape[0]
+    groups = fse_ref.shape[0]
     lens = jnp.broadcast_to(len_ref[0:1, :].astype(jnp.float32), (8, LANES))
     lane = lax.broadcasted_iota(jnp.int32, (8, LANES), 1)
     ends = lens
@@ -70,9 +70,14 @@
         row = lax.broadcasted_iota(jnp.int32, (groups, LANES), 0)
         col = lax.broadcasted_iota(jnp.int32, (groups, LANES), 1)
         spread = (row == (c + col) // GROUP).astype(jnp.float32)
-        fexp_ref[:, c : c + LANES] = jnp.dot(
-            fse, spread, preferred_element_type=jnp.float32, precision=lax.Precision.HIGHEST
+        fexp_ref[0:SHORT_TAPS, c : c + LANES] = lax.dot_general(
+            fse, spread, (((0,), (0,)), ((), ())),
+            preferred_element_type=jnp.float32, precision=lax.Precision.HIGHEST,
         )
+
+
+def turn_kernel(after_ref, fmr_ref, base_ref, rev_ref):
+    groups = fmr_ref.shape[0]
     row = lax.broadcasted_iota(jnp.int32, (LANES, LANES), 0)
     col = lax.broadcasted_iota(jnp.int32, (LANES, LANES), 1)
     flip = ((row + col) % MEDIUM_TAPS == 0).astype(jnp.bfloat16)
@@ -84,6 +89,10 @@
         return carry
 
     lax.fori_loop(0, groups, one, 0, unroll=8)
+
+
+def scale_of(total):
+    return lax.rsqrt(total / D + norm_epsilon)
 
 
 def scale_columns(sums_ref, scale_ref):
@@ -91,44 +100,35 @@
     total = sums_ref[0]
     for i in range(1, tp):
         total = total + sums_ref[i]
-    scale = lax.rsqrt(total / D + norm_epsilon)
+    scale = scale_of(total)
     own = scale.shape[1]
     scale_ref[0:HALO, :] = as_column(scale[0:1])[own - HALO :, :]
     scale_ref[HALO:, :] = as_column(scale[1:2])
 
 
-def masks_of(off_ref, mask_ref, taps):
-    for r in range(0, off_ref.shape[0], CHUNK):
-        off = off_ref[r : r + CHUNK, :]
+def masks_of(off_ref, mask_ref, taps, first=0):
+    for r in range(0, mask_ref.shape[1], CHUNK):
+        off = off_ref[first + r : first + r + CHUNK, :]
         for j in range(1, taps):
             mask_ref[j - 1, r : r + CHUNK, :] = (off >= j).astype(jnp.float32)
 
 
-def se_kernel(
-    x_ref, halo_ref, sums_ref, off_ref, gain_ref, feat_ref, fexp_ref, mid_ref, s_ref,
+def se_rows(
+    raw, rows, skip, width, gain_ref, feat_ref, fexp_ref, mid_ref,
     scale_ref, mask_ref, norm_ref, prod_ref, q_ref, acc_ref,
 ):
-    own, width = x_ref.shape
-    ext = HALO + own
-    scale_columns(sums_ref, scale_ref)
-    masks_of(off_ref, mask_ref, SHORT_TAPS)
     norm_ref[0:PAD, :] = jnp.zeros((PAD, LANES), jnp.float32)
     prod_ref[0:PAD, :] = jnp.zeros((PAD, LANES), jnp.float32)
     acc_ref[...] = jnp.zeros(acc_ref.shape, jnp.float32)
 
-    def raw(e, cols):
-        if e < HALO:
-            return halo_ref[e : e + CHUNK, cols].astype(jnp.float32)
-        return x_ref[e - HALO : e - HALO + CHUNK, cols].astype(jnp.float32)
-
     def tile(i, carry):
         cols = pl.ds(pl.multiple_of(i * LANES, LANES), LANES)
         gain = gain_ref[0:1, cols]
-        for e in range(0, ext, CHUNK):
+        for e in range(0, rows, CHUNK):
             n = raw(e, cols) * scale_ref[e : e + CHUNK, :] * gain
             norm_ref[PAD + e : PAD + e + CHUNK, :] = n.astype(jnp.bfloat16).astype(jnp.float32)
         taps = [[feat_ref[s, j : j + 1, cols] for j in range(FEAT_TAPS)] for s in range(3)]
-        for e in range(0, ext, CHUNK):
+        for e in range(0, rows, CHUNK):
             xs = [norm_ref[PAD + e : PAD + e + CHUNK, :]]
             for j in range(1, FEAT_TAPS):
                 xs.append(norm_ref[PAD + e - j : PAD + e - j + CHUNK, :] * mask_ref[j - 1, e : e + CHUNK, :])
@@ -138,7 +138,7 @@
             prod_ref[PAD + e : PAD + e + CHUNK, :] = k * v
             q_ref[e : e + CHUNK, :] = q
         filt = [fexp_ref[j : j + 1, cols] for j in range(SHORT_TAPS)]
-        for e in range(0, ext, CHUNK):
+        for e in range(skip, rows, CHUNK):
             total = filt[0] * prod_ref[PAD + e : PAD + e + CHUNK, :]
             for j in range(1, SHORT_TAPS):
                 total = total + filt[j] * (
@@ -147,24 +147,60 @@
             mid = (raw(e, cols) + q_ref[e : e + CHUNK, :] * total).astype(jnp.bfloat16)
             mid_ref[e : e + CHUNK, cols] = mid
             mid = mid.astype(jnp.float32)
-            at = slice(own - HALO + e, own - HALO + e + CHUNK)
-            acc_ref[at, :] = acc_ref[at, :] + mid * mid
+            acc_ref[e : e + CHUNK, :] = acc_ref[e : e + CHUNK, :] + mid * mid
         return carry
 
     lax.fori_loop(0, width // LANES, tile, 0)
-    for part in range(2):
-        for r in range(0, own, LANES):
-            at = part * own + r
-            col = jnp.sum(acc_ref[at : at + LANES, :], axis=1, keepdims=True)
-            s_ref[part : part + 1, r : r + LANES] = as_row(col)
+
+
+def se_own_kernel(
+    x_ref, total_ref, off_ref, gain_ref, feat_ref, fexp_ref, mid_ref, s_ref, scale_ref, mask_ref, *scratch,
+):
+    own, width = x_ref.shape
+    acc_ref = scratch[-1]
+    scale_ref[...] = as_column(scale_of(total_ref[...]))
+    masks_of(off_ref, mask_ref, SHORT_TAPS, HALO)
+    mid_ref[0:CHUNK, :] = jnp.zeros((CHUNK, width), jnp.bfloat16)
+    se_rows(
+        lambda e, cols: x_ref[e : e + CHUNK, cols].astype(jnp.float32),
+        own, CHUNK, width, gain_ref, feat_ref, fexp_ref, mid_ref, scale_ref, mask_ref, *scratch,
+    )
+    for r in range(0, own, LANES):
+        s_ref[0:1, r : r + LANES] = as_row(jnp.sum(acc_ref[r : r + LANES, :], axis=1, keepdims=True))
+
+
+def se_halo_kernel(
+    x_ref, halo_ref, total_ref, before_ref, part_ref, off_ref, gain_ref, feat_ref, fexp_ref, mid_ref, s_ref,
+    scale_ref, mask_ref, *scratch,
+):
+    own, width = x_ref.shape
+    acc_ref = scratch[-1]
+    scale_ref[0:HALO, :] = as_column(scale_of(before_ref[...]))[own - HALO :, :]
+    scale_ref[HALO:, :] = as_column(scale_of(total_ref[...]))[0:CHUNK, :]
+    masks_of(off_ref, mask_ref, SHORT_TAPS)
+
+    def raw(e, cols):
+        if e < HALO:
+            return halo_ref[e : e + CHUNK, cols].astype(jnp.float32)
+        return x_ref[e - HALO : e - HALO + CHUNK, cols].astype(jnp.float32)
+
+    se_rows(
+        raw, HALO + CHUNK, 0, width, gain_ref, feat_ref, fexp_ref, mid_ref, scale_ref, mask_ref, *scratch
+    )
+    halo_part = jnp.sum(acc_ref[0:HALO, :], axis=1, keepdims=True)
+    halo_part = jnp.concatenate([jnp.zeros((own - HALO, 1), jnp.float32), halo_part], axis=0)
+    own_part = jnp.sum(acc_ref[HALO:, :], axis=1, keepdims=True)
+    own_part = jnp.concatenate([own_part, jnp.zeros((own - CHUNK, 1), jnp.float32)], axis=0)
+    s_ref[0:1, :] = as_row(halo_part)
+    s_ref[1:2, :] = as_row(own_part) + part_ref[...]
 
 
 def mr_kernel(
-    mid_ref, sums_ref, off_ref, gain_ref, feat_ref, base_ref, out_ref,
+    early_ref, mid_ref, sums_ref, off_ref, gain_ref, feat_ref, base_ref, out_ref,
     scale_ref, mask_ref, norm_ref, mixed_ref, q_ref, keep_ref, toep_ref,
 ):
-    ext, width = mid_ref.shape
-    own = ext - HALO
+    own, width = mid_ref.shape
+    ext = HALO + own
     blocks = own // LANES
     per_tile = LANES // GROUP
     scale_columns(sums_ref, scale_ref)
@@ -179,13 +215,19 @@
         within = (row >= col) & (lag <= off)
         keep_ref[b, :, 0:LANES] = before.astype(jnp.float32).astype(jnp.bfloat16)
         keep_ref[b, :, LANES:] = within.astype(jnp.float32).astype(jnp.bfloat16)
+    early = early_ref.shape[0]
+
+    def middle(e, cols):
+        held = early_ref[e : e + CHUNK, cols] if e < early else mid_ref[e - HALO : e - HALO + CHUNK, cols]
+        return held.astype(jnp.float32)
+
     group_of = lax.broadcasted_iota(jnp.int32, (LANES, LANES), 1) // GROUP
 
     def tile(i, carry):
         cols = pl.ds(pl.multiple_of(i * LANES, LANES), LANES)
         gain = gain_ref[0:1, cols]
         for e in range(0, ext, CHUNK):
-            n = mid_ref[e : e + CHUNK, cols].astype(jnp.float32) * scale_ref[e : e + CHUNK, :] * gain
+            n = middle(e, cols) * scale_ref[e : e + CHUNK, :] * gain
             norm_ref[PAD + e : PAD + e + CHUNK, :] = n.astype(jnp.bfloat16).astype(jnp.float32)
         taps = [[feat_ref[s, j : j + 1, cols] for j in range(FEAT_TAPS)] for s in range(3)]
         for e in range(HALO - LANES, ext, CHUNK):
@@ -208,15 +250,14 @@
                     toep_ref[b, at, LANES:] = turned * keep_ref[b, r : r + GROUP, LANES:]
         for b in range(blocks):
             window = mixed_ref[b * LANES : (b + 2) * LANES, :]
-            medium = jnp.zeros((LANES, LANES), jnp.float32)
-            for g in range(per_tile):
-                y = jnp.dot(
-                    toep_ref[b, g * LANES : (g + 1) * LANES, :], window, preferred_element_type=jnp.float32
-                )
-                medium = y if g == 0 else jnp.where(group_of == g, y, medium)
-            rows = slice(b * LANES, (b + 1) * LANES)
-            mid = mid_ref[HALO + b * LANES : HALO + (b + 1) * LANES, cols].astype(jnp.float32)
-            out_ref[rows, cols] = (mid + q_ref[rows, :] * medium).astype(jnp.bfloat16)
+            y = jnp.dot(toep_ref[b], window, preferred_element_type=jnp.float32)
+            medium = y[0:LANES]
+            for g in range(1, per_tile):
+                medium = jnp.where(group_of == g, y[g * LANES : (g + 1) * LANES], medium)
+            for r in range(0, LANES, CHUNK):
+                t = b * LANES + r
+                out = middle(HALO + t, cols) + q_ref[t : t + CHUNK, :] * medium[r : r + CHUNK]
+                out_ref[t : t + CHUNK, cols] = out.astype(jnp.bfloat16)
         return carry
 
     lax.fori_loop(0, width // LANES, tile, 0)
@@ -239,52 +280,67 @@
     return run
 
 
+def se_scratch(rows):
+    return [
+        pltpu.VMEM((rows, LANES), jnp.float32),
+        pltpu.VMEM((SHORT_TAPS - 1, rows, LANES), jnp.float32),
+        pltpu.VMEM((PAD + rows, LANES), jnp.float32),
+        pltpu.VMEM((PAD + rows, LANES), jnp.float32),
+        pltpu.VMEM((rows, LANES), jnp.float32),
+        pltpu.VMEM((rows, LANES), jnp.float32),
+    ]
+
+
+def se_own_call(x, *rest):
+    own, width = x.shape
+    shapes = (jax.ShapeDtypeStruct((own, width), jnp.bfloat16), jax.ShapeDtypeStruct((1, own), jnp.float32))
+    return call(se_own_kernel, shapes, se_scratch(own), 25 << 20, 2 << 20)(x, *rest)
+
+
+def se_halo_call(x, *rest):
+    own, width = x.shape
+    rows = HALO + CHUNK
+    shapes = (jax.ShapeDtypeStruct((rows, width), jnp.bfloat16), jax.ShapeDtypeStruct((2, own), jnp.float32))
+    return call(se_halo_kernel, shapes, se_scratch(rows), 25 << 20, 2 << 20)(x, *rest)
+
+
+def mr_call(early, mid, *rest):
+    own, width = mid.shape
+    ext = HALO + own
+    scratch = [
+        pltpu.VMEM((ext, LANES), jnp.float32),
+        pltpu.VMEM((FEAT_TAPS - 1, ext, LANES), jnp.float32),
+        pltpu.VMEM((PAD + ext, LANES), jnp.float32),
+        pltpu.VMEM((own + LANES, LANES), jnp.bfloat16),
+        pltpu.VMEM((own, LANES), jnp.float32),
+        pltpu.VMEM((own // LANES, LANES, 2 * LANES), jnp.bfloat16),
+        pltpu.VMEM((own // LANES, (LANES // GROUP) * LANES, 2 * LANES), jnp.bfloat16),
+    ]
+    return call(mr_kernel, jax.ShapeDtypeStruct((own, width), jnp.bfloat16), scratch, 1 << 30, 4 << 20)(early, mid, *rest)
+
+
 def shards(hidden, doc_lengths, gain_se, gain_mr, feat_se, feat_mr, filter_se, filter_mr):
-    f32, bf16 = jnp.float32, jnp.bfloat16
+    f32 = jnp.float32
     shape = jax.ShapeDtypeStruct
     own, width = hidden.shape[1:]
-    ext = HALO + own
     groups = filter_se.shape[0]
     x = hidden[0]
     first = (lax.axis_index("ctx") * own).astype(jnp.int32).reshape(1)
+    halo = shifted(x[own - HALO :], "ctx", 1)
     part = call(sums_kernel, shape((1, own), f32), [], 1 << 20, 1 << 20)(x)
-    before = shifted(part, "ctx", 1)
-    halo = shifted(x[own - HALO :], "ctx", 1)
-    off, fexp, base = call(
-        prep_kernel,
-        (shape((ext, LANES), f32), shape((8, width), f32), shape((groups, GROUP, LANES), f32)),
-        [pltpu.VMEM((groups, LANES), f32)], 1 << 24, 1 << 20, smem=1,
-    )(first, doc_lengths, jnp.pad(filter_se.T, ((0, 1), (0, 0))), filter_mr)
-    sums = lax.all_gather(jnp.concatenate([before, part], axis=0), "tp")
-    mid, part_two = call(
-        se_kernel,
-        (shape((ext, width), bf16), shape((2, own), f32)),
-        [
-            pltpu.VMEM((ext, LANES), f32),
-            pltpu.VMEM((SHORT_TAPS - 1, ext, LANES), f32),
-            pltpu.VMEM((PAD + ext, LANES), f32),
-            pltpu.VMEM((PAD + ext, LANES), f32),
-            pltpu.VMEM((ext, LANES), f32),
-            pltpu.VMEM((2 * own, LANES), f32),
-        ],
-        50 << 20, 4 << 20,
-    )(x, halo, sums, off, gain_se.reshape(1, width), feat_se, fexp)
+    total = jnp.sum(lax.all_gather(part, "tp"), axis=0)
+    before = shifted(total, "ctx", 1)
+    off, fexp = call(
+        place_kernel, (shape((HALO + own, LANES), f32), shape((8, width), f32)), [], 1 << 24, 1 << 20, smem=1
+    )(first, total, doc_lengths, filter_se)
+    base = call(
+        turn_kernel, shape((groups, GROUP, LANES), f32), [pltpu.VMEM((groups, LANES), f32)], 1 << 24, 1 << 20
+    )(total, filter_mr)
+    gain = gain_se.reshape(1, width)
+    mid, part_two = se_own_call(x, total, off, gain, feat_se, fexp)
+    early, part_two = se_halo_call(x, halo, total, before, part_two, off, gain, feat_se, fexp)
     sums_two = lax.all_gather(part_two, "tp")
-    out = call(
-        mr_kernel,
-        shape((own, width), bf16),
-        [
-            pltpu.VMEM((ext, LANES), f32),
-            pltpu.VMEM((FEAT_TAPS - 1, ext, LANES), f32),
-            pltpu.VMEM((PAD + ext, LANES), f32),
-            pltpu.VMEM((own + LANES, LANES), bf16),
-            pltpu.VMEM((own, LANES), f32),
-            pltpu.VMEM((own // LANES, LANES, 2 * LANES), bf16),
-            pltpu.VMEM((own // LANES, (LANES // GROUP) * LANES, 2 * LANES), bf16),
-        ],
-        1 << 30, 4 << 20,
-    )(mid, sums_two, off, gain_mr.reshape(1, width), feat_mr, base)
-    return out[None]
+    return mr_call(early, mid, sums_two, off, gain_mr.reshape(1, width), feat_mr, base)[None]
 
 
 def solution(mesh):

time: 63.6 us -> 55.9 us (0.88)
  the two profiles are of different devices: /device:TPU:2 before, /device:TPU:34 now
where the time goes in v3:
time: 55.9 us; the launch traced here: 55.7 us
  blocking collectives  30 us (54%)
  Pallas kernels  20.2 us (36%)
  starting transfers between devices  3.94 us (7%)
  local copies, waits for them, and re-layouts  1.35 us (2%)
    pallas_call x6, Pallas kernels, run(): pl.pallas_call(kernel, out_shape=out_shape, in_specs=specs, out_specs=jax...  20.2 us
    all_gather x1, blocking collectives, shards(): sums_two = lax.all_gather(part_two, 'tp')  16.5 us
    all_gather x1, blocking collectives, shards(): total = jnp.sum(lax.all_gather(part, 'tp'), axis=0)  13.5 us
    ppermute x2, starting transfers between devices, shifted(): return lax.ppermute(x, axis, pairs)  3.94 us
    slice x1, local copies, waits for them, and re-layouts, shards(): halo = shifted(x[own - HALO:], 'ctx', 1)  1.2 us
  transfers between devices with their start and end apart: 2, of which 0 were waited for; matrix products, arithmetic and copies ran while one was open for 0% of the time, Pallas kernels for 12%

profile of v3, /device:TPU:34, one launch (start us, length us, event | category | flops | bytes accessed | tf_op | source)
XLA Modules:
  0.0 55.7 jit_solution(7586340884574765366)
XLA Ops:
  0.0 0.0 copy-start
  0.0 1.2 %slice_bitcast_fusion = bf16[144,2048]{1,0:T(8,128)(2,1)S(1)} fusion(bf16[1,256,2048]{2,1,0:T(8,128)(2,1)} %param.8), kind=kLoop, calls=%fused_computation | loop fusion | bytes 1179648 | tf_op jit(solution)/shard_map/slice | solution.py:329
  1.2 1.9 %collective-permute-start = (bf16[144,2048]{1,0:T(8,128)(2,1)S(1)}, bf16[144,2048]{1,0:T(8,128)(2,1)S(1)}, u32[]{:S(2)}, u32[]{:S(2)}) collective-permute-start(bf16[144,2048]{1,0:T(8,128)(2,1)S(1)} %slice_bitcast_fusion), channel_id=1, source_target_pairs={{0,4},{4,8},{8,12},{12,16},{16,20},{20,24},{24,28},{28,32},{32,36}... | collective-permute-start | bytes 1769480 | tf_op jit(solution)/shard_map/ppermute | solution.py:25
  3.1 0.0 copy-done
  3.1 0.0 copy-start.7
  3.2 0.0 copy-start.6
  3.2 0.4 shard_map.82
  3.6 0.0 copy-start.1
  3.6 13.5 %all-gather.2 = f32[4,1,256]{2,1,0:T(1,128)S(1)} all-gather(f32[1,1,256]{2,1,0:T(1,128)S(1)} %bitcast.21), channel_id=2, replica_groups=mesh['ctx'=64,'tp'=4] {'tp'}, dimensions={0}, use_global_device_ids=true | all-gather | bytes 5120 | tf_op jit(solution)/shard_map/all_gather | solution.py:331
  17.1 2.0 %collective-permute-start.1 = (f32[1,256]{1,0:T(1,128)S(1)}, f32[1,256]{1,0:T(1,128)S(1)}, u32[]{:S(2)}, u32[]{:S(2)}) collective-permute-start(f32[1,256]{1,0:T(1,128)S(1)} %bitcast.15), channel_id=1, source_target_pairs={{0,4},{4,8},{8,12},{12,16},{16,20},{20,24},{24,28},{28,32},{32,36}... | collective-permute-start | bytes 3080 | tf_op jit(solution)/shard_map/ppermute | solution.py:25
  19.1 0.0 copy-done.7
  19.1 0.1 copy.10.fse_ref
  19.2 0.0 copy-done.6
  19.2 0.0 copy-start.3
  19.3 0.7 %shard_map.83 = (f32[400,128]{1,0:T(8,128)S(1)}, f32[8,2048]{1,0:T(8,128)S(1)}) custom-call(s32[1]{0:T(128)} %bitcast.4.first_ref, f32[1,256]{1,0:T(1,128)S(1)} %bitcast.16, s32[1,128]{1,0:T(1,128)S(1)} %copy-done.6, f32[128,7]{1,0:T(8,128)S(1)} %copy.10.fse_ref), custom_call_target="tpu_custom_call" | custom-call | flops 16777216 | bytes 1048576 | tf_op jit(solution)/shard_map/pallas_call | solution.py:274
  20.0 0.0 copy-done.1
  20.0 0.0 copy-done.3
  20.0 0.0 copy-start.4
  20.0 3.9 %shard_map.84 = (bf16[256,2048]{1,0:T(8,128)(2,1)S(1)}, f32[1,256]{1,0:T(1,128)S(1)}) custom-call(bf16[256,2048]{1,0:T(8,128)(2,1)S(1)} %bitcast.11, f32[1,256]{1,0:T(1,128)S(1)} %bitcast.17, f32[400,128]{1,0:T(8,128)S(1)} %get-tuple-element.11.off_ref, f32[1,2048]{1,0:T(1,128)S(1)} %bitcast.13, f32[3,3,2048]{2,1,0:T(4,128)S(1)} %copy-done.1, ...), custom_call_target="tpu_custom_call" | custom-call | flops 26214400 | bytes 2097152 | tf_op jit(solution)/shard_map/pallas_call | solution.py:274
  23.8 0.0 copy-done.4
  23.9 1.5 %shard_map.86.base_ref = f32[128,16,128]{2,1,0:T(8,128)S(1)} custom-call(f32[1,256]{1,0:T(1,128)S(1)} %bitcast.18, bf16[128,128]{1,0:T(8,128)(2,1)S(1)} %copy-done.4), custom_call_target="tpu_custom_call" | custom-call | flops 16777216 | bytes 1048576 | tf_op jit(solution)/shard_map/pallas_call | solution.py:274
  25.3 0.0 collective-permute-done.1.before_ref
  25.3 0.0 collective-permute-done.halo_ref
  25.3 0.0 copy-start.2
  25.4 2.8 %shard_map.85 = (bf16[160,2048]{1,0:T(8,128)(2,1)S(1)}, f32[2,256]{1,0:T(2,128)S(1)}) custom-call(bf16[256,2048]{1,0:T(8,128)(2,1)S(1)} %bitcast.12, bf16[144,2048]{1,0:T(8,128)(2,1)S(1)} %collective-permute-done.halo_ref, f32[1,256]{1,0:T(1,128)S(1)} %bitcast.19, f32[1,256]{1,0:T(1,128)S(1)} %collective-permute-done.1.before_ref, ...), custom_call_target="tpu_custom_call" | custom-call | flops 26214400 | bytes 2097152 | tf_op jit(solution)/shard_map/pallas_call | solution.py:274
  28.2 0.0 copy-start.5
  28.2 16.5 %all-gather.3.sums_ref = f32[4,2,256]{2,1,0:T(2,128)S(1)} all-gather(f32[1,2,256]{2,1,0:T(2,128)S(1)} %bitcast.22), channel_id=3, replica_groups=mesh['ctx'=64,'tp'=4] {'tp'}, dimensions={0}, use_global_device_ids=true | all-gather | bytes 10240 | tf_op jit(solution)/shard_map/all_gather | solution.py:342
  44.7 0.0 copy-done.2
  44.7 0.0 copy-done.5
  44.7 11.0 %shard_map.87 = bf16[256,2048]{1,0:T(8,128)(2,1)} custom-call(bf16[160,2048]{1,0:T(8,128)(2,1)S(1)} %get-tuple-element.14.early_ref, bf16[256,2048]{1,0:T(8,128)(2,1)S(1)} %get-tuple-element.15.mid_ref, f32[4,2,256]{2,1,0:T(2,128)S(1)} %all-gather.3.sums_ref, f32[400,128]{1,0:T(8,128)S(1)} %get-tuple-element.11.off_ref, f32[1,2048]{1,0:T(1,128)S(1)} %bitcast.20, ...), custom_call_target="tpu_custom_call" | custom-call | flops 1073741824 | bytes 4194304 | tf_op jit(solution)/shard_map/pallas_call | solution.py:274
  (1 shorter events, 0.0 us)
Async XLA Ops:
  0.0 3.1 %copy-start = (bf16[1,256,2048]{2,1,0:T(8,128)(2,1)S(1)}, bf16[1,256,2048]{2,1,0:T(8,128)(2,1)}, u32[]{:S(2)}) copy-start(bf16[1,256,2048]{2,1,0:T(8,128)(2,1)} %param.8) | copy-start | bytes 3145732
  1.2 24.1 %collective-permute-start = (bf16[144,2048]{1,0:T(8,128)(2,1)S(1)}, bf16[144,2048]{1,0:T(8,128)(2,1)S(1)}, u32[]{:S(2)}, u32[]{:S(2)}) collective-permute-start(bf16[144,2048]{1,0:T(8,128)(2,1)S(1)} %slice_bitcast_fusion), channel_id=1, source_target_pairs={{0,4},{4,8},{8,12},{12,16},{16,20},{20,24},{24,28},{28,32},{32,36}... | collective-permute-start | bytes 1769480 | tf_op jit(solution)/shard_map/ppermute | solution.py:25
  3.1 16.0 %copy-start.7 = (f32[128,7]{0,1:T(8,128)S(1)}, f32[128,7]{0,1:T(8,128)}, u32[]{:S(2)}) copy-start(f32[128,7]{0,1:T(8,128)} %param.14) | copy-start | bytes 10756
  3.2 16.1 %copy-start.6 = (s32[1,128]{1,0:T(1,128)S(1)}, s32[1,128]{1,0:T(1,128)}, u32[]{:S(2)}) copy-start(s32[1,128]{1,0:T(1,128)} %len_ref.1) | copy-start | bytes 1540
  3.6 16.4 %copy-start.1 = (f32[3,3,2048]{2,1,0:T(4,128)S(1)}, f32[3,3,2048]{2,1,0:T(4,128)}, u32[]{:S(2)}) copy-start(f32[3,3,2048]{2,1,0:T(4,128)} %feat_ref.4) | copy-start | bytes 221188
  17.1 8.3 %collective-permute-start.1 = (f32[1,256]{1,0:T(1,128)S(1)}, f32[1,256]{1,0:T(1,128)S(1)}, u32[]{:S(2)}, u32[]{:S(2)}) collective-permute-start(f32[1,256]{1,0:T(1,128)S(1)} %bitcast.15), channel_id=1, source_target_pairs={{0,4},{4,8},{8,12},{12,16},{16,20},{20,24},{24,28},{28,32},{32,36}... | collective-permute-start | bytes 3080 | tf_op jit(solution)/shard_map/ppermute | solution.py:25
  19.2 0.7 %copy-start.3 = (f32[2048]{0:T(1024)S(1)}, f32[2048]{0:T(1024)}, u32[]{:S(2)}) copy-start(f32[2048]{0:T(1024)} %param.10) | copy-start | bytes 24580
  20.0 3.9 %copy-start.4 = (bf16[128,128]{1,0:T(8,128)(2,1)S(1)}, bf16[128,128]{1,0:T(8,128)(2,1)}, u32[]{:S(2)}) copy-start(bf16[128,128]{1,0:T(8,128)(2,1)} %fmr_ref.1) | copy-start | bytes 98308
  25.3 19.3 %copy-start.2 = (f32[3,3,2048]{2,1,0:T(4,128)S(1)}, f32[3,3,2048]{2,1,0:T(4,128)}, u32[]{:S(2)}) copy-start(f32[3,3,2048]{2,1,0:T(4,128)} %feat_ref.5) | copy-start | bytes 221188
  28.2 16.5 %copy-start.5 = (f32[2048]{0:T(1024)S(1)}, f32[2048]{0:T(1024)}, u32[]{:S(2)}) copy-start(f32[2048]{0:T(1024)} %param.11) | copy-start | bytes 24580

commit v4 on v3

--- a/solution.py
+++ b/solution.py
@@ -23,6 +23,11 @@
     peers = lax.axis_size(axis)
     pairs = [(i, i + by) for i in range(peers) if 0 <= i + by < peers]
     return lax.ppermute(x, axis, pairs)
+
+
+def turned(x, axis, by):
+    peers = lax.axis_size(axis)
+    return lax.ppermute(x, axis, [(i, (i + by) % peers) for i in range(peers)])
 
 
 def as_row(column):
@@ -48,7 +53,7 @@
             s_ref[0:1, r - 64 : r + 64] = as_row(jnp.concatenate([held, col], axis=0))
 
 
-def place_kernel(first_ref, after_ref, len_ref, fse_ref, off_ref, fexp_ref):
+def place_kernel(first_ref, len_ref, fse_ref, off_ref, fexp_ref):
     ext = off_ref.shape[0]
     width = fexp_ref.shape[1]
     groups = fse_ref.shape[0]
@@ -78,10 +83,7 @@
 
 def turn_kernel(after_ref, fmr_ref, base_ref, rev_ref):
     groups = fmr_ref.shape[0]
-    row = lax.broadcasted_iota(jnp.int32, (LANES, LANES), 0)
-    col = lax.broadcasted_iota(jnp.int32, (LANES, LANES), 1)
-    flip = ((row + col) % MEDIUM_TAPS == 0).astype(jnp.bfloat16)
-    rev_ref[...] = jnp.dot(fmr_ref[...], flip, preferred_element_type=jnp.float32)
+    rev_ref[...] = fmr_ref[...].astype(jnp.float32)
 
     def one(g, carry):
         h = jnp.broadcast_to(rev_ref[pl.ds(g, 1), :], (GROUP, LANES))
@@ -96,14 +98,13 @@
 
 
 def scale_columns(sums_ref, scale_ref):
-    tp = sums_ref.shape[0]
-    total = sums_ref[0]
-    for i in range(1, tp):
-        total = total + sums_ref[i]
+    total = sums_ref[0][...]
+    for other in sums_ref[1:]:
+        total = total + other[...]
     scale = scale_of(total)
-    own = scale.shape[1]
-    scale_ref[0:HALO, :] = as_column(scale[0:1])[own - HALO :, :]
-    scale_ref[HALO:, :] = as_column(scale[1:2])
+    own = scale.shape[1] // 2
+    scale_ref[0:HALO, :] = as_column(scale[:, 0:own])[own - HALO :, :]
+    scale_ref[HALO:, :] = as_column(scale[:, own:])
 
 
 def masks_of(off_ref, mask_ref, taps, first=0):
@@ -191,76 +192,95 @@
     halo_part = jnp.concatenate([jnp.zeros((own - HALO, 1), jnp.float32), halo_part], axis=0)
     own_part = jnp.sum(acc_ref[HALO:, :], axis=1, keepdims=True)
     own_part = jnp.concatenate([own_part, jnp.zeros((own - CHUNK, 1), jnp.float32)], axis=0)
-    s_ref[0:1, :] = as_row(halo_part)
-    s_ref[1:2, :] = as_row(own_part) + part_ref[...]
+    s_ref[0:1, 0:own] = as_row(halo_part)
+    s_ref[0:1, own:] = as_row(own_part) + part_ref[...]
 
 
 def mr_kernel(
-    early_ref, mid_ref, sums_ref, off_ref, gain_ref, feat_ref, base_ref, out_ref,
-    scale_ref, mask_ref, norm_ref, mixed_ref, q_ref, keep_ref, toep_ref,
+    early_ref, mid_ref, sums0_ref, sums1_ref, sums2_ref, sums3_ref, off_ref, gain_ref, feat_ref, base_ref, out_ref,
+    scale_ref, mask_ref, norm_ref, keep_ref, *slots,
 ):
     own, width = mid_ref.shape
     ext = HALO + own
     blocks = own // LANES
     per_tile = LANES // GROUP
-    scale_columns(sums_ref, scale_ref)
+    scale_columns((sums0_ref, sums1_ref, sums2_ref, sums3_ref), scale_ref)
     masks_of(off_ref, mask_ref, FEAT_TAPS)
     norm_ref[0:PAD, :] = jnp.zeros((PAD, LANES), jnp.float32)
     row = lax.broadcasted_iota(jnp.int32, (LANES, LANES), 0)
     col = lax.broadcasted_iota(jnp.int32, (LANES, LANES), 1)
     for b in range(blocks):
-        off = off_ref[HALO + b * LANES : HALO + (b + 1) * LANES, :]
-        lag = (row - col).astype(jnp.float32)
-        before = (col > row) & (lag + MEDIUM_TAPS <= off)
-        within = (row >= col) & (lag <= off)
-        keep_ref[b, :, 0:LANES] = before.astype(jnp.float32).astype(jnp.bfloat16)
-        keep_ref[b, :, LANES:] = within.astype(jnp.float32).astype(jnp.bfloat16)
+        off = off_ref[HALO + b * LANES : HALO + (b + 1) * LANES, :].T
+        lag = (col - row).astype(jnp.float32)
+        before = (row > col) & (lag + MEDIUM_TAPS <= off)
+        within = (row <= col) & (lag <= off)
+        at = slice(b * LANES, (b + 1) * LANES)
+        keep_ref[0:LANES, at] = before.astype(jnp.float32).astype(jnp.bfloat16)
+        keep_ref[LANES:, at] = within.astype(jnp.float32).astype(jnp.bfloat16)
     early = early_ref.shape[0]
 
     def middle(e, cols):
         held = early_ref[e : e + CHUNK, cols] if e < early else mid_ref[e - HALO : e - HALO + CHUNK, cols]
         return held.astype(jnp.float32)
 
-    group_of = lax.broadcasted_iota(jnp.int32, (LANES, LANES), 1) // GROUP
-
-    def tile(i, carry):
+
+    def ready(i, slot):
+        mixed_ref, q_ref = slot
         cols = pl.ds(pl.multiple_of(i * LANES, LANES), LANES)
         gain = gain_ref[0:1, cols]
         for e in range(0, ext, CHUNK):
             n = middle(e, cols) * scale_ref[e : e + CHUNK, :] * gain
             norm_ref[PAD + e : PAD + e + CHUNK, :] = n.astype(jnp.bfloat16).astype(jnp.float32)
         taps = [[feat_ref[s, j : j + 1, cols] for j in range(FEAT_TAPS)] for s in range(3)]
+        prods = []
         for e in range(HALO - LANES, ext, CHUNK):
             xs = [norm_ref[PAD + e : PAD + e + CHUNK, :]]
             for j in range(1, FEAT_TAPS):
                 xs.append(norm_ref[PAD + e - j : PAD + e - j + CHUNK, :] * mask_ref[j - 1, e : e + CHUNK, :])
             k, v = (taps[s][0] * xs[0] + taps[s][1] * xs[1] + taps[s][2] * xs[2] for s in (1, 2))
-            w = e - (HALO - LANES)
-            mixed_ref[w : w + CHUNK, :] = (k * v).astype(jnp.bfloat16)
+            prods.append(k * v)
+            if len(prods) == LANES // CHUNK:
+                w = e + CHUNK - HALO
+                mixed_ref[:, w : w + LANES] = jnp.concatenate(prods, axis=0).T.astype(jnp.bfloat16)
+                prods = []
             if e >= HALO:
                 q = taps[0][0] * xs[0] + taps[0][1] * xs[1] + taps[0][2] * xs[2]
                 q_ref[e - HALO : e - HALO + CHUNK, :] = q
+
+    def finish(i, slot):
+        mixed_ref, q_ref = slot
+        cols = pl.ds(pl.multiple_of(i * LANES, LANES), LANES)
+        parts = [[] for _ in range(blocks)]
         for g in range(per_tile):
-            base = base_ref[i * per_tile + g]
-            for r in range(0, LANES, GROUP):
-                turned = (pltpu.roll(base, r, 1) if r else base).astype(jnp.bfloat16)
-                for b in range(blocks):
-                    at = slice(g * LANES + r, g * LANES + r + GROUP)
-                    toep_ref[b, at, 0:LANES] = turned * keep_ref[b, r : r + GROUP, 0:LANES]
-                    toep_ref[b, at, LANES:] = turned * keep_ref[b, r : r + GROUP, LANES:]
+            base = base_ref[i * per_tile + g].astype(jnp.bfloat16)
+            circ = jnp.concatenate([pltpu.roll(base, r, 1) if r else base for r in range(0, LANES, GROUP)], axis=0)
+            rows = slice(g * GROUP, (g + 1) * GROUP)
+            toep = jnp.concatenate([jnp.concatenate([circ] * blocks, axis=1)] * 2, axis=0) * keep_ref[...]
+            window = jnp.concatenate(
+                [mixed_ref[rows, b * LANES : (b + 2) * LANES] for b in range(blocks)], axis=0
+            )
+            y = jnp.dot(window, toep, preferred_element_type=jnp.float32)
+            for b in range(blocks):
+                parts[b].append(y[b * GROUP : (b + 1) * GROUP, b * LANES : (b + 1) * LANES])
+        medium = [jnp.concatenate(part, axis=0).T for part in parts]
         for b in range(blocks):
-            window = mixed_ref[b * LANES : (b + 2) * LANES, :]
-            y = jnp.dot(toep_ref[b], window, preferred_element_type=jnp.float32)
-            medium = y[0:LANES]
-            for g in range(1, per_tile):
-                medium = jnp.where(group_of == g, y[g * LANES : (g + 1) * LANES], medium)
             for r in range(0, LANES, CHUNK):
                 t = b * LANES + r
-                out = middle(HALO + t, cols) + q_ref[t : t + CHUNK, :] * medium[r : r + CHUNK]
+                out = middle(HALO + t, cols) + q_ref[t : t + CHUNK, :] * medium[b][r : r + CHUNK]
                 out_ref[t : t + CHUNK, cols] = out.astype(jnp.bfloat16)
+
+    tiles = width // LANES
+    slots = (slots[:2], slots[2:])
+    ready(0, slots[0])
+
+    def pair(j, carry):
+        for at in range(2):
+            i = 2 * j + at
+            ready(jnp.minimum(i + 1, tiles - 1), slots[1 - at])
+            finish(i, slots[at])
         return carry
 
-    lax.fori_loop(0, width // LANES, tile, 0)
+    lax.fori_loop(0, tiles // 2, pair, 0)
 
 
 def call(kernel, out_shape, scratch, flops, nbytes, smem=0):
@@ -300,21 +320,25 @@
 def se_halo_call(x, *rest):
     own, width = x.shape
     rows = HALO + CHUNK
-    shapes = (jax.ShapeDtypeStruct((rows, width), jnp.bfloat16), jax.ShapeDtypeStruct((2, own), jnp.float32))
+    shapes = (jax.ShapeDtypeStruct((rows, width), jnp.bfloat16), jax.ShapeDtypeStruct((1, 2 * own), jnp.float32))
     return call(se_halo_kernel, shapes, se_scratch(rows), 25 << 20, 2 << 20)(x, *rest)
 
 
 def mr_call(early, mid, *rest):
     own, width = mid.shape
     ext = HALO + own
+    blocks = own // LANES
+    slot = [
+        pltpu.VMEM((LANES, own + LANES), jnp.bfloat16),
+        pltpu.VMEM((own, LANES), jnp.float32),
+    ]
     scratch = [
         pltpu.VMEM((ext, LANES), jnp.float32),
         pltpu.VMEM((FEAT_TAPS - 1, ext, LANES), jnp.float32),
         pltpu.VMEM((PAD + ext, LANES), jnp.float32),
-        pltpu.VMEM((own + LANES, LANES), jnp.bfloat16),
-        pltpu.VMEM((own, LANES), jnp.float32),
-        pltpu.VMEM((own // LANES, LANES, 2 * LANES), jnp.bfloat16),
-        pltpu.VMEM((own // LANES, (LANES // GROUP) * LANES, 2 * LANES), jnp.bfloat16),
+        pltpu.VMEM((2 * LANES, blocks * LANES), jnp.bfloat16),
+        *slot,
+        *slot,
     ]
     return call(mr_kernel, jax.ShapeDtypeStruct((own, width), jnp.bfloat16), scratch, 1 << 30, 4 << 20)(early, mid, *rest)
 
@@ -328,19 +352,19 @@
     first = (lax.axis_index("ctx") * own).astype(jnp.int32).reshape(1)
     halo = shifted(x[own - HALO :], "ctx", 1)
     part = call(sums_kernel, shape((1, own), f32), [], 1 << 20, 1 << 20)(x)
-    total = jnp.sum(lax.all_gather(part, "tp"), axis=0)
+    total = part + turned(part, "tp", 3) + turned(part, "tp", 1) + turned(part, "tp", 2)
     before = shifted(total, "ctx", 1)
     off, fexp = call(
         place_kernel, (shape((HALO + own, LANES), f32), shape((8, width), f32)), [], 1 << 24, 1 << 20, smem=1
-    )(first, total, doc_lengths, filter_se)
+    )(first, doc_lengths, filter_se)
     base = call(
         turn_kernel, shape((groups, GROUP, LANES), f32), [pltpu.VMEM((groups, LANES), f32)], 1 << 24, 1 << 20
     )(total, filter_mr)
     gain = gain_se.reshape(1, width)
     mid, part_two = se_own_call(x, total, off, gain, feat_se, fexp)
     early, part_two = se_halo_call(x, halo, total, before, part_two, off, gain, feat_se, fexp)
-    sums_two = lax.all_gather(part_two, "tp")
-    return mr_call(early, mid, sums_two, off, gain_mr.reshape(1, width), feat_mr, base)[None]
+    sums_two = [part_two] + [turned(part_two, "tp", by) for by in (3, 1, 2)]
+    return mr_call(early, mid, *sums_two, off, gain_mr.reshape(1, width), feat_mr, base)[None]
 
 
 def solution(mesh):

time: 55.9 us -> 45.5 us (0.81)
  the two profiles are of different devices: /device:TPU:34 before, /device:TPU:2 now
where the time goes in v4:
time: 45.5 us; the launch traced here: 45.4 us
  starting transfers between devices  22.7 us (50%)
  Pallas kernels  16.2 us (36%)
  waiting for transfers between devices  5.08 us (11%)
  local copies, waits for them, and re-layouts  1.34 us (3%)
    ppermute x6, starting transfers between devices, turned(): return lax.ppermute(x, axis, [(i, (i + by) % peers) for i in range(peers)])  17.1 us
    pallas_call x6, Pallas kernels, run(): pl.pallas_call(kernel, out_shape=out_shape, in_specs=specs, out_specs=jax...  16.2 us
    ppermute x2, starting transfers between devices, shifted(): return lax.ppermute(x, axis, pairs)  5.55 us
    ppermute x6, waiting for transfers between devices, turned(): return lax.ppermute(x, axis, [(i, (i + by) % peers) for i in range(peers)])  4.13 us
    slice x1, local copies, waits for them, and re-layouts, shards(): halo = shifted(x[own - HALO:], 'ctx', 1)  1.19 us
    ppermute x2, waiting for transfers between devices, shifted(): return lax.ppermute(x, axis, pairs)  0.95 us
  transfers between devices with their start and end apart: 8, of which 5 were waited for; matrix products, arithmetic and copies ran while one was open for 0% of the time, Pallas kernels for 14%

profile of v4, /device:TPU:2, one launch (start us, length us, event | category | flops | bytes accessed | tf_op | source)
XLA Modules:
  0.0 45.4 jit_solution(5706524218205588572)
XLA Ops:
  0.0 0.0 copy-start
  0.0 1.2 %slice_bitcast_fusion = bf16[144,2048]{1,0:T(8,128)(2,1)S(1)} fusion(bf16[1,256,2048]{2,1,0:T(8,128)(2,1)} %param.8), kind=kLoop, calls=%fused_computation | loop fusion | bytes 1179648 | tf_op jit(solution)/shard_map/slice | solution.py:353
  1.2 1.9 %collective-permute-start = (bf16[144,2048]{1,0:T(8,128)(2,1)S(1)}, bf16[144,2048]{1,0:T(8,128)(2,1)S(1)}, u32[]{:S(2)}, u32[]{:S(2)}) collective-permute-start(bf16[144,2048]{1,0:T(8,128)(2,1)S(1)} %slice_bitcast_fusion), channel_id=1, source_target_pairs={{0,4},{4,8},{8,12},{12,16},{16,20},{20,24},{24,28},{28,32},{32,36}... | collective-permute-start | bytes 1769480 | tf_op jit(solution)/shard_map/ppermute | solution.py:25
  3.1 0.0 copy-done
  3.1 0.0 copy-start.7
  3.1 0.0 copy-start.6
  3.2 0.4 shard_map.82
  3.6 0.0 copy-start.1
  3.6 7.3 %collective-permute-start.3 = (f32[1,256]{1,0:T(1,128)S(1)}, f32[1,256]{1,0:T(1,128)S(1)}, u32[]{:S(2)}, u32[]{:S(2)}) collective-permute-start(f32[1,256]{1,0:T(1,128)S(1)} %shard_map.82), channel_id=1, source_target_pairs={{0,2},{1,3},{2,0},{3,1},{4,6},{5,7},{6,4},{7,5},{8,10},{9,11},{10,... | collective-permute-start | bytes 3080 | tf_op jit(solution)/shard_map/ppermute | solution.py:30
  10.8 1.5 %collective-permute-start.2 = (f32[1,256]{1,0:T(1,128)S(1)}, f32[1,256]{1,0:T(1,128)S(1)}, u32[]{:S(2)}, u32[]{:S(2)}) collective-permute-start(f32[1,256]{1,0:T(1,128)S(1)} %shard_map.82), channel_id=1, source_target_pairs={{0,1},{1,2},{2,3},{3,0},{4,5},{5,6},{6,7},{7,4},{8,9},{9,10},{10,1... | collective-permute-start | bytes 3080 | tf_op jit(solution)/shard_map/ppermute | solution.py:30
  12.3 2.7 %collective-permute-start.1 = (f32[1,256]{1,0:T(1,128)S(1)}, f32[1,256]{1,0:T(1,128)S(1)}, u32[]{:S(2)}, u32[]{:S(2)}) collective-permute-start(f32[1,256]{1,0:T(1,128)S(1)} %shard_map.82), channel_id=1, source_target_pairs={{0,3},{1,0},{2,1},{3,2},{4,7},{5,4},{6,5},{7,6},{8,11},{9,8},{10,9... | collective-permute-start | bytes 3080 | tf_op jit(solution)/shard_map/ppermute | solution.py:30
  15.0 0.0 copy-done.7
  15.0 0.1 copy.9.fse_ref
  15.1 0.0 copy-done.6
  15.1 0.7 %shard_map.83 = (f32[400,128]{1,0:T(8,128)S(1)}, f32[8,2048]{1,0:T(8,128)S(1)}) custom-call(s32[1]{0:T(128)} %bitcast.2.first_ref, s32[1,128]{1,0:T(1,128)S(1)} %copy-done.6, f32[128,7]{1,0:T(8,128)S(1)} %copy.9.fse_ref), custom_call_target="tpu_custom_call" | custom-call | flops 16777216 | bytes 1048576 | tf_op jit(solution)/shard_map/pallas_call | solution.py:294
  15.8 0.0 copy-start.3
  15.8 0.0 collective-permute-done.3
  15.8 0.8 %collective-permute-done.2 = f32[1,256]{1,0:T(1,128)S(1)} collective-permute-done((f32[1,256]{1,0:T(1,128)S(1)}, f32[1,256]{1,0:T(1,128)S(1)}, u32[]{:S(2)}, u32[]{:S(2)}) %collective-permute-start.2) | collective-permute-done | bytes 1056 | tf_op jit(solution)/shard_map/ppermute | solution.py:30
  16.6 0.2 collective-permute-done.1
  16.8 3.6 %collective-permute-start.4 = (f32[1,256]{1,0:T(1,128)S(1)}, f32[1,256]{1,0:T(1,128)S(1)}, u32[]{:S(2)}, u32[]{:S(2)}) collective-permute-start(f32[1,256]{1,0:T(1,128)S(1)} %add_add_fusion.total_ref.after_ref), channel_id=1, source_target_pairs={{0,4},{4,8},{8,12},{12,16},{16,20},{20,24},{24,28},{28,32},{32,36}... | collective-permute-start | bytes 3080 | tf_op jit(solution)/shard_map/ppermute | solution.py:25
  20.4 0.0 copy-done.1
  20.4 0.0 copy-done.3
  20.4 3.9 %shard_map.84 = (bf16[256,2048]{1,0:T(8,128)(2,1)S(1)}, f32[1,256]{1,0:T(1,128)S(1)}) custom-call(bf16[256,2048]{1,0:T(8,128)(2,1)S(1)} %bitcast.8, f32[1,256]{1,0:T(1,128)S(1)} %add_add_fusion.total_ref.after_ref, f32[400,128]{1,0:T(8,128)S(1)} %get-tuple-element.11.off_ref, f32[1,2048]{1,0:T(1,128)S(1)} %bitcast.10, f32[3,3,2048]{2,1,0:T(4,128)S(1)} %copy-done.1, ...), custom_call_target="tpu_custom_call" | custom-call | flops 26214400 | bytes 2097152 | tf_op jit(solution)/shard_map/pallas_call | solution.py:294
  24.3 0.9 %collective-permute-done.4.before_ref = f32[1,256]{1,0:T(1,128)S(1)} collective-permute-done((f32[1,256]{1,0:T(1,128)S(1)}, f32[1,256]{1,0:T(1,128)S(1)}, u32[]{:S(2)}, u32[]{:S(2)}) %collective-permute-start.4) | collective-permute-done | bytes 1056 | tf_op jit(solution)/shard_map/ppermute | solution.py:25
  25.2 0.0 collective-permute-done.halo_ref
  25.2 0.0 copy-start.4
  25.2 2.8 %shard_map.85 = (bf16[160,2048]{1,0:T(8,128)(2,1)S(1)}, f32[1,512]{1,0:T(1,128)S(1)}) custom-call(bf16[256,2048]{1,0:T(8,128)(2,1)S(1)} %bitcast.9, bf16[144,2048]{1,0:T(8,128)(2,1)S(1)} %collective-permute-done.halo_ref, f32[1,256]{1,0:T(1,128)S(1)} %add_add_fusion.total_ref.after_ref, f32[1,256]{1,0:T(1,128)S(1)} %collective-permute-done.4.before_ref, ...), custom_call_target="tpu_custom_call" | custom-call | flops 26214400 | bytes 2097152 | tf_op jit(solution)/shard_map/pallas_call | solution.py:294
  28.1 0.0 copy-start.2
  28.1 1.6 %collective-permute-start.7 = (f32[1,512]{1,0:T(1,128)S(1)}, f32[1,512]{1,0:T(1,128)S(1)}, u32[]{:S(2)}, u32[]{:S(2)}) collective-permute-start(f32[1,512]{1,0:T(1,128)S(1)} %get-tuple-element.16.sums0_ref), channel_id=1, source_target_pairs={{0,2},{1,3},{2,0},{3,1},{4,6},{5,7},{6,4},{7,5},{8,10},{9,11},{10,... | collective-permute-start | bytes 6152 | tf_op jit(solution)/shard_map/ppermute | solution.py:30
  29.6 4.1 %collective-permute-start.6 = (f32[1,512]{1,0:T(1,128)S(1)}, f32[1,512]{1,0:T(1,128)S(1)}, u32[]{:S(2)}, u32[]{:S(2)}) collective-permute-start(f32[1,512]{1,0:T(1,128)S(1)} %get-tuple-element.16.sums0_ref), channel_id=1, source_target_pairs={{0,1},{1,2},{2,3},{3,0},{4,5},{5,6},{6,7},{7,4},{8,9},{9,10},{10,1... | collective-permute-start | bytes 6152 | tf_op jit(solution)/shard_map/ppermute | solution.py:30
  33.8 0.0 collective-permute-start.5
  33.8 0.0 copy-done.4
  33.8 0.0 copy-start.5
  33.8 1.3 %shard_map.86.base_ref = f32[128,16,128]{2,1,0:T(8,128)S(1)} custom-call(f32[1,256]{1,0:T(1,128)S(1)} %add_add_fusion.total_ref.after_ref, bf16[128,128]{1,0:T(8,128)(2,1)S(1)} %copy-done.4), custom_call_target="tpu_custom_call" | custom-call | flops 16777216 | bytes 1048576 | tf_op jit(solution)/shard_map/pallas_call | solution.py:294
  35.1 0.5 %collective-permute-done.7.sums3_ref = f32[1,512]{1,0:T(1,128)S(1)} collective-permute-done((f32[1,512]{1,0:T(1,128)S(1)}, f32[1,512]{1,0:T(1,128)S(1)}, u32[]{:S(2)}, u32[]{:S(2)}) %collective-permute-start.7) | collective-permute-done | bytes 2080 | tf_op jit(solution)/shard_map/ppermute | solution.py:30
  35.6 0.0 collective-permute-done.6.sums2_ref
  35.6 2.6 %collective-permute-done.5.sums1_ref = f32[1,512]{1,0:T(1,128)S(1)} collective-permute-done((f32[1,512]{1,0:T(1,128)S(1)}, f32[1,512]{1,0:T(1,128)S(1)}, u32[]{:S(2)}, u32[]{:S(2)}) %collective-permute-start.5) | collective-permute-done | bytes 2080 | tf_op jit(solution)/shard_map/ppermute | solution.py:30
  38.2 0.0 copy-done.2
  38.2 0.0 copy-done.5
  38.2 7.1 %shard_map.87 = bf16[256,2048]{1,0:T(8,128)(2,1)} custom-call(bf16[160,2048]{1,0:T(8,128)(2,1)S(1)} %get-tuple-element.14.early_ref, bf16[256,2048]{1,0:T(8,128)(2,1)S(1)} %get-tuple-element.15.mid_ref, f32[1,512]{1,0:T(1,128)S(1)} %get-tuple-element.16.sums0_ref, f32[1,512]{1,0:T(1,128)S(1)} %collective-permute-done.5.sums1_ref, ...), custom_call_target="tpu_custom_call" | custom-call | flops 1073741824 | bytes 4194304 | tf_op jit(solution)/shard_map/pallas_call | solution.py:294
  (1 shorter events, 0.0 us)
Async XLA Ops:
  0.0 3.1 %copy-start = (bf16[1,256,2048]{2,1,0:T(8,128)(2,1)S(1)}, bf16[1,256,2048]{2,1,0:T(8,128)(2,1)}, u32[]{:S(2)}) copy-start(bf16[1,256,2048]{2,1,0:T(8,128)(2,1)} %param.8) | copy-start | bytes 3145732
  1.2 24.0 %collective-permute-start = (bf16[144,2048]{1,0:T(8,128)(2,1)S(1)}, bf16[144,2048]{1,0:T(8,128)(2,1)S(1)}, u32[]{:S(2)}, u32[]{:S(2)}) collective-permute-start(bf16[144,2048]{1,0:T(8,128)(2,1)S(1)} %slice_bitcast_fusion), channel_id=1, source_target_pairs={{0,4},{4,8},{8,12},{12,16},{16,20},{20,24},{24,28},{28,32},{32,36}... | collective-permute-start | bytes 1769480 | tf_op jit(solution)/shard_map/ppermute | solution.py:25
  3.1 11.8 %copy-start.7 = (f32[128,7]{0,1:T(8,128)S(1)}, f32[128,7]{0,1:T(8,128)}, u32[]{:S(2)}) copy-start(f32[128,7]{0,1:T(8,128)} %param.14) | copy-start | bytes 10756
  3.1 11.9 %copy-start.6 = (s32[1,128]{1,0:T(1,128)S(1)}, s32[1,128]{1,0:T(1,128)}, u32[]{:S(2)}) copy-start(s32[1,128]{1,0:T(1,128)} %len_ref.1) | copy-start | bytes 1540
  3.6 16.8 %copy-start.1 = (f32[3,3,2048]{2,1,0:T(4,128)S(1)}, f32[3,3,2048]{2,1,0:T(4,128)}, u32[]{:S(2)}) copy-start(f32[3,3,2048]{2,1,0:T(4,128)} %feat_ref.4) | copy-start | bytes 221188
  3.6 12.2 %collective-permute-start.3 = (f32[1,256]{1,0:T(1,128)S(1)}, f32[1,256]{1,0:T(1,128)S(1)}, u32[]{:S(2)}, u32[]{:S(2)}) collective-permute-start(f32[1,256]{1,0:T(1,128)S(1)} %shard_map.82), channel_id=1, source_target_pairs={{0,2},{1,3},{2,0},{3,1},{4,6},{5,7},{6,4},{7,5},{8,10},{9,11},{10,... | collective-permute-start | bytes 3080 | tf_op jit(solution)/shard_map/ppermute | solution.py:30
  10.8 5.8 %collective-permute-start.2 = (f32[1,256]{1,0:T(1,128)S(1)}, f32[1,256]{1,0:T(1,128)S(1)}, u32[]{:S(2)}, u32[]{:S(2)}) collective-permute-start(f32[1,256]{1,0:T(1,128)S(1)} %shard_map.82), channel_id=1, source_target_pairs={{0,1},{1,2},{2,3},{3,0},{4,5},{5,6},{6,7},{7,4},{8,9},{9,10},{10,1... | collective-permute-start | bytes 3080 | tf_op jit(solution)/shard_map/ppermute | solution.py:30
  12.3 4.5 %collective-permute-start.1 = (f32[1,256]{1,0:T(1,128)S(1)}, f32[1,256]{1,0:T(1,128)S(1)}, u32[]{:S(2)}, u32[]{:S(2)}) collective-permute-start(f32[1,256]{1,0:T(1,128)S(1)} %shard_map.82), channel_id=1, source_target_pairs={{0,3},{1,0},{2,1},{3,2},{4,7},{5,4},{6,5},{7,6},{8,11},{9,8},{10,9... | collective-permute-start | bytes 3080 | tf_op jit(solution)/shard_map/ppermute | solution.py:30
  15.8 4.6 %copy-start.3 = (f32[2048]{0:T(1024)S(1)}, f32[2048]{0:T(1024)}, u32[]{:S(2)}) copy-start(f32[2048]{0:T(1024)} %param.10) | copy-start | bytes 24580
  16.8 8.5 %collective-permute-start.4 = (f32[1,256]{1,0:T(1,128)S(1)}, f32[1,256]{1,0:T(1,128)S(1)}, u32[]{:S(2)}, u32[]{:S(2)}) collective-permute-start(f32[1,256]{1,0:T(1,128)S(1)} %add_add_fusion.total_ref.after_ref), channel_id=1, source_target_pairs={{0,4},{4,8},{8,12},{12,16},{16,20},{20,24},{24,28},{28,32},{32,36}... | collective-permute-start | bytes 3080 | tf_op jit(solution)/shard_map/ppermute | solution.py:25
  25.2 8.5 %copy-start.4 = (bf16[128,128]{1,0:T(8,128)(2,1)S(1)}, bf16[128,128]{1,0:T(8,128)(2,1)}, u32[]{:S(2)}) copy-start(bf16[128,128]{1,0:T(8,128)(2,1)} %fmr_ref.1) | copy-start | bytes 98308
  28.1 10.2 %copy-start.2 = (f32[3,3,2048]{2,1,0:T(4,128)S(1)}, f32[3,3,2048]{2,1,0:T(4,128)}, u32[]{:S(2)}) copy-start(f32[3,3,2048]{2,1,0:T(4,128)} %feat_ref.5) | copy-start | bytes 221188
  28.1 7.6 %collective-permute-start.7 = (f32[1,512]{1,0:T(1,128)S(1)}, f32[1,512]{1,0:T(1,128)S(1)}, u32[]{:S(2)}, u32[]{:S(2)}) collective-permute-start(f32[1,512]{1,0:T(1,128)S(1)} %get-tuple-element.16.sums0_ref), channel_id=1, source_target_pairs={{0,2},{1,3},{2,0},{3,1},{4,6},{5,7},{6,4},{7,5},{8,10},{9,11},{10,... | collective-permute-start | bytes 6152 | tf_op jit(solution)/shard_map/ppermute | solution.py:30
  29.6 6.0 %collective-permute-start.6 = (f32[1,512]{1,0:T(1,128)S(1)}, f32[1,512]{1,0:T(1,128)S(1)}, u32[]{:S(2)}, u32[]{:S(2)}) collective-permute-start(f32[1,512]{1,0:T(1,128)S(1)} %get-tuple-element.16.sums0_ref), channel_id=1, source_target_pairs={{0,1},{1,2},{2,3},{3,0},{4,5},{5,6},{6,7},{7,4},{8,9},{9,10},{10,1... | collective-permute-start | bytes 6152 | tf_op jit(solution)/shard_map/ppermute | solution.py:30
  33.8 4.5 %collective-permute-start.5 = (f32[1,512]{1,0:T(1,128)S(1)}, f32[1,512]{1,0:T(1,128)S(1)}, u32[]{:S(2)}, u32[]{:S(2)}) collective-permute-start(f32[1,512]{1,0:T(1,128)S(1)} %get-tuple-element.16.sums0_ref), channel_id=1, source_target_pairs={{0,3},{1,0},{2,1},{3,2},{4,7},{5,4},{6,5},{7,6},{8,11},{9,8},{10,9... | collective-permute-start | bytes 6152 | tf_op jit(solution)/shard_map/ppermute | solution.py:30
  33.8 4.5 %copy-start.5 = (f32[2048]{0:T(1024)S(1)}, f32[2048]{0:T(1024)}, u32[]{:S(2)}) copy-start(f32[2048]{0:T(1024)} %param.11) | copy-start | bytes 24580

commit v5 on v4

--- a/solution.py
+++ b/solution.py
@@ -30,27 +30,26 @@
     return lax.ppermute(x, axis, [(i, (i + by) % peers) for i in range(peers)])
 
 
-def as_row(column):
-    rows = column.shape[0]
-    return jnp.broadcast_to(column, (rows, LANES)).T[0:1]
+def lane_sums(held):
+    return jnp.sum(held.T, axis=0, keepdims=True)
 
 
 def as_column(row):
-    return jnp.broadcast_to(row, (LANES, row.shape[1])).T
+    rows = row.shape[1]
+    return jnp.broadcast_to(jnp.broadcast_to(row, (8, rows)).T[:, 0:1], (rows, LANES))
 
 
 def sums_kernel(x_ref, s_ref):
     rows, width = x_ref.shape
-    for r in range(0, rows, 64):
-        total = jnp.zeros((64, LANES), jnp.float32)
-        for c in range(0, width, LANES):
-            x = x_ref[r : r + 64, c : c + LANES].astype(jnp.float32)
-            total = total + x * x
-        col = jnp.sum(total, axis=1, keepdims=True)
-        if r % 128 == 0:
-            held = col
-        else:
-            s_ref[0:1, r - 64 : r + 64] = as_row(jnp.concatenate([held, col], axis=0))
+    for r in range(0, rows, LANES):
+        total = []
+        for h in range(r, r + LANES, 32):
+            part = jnp.zeros((32, LANES), jnp.float32)
+            for c in range(0, width, LANES):
+                x = x_ref[h : h + 32, c : c + LANES].astype(jnp.float32)
+                part = part + x * x
+            total.append(part)
+        s_ref[0:1, r : r + LANES] = lane_sums(jnp.concatenate(total, axis=0))
 
 
 def place_kernel(first_ref, len_ref, fse_ref, off_ref, fexp_ref):
@@ -69,7 +68,8 @@
     for r in range(0, ext, CHUNK):
         pos = (lax.broadcasted_iota(jnp.int32, (CHUNK, LANES), 0) + (first + r)).astype(jnp.float32)
         doc_first = jnp.max(jnp.where(starts <= pos, starts, 0.0), axis=1, keepdims=True)
-        off_ref[r : r + CHUNK, :] = pos - doc_first
+        off = jnp.broadcast_to(pos - doc_first, (CHUNK, LANES))
+        off_ref[r : r + CHUNK, :] = off
     fse = fse_ref[...]
     for c in range(0, width, LANES):
         row = lax.broadcasted_iota(jnp.int32, (groups, LANES), 0)
@@ -81,16 +81,26 @@
         )
 
 
-def turn_kernel(after_ref, fmr_ref, base_ref, rev_ref):
+def turn_kernel(after_ref, fmr_ref, off_ref, base_ref, keep_ref, rev_ref):
     groups = fmr_ref.shape[0]
     rev_ref[...] = fmr_ref[...].astype(jnp.float32)
 
     def one(g, carry):
         h = jnp.broadcast_to(rev_ref[pl.ds(g, 1), :], (GROUP, LANES))
-        base_ref[g] = pltpu.roll(h, 0, 1, stride=1, stride_axis=0)
+        base_ref[g] = pltpu.roll(h, 0, 1, stride=1, stride_axis=0).astype(jnp.bfloat16)
         return carry
 
     lax.fori_loop(0, groups, one, 0, unroll=8)
+    row = lax.broadcasted_iota(jnp.int32, (LANES, LANES), 0)
+    col = lax.broadcasted_iota(jnp.int32, (LANES, LANES), 1)
+    lag = (col - row).astype(jnp.float32)
+    for b in range(keep_ref.shape[1] // LANES):
+        off = off_ref[HALO + b * LANES : HALO + (b + 1) * LANES, :].T
+        before = (row > col) & (lag + MEDIUM_TAPS <= off)
+        within = (row <= col) & (lag <= off)
+        at = slice(b * LANES, (b + 1) * LANES)
+        keep_ref[0:LANES, at] = before.astype(jnp.float32).astype(jnp.bfloat16)
+        keep_ref[LANES:, at] = within.astype(jnp.float32).astype(jnp.bfloat16)
 
 
 def scale_of(total):
@@ -115,8 +125,8 @@
 
 
 def se_rows(
-    raw, rows, skip, width, gain_ref, feat_ref, fexp_ref, mid_ref,
-    scale_ref, mask_ref, norm_ref, prod_ref, q_ref, acc_ref,
+    raw, rows, skip, width, mask_ref, gain_ref, feat_ref, fexp_ref, mid_ref,
+    scale_ref, norm_ref, prod_ref, q_ref, acc_ref,
 ):
     norm_ref[0:PAD, :] = jnp.zeros((PAD, LANES), jnp.float32)
     prod_ref[0:PAD, :] = jnp.zeros((PAD, LANES), jnp.float32)
@@ -126,9 +136,8 @@
         cols = pl.ds(pl.multiple_of(i * LANES, LANES), LANES)
         gain = gain_ref[0:1, cols]
         for e in range(0, rows, CHUNK):
-            n = raw(e, cols) * scale_ref[e : e + CHUNK, :] * gain
-            norm_ref[PAD + e : PAD + e + CHUNK, :] = n.astype(jnp.bfloat16).astype(jnp.float32)
-        taps = [[feat_ref[s, j : j + 1, cols] for j in range(FEAT_TAPS)] for s in range(3)]
+            norm_ref[PAD + e : PAD + e + CHUNK, :] = raw(e, cols) * scale_ref[e : e + CHUNK, :]
+        taps = [[feat_ref[s, j : j + 1, cols] * gain for j in range(FEAT_TAPS)] for s in range(3)]
         for e in range(0, rows, CHUNK):
             xs = [norm_ref[PAD + e : PAD + e + CHUNK, :]]
             for j in range(1, FEAT_TAPS):
@@ -145,13 +154,12 @@
                 total = total + filt[j] * (
                     prod_ref[PAD + e - j : PAD + e - j + CHUNK, :] * mask_ref[j - 1, e : e + CHUNK, :]
                 )
-            mid = (raw(e, cols) + q_ref[e : e + CHUNK, :] * total).astype(jnp.bfloat16)
-            mid_ref[e : e + CHUNK, cols] = mid
-            mid = mid.astype(jnp.float32)
+            mid = raw(e, cols) + q_ref[e : e + CHUNK, :] * total
+            mid_ref[e : e + CHUNK, cols] = mid.astype(jnp.bfloat16)
             acc_ref[e : e + CHUNK, :] = acc_ref[e : e + CHUNK, :] + mid * mid
         return carry
 
-    lax.fori_loop(0, width // LANES, tile, 0)
+    lax.fori_loop(0, width // LANES, tile, 0, unroll=2)
 
 
 def se_own_kernel(
@@ -164,10 +172,10 @@
     mid_ref[0:CHUNK, :] = jnp.zeros((CHUNK, width), jnp.bfloat16)
     se_rows(
         lambda e, cols: x_ref[e : e + CHUNK, cols].astype(jnp.float32),
-        own, CHUNK, width, gain_ref, feat_ref, fexp_ref, mid_ref, scale_ref, mask_ref, *scratch,
+        own, CHUNK, width, mask_ref, gain_ref, feat_ref, fexp_ref, mid_ref, scale_ref, *scratch,
     )
     for r in range(0, own, LANES):
-        s_ref[0:1, r : r + LANES] = as_row(jnp.sum(acc_ref[r : r + LANES, :], axis=1, keepdims=True))
+        s_ref[0:1, r : r + LANES] = lane_sums(acc_ref[r : r + LANES, :])
 
 
 def se_halo_kernel(
@@ -176,8 +184,9 @@
 ):
     own, width = x_ref.shape
     acc_ref = scratch[-1]
+    edge = LANES - CHUNK
     scale_ref[0:HALO, :] = as_column(scale_of(before_ref[...]))[own - HALO :, :]
-    scale_ref[HALO:, :] = as_column(scale_of(total_ref[...]))[0:CHUNK, :]
+    scale_ref[HALO:, :] = as_column(scale_of(total_ref[:, 0:LANES]))[0:CHUNK, :]
     masks_of(off_ref, mask_ref, SHORT_TAPS)
 
     def raw(e, cols):
@@ -186,19 +195,20 @@
         return x_ref[e - HALO : e - HALO + CHUNK, cols].astype(jnp.float32)
 
     se_rows(
-        raw, HALO + CHUNK, 0, width, gain_ref, feat_ref, fexp_ref, mid_ref, scale_ref, mask_ref, *scratch
+        raw, HALO + CHUNK, 0, width, mask_ref, gain_ref, feat_ref, fexp_ref, mid_ref, scale_ref, *scratch
     )
-    halo_part = jnp.sum(acc_ref[0:HALO, :], axis=1, keepdims=True)
-    halo_part = jnp.concatenate([jnp.zeros((own - HALO, 1), jnp.float32), halo_part], axis=0)
-    own_part = jnp.sum(acc_ref[HALO:, :], axis=1, keepdims=True)
-    own_part = jnp.concatenate([own_part, jnp.zeros((own - CHUNK, 1), jnp.float32)], axis=0)
-    s_ref[0:1, 0:own] = as_row(halo_part)
-    s_ref[0:1, own:] = as_row(own_part) + part_ref[...]
+    pad = jnp.zeros((edge, LANES), jnp.float32)
+    s_ref[0:1, 0:LANES] = lane_sums(jnp.concatenate([pad, acc_ref[0:CHUNK, :]], axis=0))
+    s_ref[0:1, LANES:own] = lane_sums(acc_ref[CHUNK:HALO, :])
+    s_ref[0:1, own : own + LANES] = part_ref[:, 0:LANES] + lane_sums(
+        jnp.concatenate([acc_ref[HALO:, :], pad], axis=0)
+    )
+    s_ref[0:1, own + LANES :] = part_ref[:, LANES:]
 
 
 def mr_kernel(
-    early_ref, mid_ref, sums0_ref, sums1_ref, sums2_ref, sums3_ref, off_ref, gain_ref, feat_ref, base_ref, out_ref,
-    scale_ref, mask_ref, norm_ref, keep_ref, *slots,
+    early_ref, mid_ref, sums0_ref, sums1_ref, sums2_ref, sums3_ref, off_ref, gain_ref, feat_ref,
+    base_ref, keep_ref, result_ref, out_ref, sems, scale_ref, mask_ref, norm_ref, *slots,
 ):
     own, width = mid_ref.shape
     ext = HALO + own
@@ -207,16 +217,6 @@
     scale_columns((sums0_ref, sums1_ref, sums2_ref, sums3_ref), scale_ref)
     masks_of(off_ref, mask_ref, FEAT_TAPS)
     norm_ref[0:PAD, :] = jnp.zeros((PAD, LANES), jnp.float32)
-    row = lax.broadcasted_iota(jnp.int32, (LANES, LANES), 0)
-    col = lax.broadcasted_iota(jnp.int32, (LANES, LANES), 1)
-    for b in range(blocks):
-        off = off_ref[HALO + b * LANES : HALO + (b + 1) * LANES, :].T
-        lag = (col - row).astype(jnp.float32)
-        before = (row > col) & (lag + MEDIUM_TAPS <= off)
-        within = (row <= col) & (lag <= off)
-        at = slice(b * LANES, (b + 1) * LANES)
-        keep_ref[0:LANES, at] = before.astype(jnp.float32).astype(jnp.bfloat16)
-        keep_ref[LANES:, at] = within.astype(jnp.float32).astype(jnp.bfloat16)
     early = early_ref.shape[0]
 
     def middle(e, cols):
@@ -229,9 +229,8 @@
         cols = pl.ds(pl.multiple_of(i * LANES, LANES), LANES)
         gain = gain_ref[0:1, cols]
         for e in range(0, ext, CHUNK):
-            n = middle(e, cols) * scale_ref[e : e + CHUNK, :] * gain
-            norm_ref[PAD + e : PAD + e + CHUNK, :] = n.astype(jnp.bfloat16).astype(jnp.float32)
-        taps = [[feat_ref[s, j : j + 1, cols] for j in range(FEAT_TAPS)] for s in range(3)]
+            norm_ref[PAD + e : PAD + e + CHUNK, :] = middle(e, cols) * scale_ref[e : e + CHUNK, :]
+        taps = [[feat_ref[s, j : j + 1, cols] * gain for j in range(FEAT_TAPS)] for s in range(3)]
         prods = []
         for e in range(HALO - LANES, ext, CHUNK):
             xs = [norm_ref[PAD + e : PAD + e + CHUNK, :]]
@@ -252,7 +251,7 @@
         cols = pl.ds(pl.multiple_of(i * LANES, LANES), LANES)
         parts = [[] for _ in range(blocks)]
         for g in range(per_tile):
-            base = base_ref[i * per_tile + g].astype(jnp.bfloat16)
+            base = base_ref[i * per_tile + g]
             circ = jnp.concatenate([pltpu.roll(base, r, 1) if r else base for r in range(0, LANES, GROUP)], axis=0)
             rows = slice(g * GROUP, (g + 1) * GROUP)
             toep = jnp.concatenate([jnp.concatenate([circ] * blocks, axis=1)] * 2, axis=0) * keep_ref[...]
@@ -273,17 +272,24 @@
     slots = (slots[:2], slots[2:])
     ready(0, slots[0])
 
+    def leave(j):
+        cols = pl.ds(pl.multiple_of(j * 2 * LANES, 2 * LANES), 2 * LANES)
+        return pltpu.make_async_copy(out_ref.at[:, cols], result_ref.at[:, cols], sems.at[j])
+
     def pair(j, carry):
         for at in range(2):
             i = 2 * j + at
             ready(jnp.minimum(i + 1, tiles - 1), slots[1 - at])
             finish(i, slots[at])
+        leave(j).start()
         return carry
 
-    lax.fori_loop(0, tiles // 2, pair, 0)
-
-
-def call(kernel, out_shape, scratch, flops, nbytes, smem=0):
+    lax.fori_loop(0, tiles // 2, pair, 0, unroll=4)
+    for j in range(tiles // 2):
+        leave(j).wait()
+
+
+def call(kernel, out_shape, scratch, flops, nbytes, smem=0, space=pltpu.VMEM):
     count = smem
     params = pltpu.CompilerParams(vmem_limit_bytes=VMEM_LIMIT)
     cost = pl.CostEstimate(flops=flops, bytes_accessed=nbytes, transcendentals=0)
@@ -293,7 +299,7 @@
         specs += [pl.BlockSpec(memory_space=pltpu.VMEM)] * (len(operands) - count)
         return pl.pallas_call(
             kernel, out_shape=out_shape, in_specs=specs,
-            out_specs=jax.tree.map(lambda _: pl.BlockSpec(memory_space=pltpu.VMEM), out_shape),
+            out_specs=jax.tree.map(lambda _: pl.BlockSpec(memory_space=space), out_shape),
             scratch_shapes=scratch, compiler_params=params, cost_estimate=cost,
         )(*operands)
 
@@ -333,14 +339,15 @@
         pltpu.VMEM((own, LANES), jnp.float32),
     ]
     scratch = [
+        pltpu.VMEM((own, width), jnp.bfloat16),
+        pltpu.SemaphoreType.DMA((width // (2 * LANES),)),
         pltpu.VMEM((ext, LANES), jnp.float32),
         pltpu.VMEM((FEAT_TAPS - 1, ext, LANES), jnp.float32),
         pltpu.VMEM((PAD + ext, LANES), jnp.float32),
-        pltpu.VMEM((2 * LANES, blocks * LANES), jnp.bfloat16),
         *slot,
         *slot,
     ]
-    return call(mr_kernel, jax.ShapeDtypeStruct((own, width), jnp.bfloat16), scratch, 1 << 30, 4 << 20)(early, mid, *rest)
+    return call(mr_kernel, jax.ShapeDtypeStruct((own, width), jnp.bfloat16), scratch, 1 << 30, 4 << 20, space=pl.ANY)(early, mid, *rest)
 
 
 def shards(hidden, doc_lengths, gain_se, gain_mr, feat_se, feat_mr, filter_se, filter_mr):
@@ -354,17 +361,22 @@
     part = call(sums_kernel, shape((1, own), f32), [], 1 << 20, 1 << 20)(x)
     total = part + turned(part, "tp", 3) + turned(part, "tp", 1) + turned(part, "tp", 2)
     before = shifted(total, "ctx", 1)
+    ext = HALO + own
     off, fexp = call(
-        place_kernel, (shape((HALO + own, LANES), f32), shape((8, width), f32)), [], 1 << 24, 1 << 20, smem=1
+        place_kernel,
+        (shape((ext, LANES), f32), shape((8, width), f32)),
+        [], 1 << 24, 1 << 20, smem=1,
     )(first, doc_lengths, filter_se)
-    base = call(
-        turn_kernel, shape((groups, GROUP, LANES), f32), [pltpu.VMEM((groups, LANES), f32)], 1 << 24, 1 << 20
-    )(total, filter_mr)
+    base, keep = call(
+        turn_kernel,
+        (shape((groups, GROUP, LANES), jnp.bfloat16), shape((2 * LANES, own), jnp.bfloat16)),
+        [pltpu.VMEM((groups, LANES), f32)], 1 << 24, 1 << 20,
+    )(total, filter_mr, off)
     gain = gain_se.reshape(1, width)
     mid, part_two = se_own_call(x, total, off, gain, feat_se, fexp)
     early, part_two = se_halo_call(x, halo, total, before, part_two, off, gain, feat_se, fexp)
     sums_two = [part_two] + [turned(part_two, "tp", by) for by in (3, 1, 2)]
-    return mr_call(early, mid, *sums_two, off, gain_mr.reshape(1, width), feat_mr, base)[None]
+    return mr_call(early, mid, *sums_two, off, gain_mr.reshape(1, width), feat_mr, base, keep)[None]
 
 
 def solution(mesh):

time: 45.5 us -> 44.2 us (0.971)
  Pallas kernels: 16.2 us -> 14.7 us
    pallas_call x6, Pallas kernels: 16.2 us -> 14.7 us  [run(): pl.pallas_call(kernel, out_shape=out_shape, in_specs=specs, out_specs=jax...]
where the time goes in v5:
time: 44.2 us; the launch traced here: 44 us
  starting transfers between devices  22.7 us (51%)
  Pallas kernels  14.7 us (33%)
  waiting for transfers between devices  5.11 us (12%)
  local copies, waits for them, and re-layouts  1.35 us (3%)
    ppermute x6, starting transfers between devices, turned(): return lax.ppermute(x, axis, [(i, (i + by) % peers) for i in range(peers)])  17.1 us
    pallas_call x6, Pallas kernels, run(): pl.pallas_call(kernel, out_shape=out_shape, in_specs=specs, out_specs=jax...  14.7 us
    ppermute x2, starting transfers between devices, shifted(): return lax.ppermute(x, axis, pairs)  5.64 us
    ppermute x6, waiting for transfers between devices, turned(): return lax.ppermute(x, axis, [(i, (i + by) % peers) for i in range(peers)])  4.08 us
    slice x1, local copies, waits for them, and re-layouts, shards(): halo = shifted(x[own - HALO:], 'ctx', 1)  1.19 us
    ppermute x2, waiting for transfers between devices, shifted(): return lax.ppermute(x, axis, pairs)  1.03 us
  transfers between devices with their start and end apart: 8, of which 5 were waited for; matrix products, arithmetic and copies ran while one was open for 0% of the time, Pallas kernels for 14%

profile of v5, /device:TPU:2, one launch (start us, length us, event | category | flops | bytes accessed | tf_op | source)
XLA Modules:
  0.0 44.0 jit_solution(8422576772908393209)
XLA Ops:
  0.0 0.0 copy-start
  0.0 1.2 %slice_bitcast_fusion = bf16[144,2048]{1,0:T(8,128)(2,1)S(1)} fusion(bf16[1,256,2048]{2,1,0:T(8,128)(2,1)} %param.8), kind=kLoop, calls=%fused_computation | loop fusion | bytes 1179648 | tf_op jit(solution)/shard_map/slice | solution.py:360
  1.2 1.9 %collective-permute-start = (bf16[144,2048]{1,0:T(8,128)(2,1)S(1)}, bf16[144,2048]{1,0:T(8,128)(2,1)S(1)}, u32[]{:S(2)}, u32[]{:S(2)}) collective-permute-start(bf16[144,2048]{1,0:T(8,128)(2,1)S(1)} %slice_bitcast_fusion), channel_id=1, source_target_pairs={{0,4},{4,8},{8,12},{12,16},{16,20},{20,24},{24,28},{28,32},{32,36}... | collective-permute-start | bytes 1769480 | tf_op jit(solution)/shard_map/ppermute | solution.py:25
  3.1 0.0 copy-done
  3.1 0.0 copy-start.7
  3.1 0.0 copy-start.4
  3.2 0.3 shard_map.82
  3.4 0.0 copy-start.1
  3.5 7.3 %collective-permute-start.3 = (f32[1,256]{1,0:T(1,128)S(1)}, f32[1,256]{1,0:T(1,128)S(1)}, u32[]{:S(2)}, u32[]{:S(2)}) collective-permute-start(f32[1,256]{1,0:T(1,128)S(1)} %shard_map.82), channel_id=1, source_target_pairs={{0,2},{1,3},{2,0},{3,1},{4,6},{5,7},{6,4},{7,5},{8,10},{9,11},{10,... | collective-permute-start | bytes 3080 | tf_op jit(solution)/shard_map/ppermute | solution.py:30
  10.7 1.5 %collective-permute-start.2 = (f32[1,256]{1,0:T(1,128)S(1)}, f32[1,256]{1,0:T(1,128)S(1)}, u32[]{:S(2)}, u32[]{:S(2)}) collective-permute-start(f32[1,256]{1,0:T(1,128)S(1)} %shard_map.82), channel_id=1, source_target_pairs={{0,1},{1,2},{2,3},{3,0},{4,5},{5,6},{6,7},{7,4},{8,9},{9,10},{10,1... | collective-permute-start | bytes 3080 | tf_op jit(solution)/shard_map/ppermute | solution.py:30
  12.2 2.7 %collective-permute-start.1 = (f32[1,256]{1,0:T(1,128)S(1)}, f32[1,256]{1,0:T(1,128)S(1)}, u32[]{:S(2)}, u32[]{:S(2)}) collective-permute-start(f32[1,256]{1,0:T(1,128)S(1)} %shard_map.82), channel_id=1, source_target_pairs={{0,3},{1,0},{2,1},{3,2},{4,7},{5,4},{6,5},{7,6},{8,11},{9,8},{10,9... | collective-permute-start | bytes 3080 | tf_op jit(solution)/shard_map/ppermute | solution.py:30
  14.9 0.0 copy-done.7
  14.9 0.1 copy.9.fse_ref
  15.0 0.0 copy-done.4
  15.0 0.7 %shard_map.83 = (f32[400,128]{1,0:T(8,128)S(1)}, f32[8,2048]{1,0:T(8,128)S(1)}) custom-call(s32[1]{0:T(128)} %bitcast.2.first_ref, s32[1,128]{1,0:T(1,128)S(1)} %copy-done.4, f32[128,7]{1,0:T(8,128)S(1)} %copy.9.fse_ref), custom_call_target="tpu_custom_call" | custom-call | flops 16777216 | bytes 1048576 | tf_op jit(solution)/shard_map/pallas_call | solution.py:300
  15.7 0.0 copy-start.2
  15.7 0.0 collective-permute-done.3
  15.7 0.8 %collective-permute-done.2 = f32[1,256]{1,0:T(1,128)S(1)} collective-permute-done((f32[1,256]{1,0:T(1,128)S(1)}, f32[1,256]{1,0:T(1,128)S(1)}, u32[]{:S(2)}, u32[]{:S(2)}) %collective-permute-start.2) | collective-permute-done | bytes 1056 | tf_op jit(solution)/shard_map/ppermute | solution.py:30
  16.5 0.2 collective-permute-done.1
  16.7 3.7 %collective-permute-start.4 = (f32[1,256]{1,0:T(1,128)S(1)}, f32[1,256]{1,0:T(1,128)S(1)}, u32[]{:S(2)}, u32[]{:S(2)}) collective-permute-start(f32[1,256]{1,0:T(1,128)S(1)} %add_add_fusion.total_ref.after_ref), channel_id=1, source_target_pairs={{0,4},{4,8},{8,12},{12,16},{16,20},{20,24},{24,28},{28,32},{32,36}... | collective-permute-start | bytes 3080 | tf_op jit(solution)/shard_map/ppermute | solution.py:25
  20.4 0.0 copy-done.1
  20.4 0.0 copy-done.2
  20.4 3.8 %shard_map.84 = (bf16[256,2048]{1,0:T(8,128)(2,1)S(1)}, f32[1,256]{1,0:T(1,128)S(1)}) custom-call(bf16[256,2048]{1,0:T(8,128)(2,1)S(1)} %bitcast.8, f32[1,256]{1,0:T(1,128)S(1)} %add_add_fusion.total_ref.after_ref, f32[400,128]{1,0:T(8,128)S(1)} %get-tuple-element.13.off_ref, f32[1,2048]{1,0:T(1,128)S(1)} %bitcast.10, f32[3,3,2048]{2,1,0:T(4,128)S(1)} %copy-done.1, ...), custom_call_target="tpu_custom_call" | custom-call | flops 26214400 | bytes 2097152 | tf_op jit(solution)/shard_map/pallas_call | solution.py:300
  24.2 1.0 %collective-permute-done.4.before_ref = f32[1,256]{1,0:T(1,128)S(1)} collective-permute-done((f32[1,256]{1,0:T(1,128)S(1)}, f32[1,256]{1,0:T(1,128)S(1)}, u32[]{:S(2)}, u32[]{:S(2)}) %collective-permute-start.4) | collective-permute-done | bytes 1056 | tf_op jit(solution)/shard_map/ppermute | solution.py:25
  25.2 0.0 collective-permute-done.halo_ref
  25.2 0.0 copy-start.3
  25.2 2.7 %shard_map.85 = (bf16[160,2048]{1,0:T(8,128)(2,1)S(1)}, f32[1,512]{1,0:T(1,128)S(1)}) custom-call(bf16[256,2048]{1,0:T(8,128)(2,1)S(1)} %bitcast.9, bf16[144,2048]{1,0:T(8,128)(2,1)S(1)} %collective-permute-done.halo_ref, f32[1,256]{1,0:T(1,128)S(1)} %add_add_fusion.total_ref.after_ref, f32[1,256]{1,0:T(1,128)S(1)} %collective-permute-done.4.before_ref, ...), custom_call_target="tpu_custom_call" | custom-call | flops 26214400 | bytes 2097152 | tf_op jit(solution)/shard_map/pallas_call | solution.py:300
  27.9 0.0 copy-start.5
  27.9 1.6 %collective-permute-start.7 = (f32[1,512]{1,0:T(1,128)S(1)}, f32[1,512]{1,0:T(1,128)S(1)}, u32[]{:S(2)}, u32[]{:S(2)}) collective-permute-start(f32[1,512]{1,0:T(1,128)S(1)} %get-tuple-element.18.sums0_ref), channel_id=1, source_target_pairs={{0,2},{1,3},{2,0},{3,1},{4,6},{5,7},{6,4},{7,5},{8,10},{9,11},{10,... | collective-permute-start | bytes 6152 | tf_op jit(solution)/shard_map/ppermute | solution.py:30
  29.5 4.1 %collective-permute-start.6 = (f32[1,512]{1,0:T(1,128)S(1)}, f32[1,512]{1,0:T(1,128)S(1)}, u32[]{:S(2)}, u32[]{:S(2)}) collective-permute-start(f32[1,512]{1,0:T(1,128)S(1)} %get-tuple-element.18.sums0_ref), channel_id=1, source_target_pairs={{0,1},{1,2},{2,3},{3,0},{4,5},{5,6},{6,7},{7,4},{8,9},{9,10},{10,1... | collective-permute-start | bytes 6152 | tf_op jit(solution)/shard_map/ppermute | solution.py:30
  33.6 0.0 collective-permute-start.5
  33.6 0.0 copy-done.3
  33.6 1.3 %shard_map.86 = (bf16[128,16,128]{2,1,0:T(8,128)(2,1)S(1)}, bf16[256,256]{1,0:T(8,128)(2,1)S(1)}) custom-call(f32[1,256]{1,0:T(1,128)S(1)} %add_add_fusion.total_ref.after_ref, bf16[128,128]{1,0:T(8,128)(2,1)S(1)} %copy-done.3, f32[400,128]{1,0:T(8,128)S(1)} %get-tuple-element.13.off_ref), custom_call_target="tpu_custom_call" | custom-call | flops 16777216 | bytes 1048576 | tf_op jit(solution)/shard_map/pallas_call | solution.py:300
  34.9 0.0 copy-start.6
  34.9 0.6 %collective-permute-done.7.sums3_ref = f32[1,512]{1,0:T(1,128)S(1)} collective-permute-done((f32[1,512]{1,0:T(1,128)S(1)}, f32[1,512]{1,0:T(1,128)S(1)}, u32[]{:S(2)}, u32[]{:S(2)}) %collective-permute-start.7) | collective-permute-done | bytes 2080 | tf_op jit(solution)/shard_map/ppermute | solution.py:30
  35.5 0.0 collective-permute-done.6.sums2_ref
  35.5 2.5 %collective-permute-done.5.sums1_ref = f32[1,512]{1,0:T(1,128)S(1)} collective-permute-done((f32[1,512]{1,0:T(1,128)S(1)}, f32[1,512]{1,0:T(1,128)S(1)}, u32[]{:S(2)}, u32[]{:S(2)}) %collective-permute-start.5) | collective-permute-done | bytes 2080 | tf_op jit(solution)/shard_map/ppermute | solution.py:30
  38.1 0.0 copy-done.5
  38.1 0.0 copy-done.6
  38.1 5.9 %shard_map.87 = bf16[256,2048]{1,0:T(8,128)(2,1)} custom-call(bf16[160,2048]{1,0:T(8,128)(2,1)S(1)} %get-tuple-element.16.early_ref, bf16[256,2048]{1,0:T(8,128)(2,1)S(1)} %get-tuple-element.17.mid_ref, f32[1,512]{1,0:T(1,128)S(1)} %get-tuple-element.18.sums0_ref, f32[1,512]{1,0:T(1,128)S(1)} %collective-permute-done.5.sums1_ref, ...), custom_call_target="tpu_custom_call" | custom-call | flops 1073741824 | bytes 4194304 | tf_op jit(solution)/shard_map/pallas_call | solution.py:300
  (1 shorter events, 0.0 us)
Async XLA Ops:
  0.0 3.1 %copy-start = (bf16[1,256,2048]{2,1,0:T(8,128)(2,1)S(1)}, bf16[1,256,2048]{2,1,0:T(8,128)(2,1)}, u32[]{:S(2)}) copy-start(bf16[1,256,2048]{2,1,0:T(8,128)(2,1)} %param.8) | copy-start | bytes 3145732
  1.2 24.0 %collective-permute-start = (bf16[144,2048]{1,0:T(8,128)(2,1)S(1)}, bf16[144,2048]{1,0:T(8,128)(2,1)S(1)}, u32[]{:S(2)}, u32[]{:S(2)}) collective-permute-start(bf16[144,2048]{1,0:T(8,128)(2,1)S(1)} %slice_bitcast_fusion), channel_id=1, source_target_pairs={{0,4},{4,8},{8,12},{12,16},{16,20},{20,24},{24,28},{28,32},{32,36}... | collective-permute-start | bytes 1769480 | tf_op jit(solution)/shard_map/ppermute | solution.py:25
  3.1 11.7 %copy-start.7 = (f32[128,7]{0,1:T(8,128)S(1)}, f32[128,7]{0,1:T(8,128)}, u32[]{:S(2)}) copy-start(f32[128,7]{0,1:T(8,128)} %param.14) | copy-start | bytes 10756
  3.1 11.8 %copy-start.4 = (s32[1,128]{1,0:T(1,128)S(1)}, s32[1,128]{1,0:T(1,128)}, u32[]{:S(2)}) copy-start(s32[1,128]{1,0:T(1,128)} %len_ref.1) | copy-start | bytes 1540
  3.4 17.0 %copy-start.1 = (f32[3,3,2048]{2,1,0:T(4,128)S(1)}, f32[3,3,2048]{2,1,0:T(4,128)}, u32[]{:S(2)}) copy-start(f32[3,3,2048]{2,1,0:T(4,128)} %feat_ref.4) | copy-start | bytes 221188
  3.5 12.2 %collective-permute-start.3 = (f32[1,256]{1,0:T(1,128)S(1)}, f32[1,256]{1,0:T(1,128)S(1)}, u32[]{:S(2)}, u32[]{:S(2)}) collective-permute-start(f32[1,256]{1,0:T(1,128)S(1)} %shard_map.82), channel_id=1, source_target_pairs={{0,2},{1,3},{2,0},{3,1},{4,6},{5,7},{6,4},{7,5},{8,10},{9,11},{10,... | collective-permute-start | bytes 3080 | tf_op jit(solution)/shard_map/ppermute | solution.py:30
  10.7 5.8 %collective-permute-start.2 = (f32[1,256]{1,0:T(1,128)S(1)}, f32[1,256]{1,0:T(1,128)S(1)}, u32[]{:S(2)}, u32[]{:S(2)}) collective-permute-start(f32[1,256]{1,0:T(1,128)S(1)} %shard_map.82), channel_id=1, source_target_pairs={{0,1},{1,2},{2,3},{3,0},{4,5},{5,6},{6,7},{7,4},{8,9},{9,10},{10,1... | collective-permute-start | bytes 3080 | tf_op jit(solution)/shard_map/ppermute | solution.py:30
  12.2 4.5 %collective-permute-start.1 = (f32[1,256]{1,0:T(1,128)S(1)}, f32[1,256]{1,0:T(1,128)S(1)}, u32[]{:S(2)}, u32[]{:S(2)}) collective-permute-start(f32[1,256]{1,0:T(1,128)S(1)} %shard_map.82), channel_id=1, source_target_pairs={{0,3},{1,0},{2,1},{3,2},{4,7},{5,4},{6,5},{7,6},{8,11},{9,8},{10,9... | collective-permute-start | bytes 3080 | tf_op jit(solution)/shard_map/ppermute | solution.py:30
  15.7 4.7 %copy-start.2 = (f32[2048]{0:T(1024)S(1)}, f32[2048]{0:T(1024)}, u32[]{:S(2)}) copy-start(f32[2048]{0:T(1024)} %param.10) | copy-start | bytes 24580
  16.7 8.6 %collective-permute-start.4 = (f32[1,256]{1,0:T(1,128)S(1)}, f32[1,256]{1,0:T(1,128)S(1)}, u32[]{:S(2)}, u32[]{:S(2)}) collective-permute-start(f32[1,256]{1,0:T(1,128)S(1)} %add_add_fusion.total_ref.after_ref), channel_id=1, source_target_pairs={{0,4},{4,8},{8,12},{12,16},{16,20},{20,24},{24,28},{28,32},{32,36}... | collective-permute-start | bytes 3080 | tf_op jit(solution)/shard_map/ppermute | solution.py:25
  25.2 8.4 %copy-start.3 = (bf16[128,128]{1,0:T(8,128)(2,1)S(1)}, bf16[128,128]{1,0:T(8,128)(2,1)}, u32[]{:S(2)}) copy-start(bf16[128,128]{1,0:T(8,128)(2,1)} %fmr_ref.1) | copy-start | bytes 98308
  27.9 10.1 %copy-start.5 = (f32[3,3,2048]{2,1,0:T(4,128)S(1)}, f32[3,3,2048]{2,1,0:T(4,128)}, u32[]{:S(2)}) copy-start(f32[3,3,2048]{2,1,0:T(4,128)} %feat_ref.5) | copy-start | bytes 221188
  27.9 7.6 %collective-permute-start.7 = (f32[1,512]{1,0:T(1,128)S(1)}, f32[1,512]{1,0:T(1,128)S(1)}, u32[]{:S(2)}, u32[]{:S(2)}) collective-permute-start(f32[1,512]{1,0:T(1,128)S(1)} %get-tuple-element.18.sums0_ref), channel_id=1, source_target_pairs={{0,2},{1,3},{2,0},{3,1},{4,6},{5,7},{6,4},{7,5},{8,10},{9,11},{10,... | collective-permute-start | bytes 6152 | tf_op jit(solution)/shard_map/ppermute | solution.py:30
  29.5 6.0 %collective-permute-start.6 = (f32[1,512]{1,0:T(1,128)S(1)}, f32[1,512]{1,0:T(1,128)S(1)}, u32[]{:S(2)}, u32[]{:S(2)}) collective-permute-start(f32[1,512]{1,0:T(1,128)S(1)} %get-tuple-element.18.sums0_ref), channel_id=1, source_target_pairs={{0,1},{1,2},{2,3},{3,0},{4,5},{5,6},{6,7},{7,4},{8,9},{9,10},{10,1... | collective-permute-start | bytes 6152 | tf_op jit(solution)/shard_map/ppermute | solution.py:30
  33.6 4.5 %collective-permute-start.5 = (f32[1,512]{1,0:T(1,128)S(1)}, f32[1,512]{1,0:T(1,128)S(1)}, u32[]{:S(2)}, u32[]{:S(2)}) collective-permute-start(f32[1,512]{1,0:T(1,128)S(1)} %get-tuple-element.18.sums0_ref), channel_id=1, source_target_pairs={{0,3},{1,0},{2,1},{3,2},{4,7},{5,4},{6,5},{7,6},{8,11},{9,8},{10,9... | collective-permute-start | bytes 6152 | tf_op jit(solution)/shard_map/ppermute | solution.py:30
  34.9 3.1 %copy-start.6 = (f32[2048]{0:T(1024)S(1)}, f32[2048]{0:T(1024)}, u32[]{:S(2)}) copy-start(f32[2048]{0:T(1024)} %param.11) | copy-start | bytes 24580

commit v6 on v5

--- a/solution.py
+++ b/solution.py
@@ -136,8 +136,9 @@
         cols = pl.ds(pl.multiple_of(i * LANES, LANES), LANES)
         gain = gain_ref[0:1, cols]
         for e in range(0, rows, CHUNK):
-            norm_ref[PAD + e : PAD + e + CHUNK, :] = raw(e, cols) * scale_ref[e : e + CHUNK, :]
-        taps = [[feat_ref[s, j : j + 1, cols] * gain for j in range(FEAT_TAPS)] for s in range(3)]
+            n = (raw(e, cols) * scale_ref[e : e + CHUNK, :] * gain).astype(jnp.bfloat16)
+            norm_ref[PAD + e : PAD + e + CHUNK, :] = n.astype(jnp.float32)
+        taps = [[feat_ref[s, j : j + 1, cols] for j in range(FEAT_TAPS)] for s in range(3)]
         for e in range(0, rows, CHUNK):
             xs = [norm_ref[PAD + e : PAD + e + CHUNK, :]]
             for j in range(1, FEAT_TAPS):
@@ -229,8 +230,9 @@
         cols = pl.ds(pl.multiple_of(i * LANES, LANES), LANES)
         gain = gain_ref[0:1, cols]
         for e in range(0, ext, CHUNK):
-            norm_ref[PAD + e : PAD + e + CHUNK, :] = middle(e, cols) * scale_ref[e : e + CHUNK, :]
-        taps = [[feat_ref[s, j : j + 1, cols] * gain for j in range(FEAT_TAPS)] for s in range(3)]
+            n = (middle(e, cols) * scale_ref[e : e + CHUNK, :] * gain).astype(jnp.bfloat16)
+            norm_ref[PAD + e : PAD + e + CHUNK, :] = n.astype(jnp.float32)
+        taps = [[feat_ref[s, j : j + 1, cols] for j in range(FEAT_TAPS)] for s in range(3)]
         prods = []
         for e in range(HALO - LANES, ext, CHUNK):
             xs = [norm_ref[PAD + e : PAD + e + CHUNK, :]]
@@ -359,7 +361,7 @@
     first = (lax.axis_index("ctx") * own).astype(jnp.int32).reshape(1)
     halo = shifted(x[own - HALO :], "ctx", 1)
     part = call(sums_kernel, shape((1, own), f32), [], 1 << 20, 1 << 20)(x)
-    total = part + turned(part, "tp", 3) + turned(part, "tp", 1) + turned(part, "tp", 2)
+    total = part + turned(part, "tp", 3) + turned(part, "tp", 2) + turned(part, "tp", 1)
     before = shifted(total, "ctx", 1)
     ext = HALO + own
     off, fexp = call(
@@ -375,7 +377,7 @@
     gain = gain_se.reshape(1, width)
     mid, part_two = se_own_call(x, total, off, gain, feat_se, fexp)
     early, part_two = se_halo_call(x, halo, total, before, part_two, off, gain, feat_se, fexp)
-    sums_two = [part_two] + [turned(part_two, "tp", by) for by in (3, 1, 2)]
+    sums_two = [part_two] + [turned(part_two, "tp", by) for by in (3, 2, 1)]
     return mr_call(early, mid, *sums_two, off, gain_mr.reshape(1, width), feat_mr, base, keep)[None]
 
 

time: 44.2 us -> 44.3 us (level)
  waiting for transfers between devices: 5.11 us -> 4.19 us
  starting transfers between devices: 22.7 us -> 23.6 us
    ppermute x6, waiting for transfers between devices: 4.08 us -> 3.18 us  [turned(): return lax.ppermute(x, axis, [(i, (i + by) % peers) for i in range(peers)])]
    ppermute x6, starting transfers between devices: 17.1 us -> 17.9 us  [turned(): return lax.ppermute(x, axis, [(i, (i + by) % peers) for i in range(peers)])]
  transfers between devices with their start and end apart: 8 -> 8, of which waited for: 5 -> 4; matrix products, arithmetic and copies ran while one was open for 0% -> 0% of each run, Pallas kernels for 14% -> 14%
where the time goes in v6:
time: 44.3 us; the launch traced here: 44.1 us
  starting transfers between devices  23.6 us (53%)
  Pallas kernels  14.8 us (33%)
  waiting for transfers between devices  4.19 us (9%)
  local copies, waits for them, and re-layouts  1.35 us (3%)
    ppermute x6, starting transfers between devices, turned(): return lax.ppermute(x, axis, [(i, (i + by) % peers) for i in range(peers)])  17.9 us
    pallas_call x6, Pallas kernels, run(): pl.pallas_call(kernel, out_shape=out_shape, in_specs=specs, out_specs=jax...  14.8 us
    ppermute x2, starting transfers between devices, shifted(): return lax.ppermute(x, axis, pairs)  5.66 us
    ppermute x6, waiting for transfers between devices, turned(): return lax.ppermute(x, axis, [(i, (i + by) % peers) for i in range(peers)])  3.18 us
    slice x1, local copies, waits for them, and re-layouts, shards(): halo = shifted(x[own - HALO:], 'ctx', 1)  1.19 us
    ppermute x2, waiting for transfers between devices, shifted(): return lax.ppermute(x, axis, pairs)  1.01 us
  transfers between devices with their start and end apart: 8, of which 4 were waited for; matrix products, arithmetic and copies ran while one was open for 0% of the time, Pallas kernels for 14%

profile of v6, /device:TPU:2, one launch (start us, length us, event | category | flops | bytes accessed | tf_op | source)
XLA Modules:
  0.0 44.1 jit_solution(18257597015236366952)
XLA Ops:
  0.0 0.0 copy-start
  0.0 1.2 %slice_bitcast_fusion = bf16[144,2048]{1,0:T(8,128)(2,1)S(1)} fusion(bf16[1,256,2048]{2,1,0:T(8,128)(2,1)} %param.8), kind=kLoop, calls=%fused_computation | loop fusion | bytes 1179648 | tf_op jit(solution)/shard_map/slice | solution.py:362
  1.2 1.9 %collective-permute-start = (bf16[144,2048]{1,0:T(8,128)(2,1)S(1)}, bf16[144,2048]{1,0:T(8,128)(2,1)S(1)}, u32[]{:S(2)}, u32[]{:S(2)}) collective-permute-start(bf16[144,2048]{1,0:T(8,128)(2,1)S(1)} %slice_bitcast_fusion), channel_id=1, source_target_pairs={{0,4},{4,8},{8,12},{12,16},{16,20},{20,24},{24,28},{28,32},{32,36}... | collective-permute-start | bytes 1769480 | tf_op jit(solution)/shard_map/ppermute | solution.py:25
  3.1 0.0 copy-done
  3.1 0.0 copy-start.7
  3.1 0.0 copy-start.4
  3.2 0.3 shard_map.82
  3.4 0.0 copy-start.1
  3.5 3.3 %collective-permute-start.3 = (f32[1,256]{1,0:T(1,128)S(1)}, f32[1,256]{1,0:T(1,128)S(1)}, u32[]{:S(2)}, u32[]{:S(2)}) collective-permute-start(f32[1,256]{1,0:T(1,128)S(1)} %shard_map.82), channel_id=1, source_target_pairs={{0,1},{1,2},{2,3},{3,0},{4,5},{5,6},{6,7},{7,4},{8,9},{9,10},{10,1... | collective-permute-start | bytes 3080 | tf_op jit(solution)/shard_map/ppermute | solution.py:30
  6.8 5.4 %collective-permute-start.2 = (f32[1,256]{1,0:T(1,128)S(1)}, f32[1,256]{1,0:T(1,128)S(1)}, u32[]{:S(2)}, u32[]{:S(2)}) collective-permute-start(f32[1,256]{1,0:T(1,128)S(1)} %shard_map.82), channel_id=1, source_target_pairs={{0,2},{1,3},{2,0},{3,1},{4,6},{5,7},{6,4},{7,5},{8,10},{9,11},{10,... | collective-permute-start | bytes 3080 | tf_op jit(solution)/shard_map/ppermute | solution.py:30
  12.2 2.7 %collective-permute-start.1 = (f32[1,256]{1,0:T(1,128)S(1)}, f32[1,256]{1,0:T(1,128)S(1)}, u32[]{:S(2)}, u32[]{:S(2)}) collective-permute-start(f32[1,256]{1,0:T(1,128)S(1)} %shard_map.82), channel_id=1, source_target_pairs={{0,3},{1,0},{2,1},{3,2},{4,7},{5,4},{6,5},{7,6},{8,11},{9,8},{10,9... | collective-permute-start | bytes 3080 | tf_op jit(solution)/shard_map/ppermute | solution.py:30
  14.9 0.0 copy-done.7
  14.9 0.1 copy.9.fse_ref
  15.0 0.0 copy-done.4
  15.0 0.7 %shard_map.83 = (f32[400,128]{1,0:T(8,128)S(1)}, f32[8,2048]{1,0:T(8,128)S(1)}) custom-call(s32[1]{0:T(128)} %bitcast.2.first_ref, s32[1,128]{1,0:T(1,128)S(1)} %copy-done.4, f32[128,7]{1,0:T(8,128)S(1)} %copy.9.fse_ref), custom_call_target="tpu_custom_call" | custom-call | flops 16777216 | bytes 1048576 | tf_op jit(solution)/shard_map/pallas_call | solution.py:302
  15.7 0.0 copy-start.2
  15.7 0.0 collective-permute-done.3
  15.7 0.0 collective-permute-done.2
  15.7 1.0 %collective-permute-done.1 = f32[1,256]{1,0:T(1,128)S(1)} collective-permute-done((f32[1,256]{1,0:T(1,128)S(1)}, f32[1,256]{1,0:T(1,128)S(1)}, u32[]{:S(2)}, u32[]{:S(2)}) %collective-permute-start.1) | collective-permute-done | bytes 1056 | tf_op jit(solution)/shard_map/ppermute | solution.py:30
  16.7 3.7 %collective-permute-start.4 = (f32[1,256]{1,0:T(1,128)S(1)}, f32[1,256]{1,0:T(1,128)S(1)}, u32[]{:S(2)}, u32[]{:S(2)}) collective-permute-start(f32[1,256]{1,0:T(1,128)S(1)} %add_add_fusion.total_ref.after_ref), channel_id=1, source_target_pairs={{0,4},{4,8},{8,12},{12,16},{16,20},{20,24},{24,28},{28,32},{32,36}... | collective-permute-start | bytes 3080 | tf_op jit(solution)/shard_map/ppermute | solution.py:25
  20.4 0.0 copy-done.1
  20.4 0.0 copy-done.2
  20.4 3.8 %shard_map.84 = (bf16[256,2048]{1,0:T(8,128)(2,1)S(1)}, f32[1,256]{1,0:T(1,128)S(1)}) custom-call(bf16[256,2048]{1,0:T(8,128)(2,1)S(1)} %bitcast.8, f32[1,256]{1,0:T(1,128)S(1)} %add_add_fusion.total_ref.after_ref, f32[400,128]{1,0:T(8,128)S(1)} %get-tuple-element.13.off_ref, f32[1,2048]{1,0:T(1,128)S(1)} %bitcast.10, f32[3,3,2048]{2,1,0:T(4,128)S(1)} %copy-done.1, ...), custom_call_target="tpu_custom_call" | custom-call | flops 26214400 | bytes 2097152 | tf_op jit(solution)/shard_map/pallas_call | solution.py:302
  24.2 1.0 %collective-permute-done.4.before_ref = f32[1,256]{1,0:T(1,128)S(1)} collective-permute-done((f32[1,256]{1,0:T(1,128)S(1)}, f32[1,256]{1,0:T(1,128)S(1)}, u32[]{:S(2)}, u32[]{:S(2)}) %collective-permute-start.4) | collective-permute-done | bytes 1056 | tf_op jit(solution)/shard_map/ppermute | solution.py:25
  25.2 0.0 collective-permute-done.halo_ref
  25.3 0.0 copy-start.3
  25.3 2.7 %shard_map.85 = (bf16[160,2048]{1,0:T(8,128)(2,1)S(1)}, f32[1,512]{1,0:T(1,128)S(1)}) custom-call(bf16[256,2048]{1,0:T(8,128)(2,1)S(1)} %bitcast.9, bf16[144,2048]{1,0:T(8,128)(2,1)S(1)} %collective-permute-done.halo_ref, f32[1,256]{1,0:T(1,128)S(1)} %add_add_fusion.total_ref.after_ref, f32[1,256]{1,0:T(1,128)S(1)} %collective-permute-done.4.before_ref, ...), custom_call_target="tpu_custom_call" | custom-call | flops 26214400 | bytes 2097152 | tf_op jit(solution)/shard_map/pallas_call | solution.py:302
  27.9 0.0 copy-start.5
  27.9 1.6 %collective-permute-start.7 = (f32[1,512]{1,0:T(1,128)S(1)}, f32[1,512]{1,0:T(1,128)S(1)}, u32[]{:S(2)}, u32[]{:S(2)}) collective-permute-start(f32[1,512]{1,0:T(1,128)S(1)} %get-tuple-element.18.sums0_ref), channel_id=1, source_target_pairs={{0,1},{1,2},{2,3},{3,0},{4,5},{5,6},{6,7},{7,4},{8,9},{9,10},{10,1... | collective-permute-start | bytes 6152 | tf_op jit(solution)/shard_map/ppermute | solution.py:30
  29.5 4.0 %collective-permute-start.6 = (f32[1,512]{1,0:T(1,128)S(1)}, f32[1,512]{1,0:T(1,128)S(1)}, u32[]{:S(2)}, u32[]{:S(2)}) collective-permute-start(f32[1,512]{1,0:T(1,128)S(1)} %get-tuple-element.18.sums0_ref), channel_id=1, source_target_pairs={{0,2},{1,3},{2,0},{3,1},{4,6},{5,7},{6,4},{7,5},{8,10},{9,11},{10,... | collective-permute-start | bytes 6152 | tf_op jit(solution)/shard_map/ppermute | solution.py:30
  33.5 0.9 %collective-permute-start.5 = (f32[1,512]{1,0:T(1,128)S(1)}, f32[1,512]{1,0:T(1,128)S(1)}, u32[]{:S(2)}, u32[]{:S(2)}) collective-permute-start(f32[1,512]{1,0:T(1,128)S(1)} %get-tuple-element.18.sums0_ref), channel_id=1, source_target_pairs={{0,3},{1,0},{2,1},{3,2},{4,7},{5,4},{6,5},{7,6},{8,11},{9,8},{10,9... | collective-permute-start | bytes 6152 | tf_op jit(solution)/shard_map/ppermute | solution.py:30
  34.5 0.0 copy-done.3
  34.5 1.3 %shard_map.86 = (bf16[128,16,128]{2,1,0:T(8,128)(2,1)S(1)}, bf16[256,256]{1,0:T(8,128)(2,1)S(1)}) custom-call(f32[1,256]{1,0:T(1,128)S(1)} %add_add_fusion.total_ref.after_ref, bf16[128,128]{1,0:T(8,128)(2,1)S(1)} %copy-done.3, f32[400,128]{1,0:T(8,128)S(1)} %get-tuple-element.13.off_ref), custom_call_target="tpu_custom_call" | custom-call | flops 16777216 | bytes 1048576 | tf_op jit(solution)/shard_map/pallas_call | solution.py:302
  35.8 0.0 copy-start.6
  35.8 0.0 collective-permute-done.7.sums3_ref
  35.8 1.2 %collective-permute-done.6.sums2_ref = f32[1,512]{1,0:T(1,128)S(1)} collective-permute-done((f32[1,512]{1,0:T(1,128)S(1)}, f32[1,512]{1,0:T(1,128)S(1)}, u32[]{:S(2)}, u32[]{:S(2)}) %collective-permute-start.6) | collective-permute-done | bytes 2080 | tf_op jit(solution)/shard_map/ppermute | solution.py:30
  37.0 1.0 %collective-permute-done.5.sums1_ref = f32[1,512]{1,0:T(1,128)S(1)} collective-permute-done((f32[1,512]{1,0:T(1,128)S(1)}, f32[1,512]{1,0:T(1,128)S(1)}, u32[]{:S(2)}, u32[]{:S(2)}) %collective-permute-start.5) | collective-permute-done | bytes 2080 | tf_op jit(solution)/shard_map/ppermute | solution.py:30
  38.0 0.0 copy-done.5
  38.0 0.0 copy-done.6
  38.0 6.1 %shard_map.87 = bf16[256,2048]{1,0:T(8,128)(2,1)} custom-call(bf16[160,2048]{1,0:T(8,128)(2,1)S(1)} %get-tuple-element.16.early_ref, bf16[256,2048]{1,0:T(8,128)(2,1)S(1)} %get-tuple-element.17.mid_ref, f32[1,512]{1,0:T(1,128)S(1)} %get-tuple-element.18.sums0_ref, f32[1,512]{1,0:T(1,128)S(1)} %collective-permute-done.5.sums1_ref, ...), custom_call_target="tpu_custom_call" | custom-call | flops 1073741824 | bytes 4194304 | tf_op jit(solution)/shard_map/pallas_call | solution.py:302
  (1 shorter events, 0.0 us)
Async XLA Ops:
  0.0 3.1 %copy-start = (bf16[1,256,2048]{2,1,0:T(8,128)(2,1)S(1)}, bf16[1,256,2048]{2,1,0:T(8,128)(2,1)}, u32[]{:S(2)}) copy-start(bf16[1,256,2048]{2,1,0:T(8,128)(2,1)} %param.8) | copy-start | bytes 3145732
  1.2 24.1 %collective-permute-start = (bf16[144,2048]{1,0:T(8,128)(2,1)S(1)}, bf16[144,2048]{1,0:T(8,128)(2,1)S(1)}, u32[]{:S(2)}, u32[]{:S(2)}) collective-permute-start(bf16[144,2048]{1,0:T(8,128)(2,1)S(1)} %slice_bitcast_fusion), channel_id=1, source_target_pairs={{0,4},{4,8},{8,12},{12,16},{16,20},{20,24},{24,28},{28,32},{32,36}... | collective-permute-start | bytes 1769480 | tf_op jit(solution)/shard_map/ppermute | solution.py:25
  3.1 11.7 %copy-start.7 = (f32[128,7]{0,1:T(8,128)S(1)}, f32[128,7]{0,1:T(8,128)}, u32[]{:S(2)}) copy-start(f32[128,7]{0,1:T(8,128)} %param.14) | copy-start | bytes 10756
  3.1 11.8 %copy-start.4 = (s32[1,128]{1,0:T(1,128)S(1)}, s32[1,128]{1,0:T(1,128)}, u32[]{:S(2)}) copy-start(s32[1,128]{1,0:T(1,128)} %len_ref.1) | copy-start | bytes 1540
  3.4 17.0 %copy-start.1 = (f32[3,3,2048]{2,1,0:T(4,128)S(1)}, f32[3,3,2048]{2,1,0:T(4,128)}, u32[]{:S(2)}) copy-start(f32[3,3,2048]{2,1,0:T(4,128)} %feat_ref.4) | copy-start | bytes 221188
  3.5 12.2 %collective-permute-start.3 = (f32[1,256]{1,0:T(1,128)S(1)}, f32[1,256]{1,0:T(1,128)S(1)}, u32[]{:S(2)}, u32[]{:S(2)}) collective-permute-start(f32[1,256]{1,0:T(1,128)S(1)} %shard_map.82), channel_id=1, source_target_pairs={{0,1},{1,2},{2,3},{3,0},{4,5},{5,6},{6,7},{7,4},{8,9},{9,10},{10,1... | collective-permute-start | bytes 3080 | tf_op jit(solution)/shard_map/ppermute | solution.py:30
  6.8 8.9 %collective-permute-start.2 = (f32[1,256]{1,0:T(1,128)S(1)}, f32[1,256]{1,0:T(1,128)S(1)}, u32[]{:S(2)}, u32[]{:S(2)}) collective-permute-start(f32[1,256]{1,0:T(1,128)S(1)} %shard_map.82), channel_id=1, source_target_pairs={{0,2},{1,3},{2,0},{3,1},{4,6},{5,7},{6,4},{7,5},{8,10},{9,11},{10,... | collective-permute-start | bytes 3080 | tf_op jit(solution)/shard_map/ppermute | solution.py:30
  12.2 4.5 %collective-permute-start.1 = (f32[1,256]{1,0:T(1,128)S(1)}, f32[1,256]{1,0:T(1,128)S(1)}, u32[]{:S(2)}, u32[]{:S(2)}) collective-permute-start(f32[1,256]{1,0:T(1,128)S(1)} %shard_map.82), channel_id=1, source_target_pairs={{0,3},{1,0},{2,1},{3,2},{4,7},{5,4},{6,5},{7,6},{8,11},{9,8},{10,9... | collective-permute-start | bytes 3080 | tf_op jit(solution)/shard_map/ppermute | solution.py:30
  15.7 4.7 %copy-start.2 = (f32[2048]{0:T(1024)S(1)}, f32[2048]{0:T(1024)}, u32[]{:S(2)}) copy-start(f32[2048]{0:T(1024)} %param.10) | copy-start | bytes 24580
  16.7 8.6 %collective-permute-start.4 = (f32[1,256]{1,0:T(1,128)S(1)}, f32[1,256]{1,0:T(1,128)S(1)}, u32[]{:S(2)}, u32[]{:S(2)}) collective-permute-start(f32[1,256]{1,0:T(1,128)S(1)} %add_add_fusion.total_ref.after_ref), channel_id=1, source_target_pairs={{0,4},{4,8},{8,12},{12,16},{16,20},{20,24},{24,28},{28,32},{32,36}... | collective-permute-start | bytes 3080 | tf_op jit(solution)/shard_map/ppermute | solution.py:25
  25.3 9.2 %copy-start.3 = (bf16[128,128]{1,0:T(8,128)(2,1)S(1)}, bf16[128,128]{1,0:T(8,128)(2,1)}, u32[]{:S(2)}) copy-start(bf16[128,128]{1,0:T(8,128)(2,1)} %fmr_ref.1) | copy-start | bytes 98308
  27.9 10.1 %copy-start.5 = (f32[3,3,2048]{2,1,0:T(4,128)S(1)}, f32[3,3,2048]{2,1,0:T(4,128)}, u32[]{:S(2)}) copy-start(f32[3,3,2048]{2,1,0:T(4,128)} %feat_ref.5) | copy-start | bytes 221188
  27.9 7.9 %collective-permute-start.7 = (f32[1,512]{1,0:T(1,128)S(1)}, f32[1,512]{1,0:T(1,128)S(1)}, u32[]{:S(2)}, u32[]{:S(2)}) collective-permute-start(f32[1,512]{1,0:T(1,128)S(1)} %get-tuple-element.18.sums0_ref), channel_id=1, source_target_pairs={{0,1},{1,2},{2,3},{3,0},{4,5},{5,6},{6,7},{7,4},{8,9},{9,10},{10,1... | collective-permute-start | bytes 6152 | tf_op jit(solution)/shard_map/ppermute | solution.py:30
  29.5 7.5 %collective-permute-start.6 = (f32[1,512]{1,0:T(1,128)S(1)}, f32[1,512]{1,0:T(1,128)S(1)}, u32[]{:S(2)}, u32[]{:S(2)}) collective-permute-start(f32[1,512]{1,0:T(1,128)S(1)} %get-tuple-element.18.sums0_ref), channel_id=1, source_target_pairs={{0,2},{1,3},{2,0},{3,1},{4,6},{5,7},{6,4},{7,5},{8,10},{9,11},{10,... | collective-permute-start | bytes 6152 | tf_op jit(solution)/shard_map/ppermute | solution.py:30
  33.5 4.5 %collective-permute-start.5 = (f32[1,512]{1,0:T(1,128)S(1)}, f32[1,512]{1,0:T(1,128)S(1)}, u32[]{:S(2)}, u32[]{:S(2)}) collective-permute-start(f32[1,512]{1,0:T(1,128)S(1)} %get-tuple-element.18.sums0_ref), channel_id=1, source_target_pairs={{0,3},{1,0},{2,1},{3,2},{4,7},{5,4},{6,5},{7,6},{8,11},{9,8},{10,9... | collective-permute-start | bytes 6152 | tf_op jit(solution)/shard_map/ppermute | solution.py:30
  35.8 2.2 %copy-start.6 = (f32[2048]{0:T(1024)S(1)}, f32[2048]{0:T(1024)}, u32[]{:S(2)}) copy-start(f32[2048]{0:T(1024)} %param.11) | copy-start | bytes 24580

commit v7 on v5

--- a/solution.py
+++ b/solution.py
@@ -159,7 +159,7 @@
             acc_ref[e : e + CHUNK, :] = acc_ref[e : e + CHUNK, :] + mid * mid
         return carry
 
-    lax.fori_loop(0, width // LANES, tile, 0, unroll=2)
+    lax.fori_loop(0, width // LANES, tile, 0, unroll=4)
 
 
 def se_own_kernel(
@@ -276,15 +276,12 @@
         cols = pl.ds(pl.multiple_of(j * 2 * LANES, 2 * LANES), 2 * LANES)
         return pltpu.make_async_copy(out_ref.at[:, cols], result_ref.at[:, cols], sems.at[j])
 
-    def pair(j, carry):
-        for at in range(2):
-            i = 2 * j + at
-            ready(jnp.minimum(i + 1, tiles - 1), slots[1 - at])
-            finish(i, slots[at])
-        leave(j).start()
-        return carry
-
-    lax.fori_loop(0, tiles // 2, pair, 0, unroll=4)
+    for i in range(tiles):
+        if i + 1 < tiles:
+            ready(i + 1, slots[1 - i % 2])
+        finish(i, slots[i % 2])
+        if i % 2:
+            leave(i // 2).start()
     for j in range(tiles // 2):
         leave(j).wait()
 
@@ -359,7 +356,7 @@
     first = (lax.axis_index("ctx") * own).astype(jnp.int32).reshape(1)
     halo = shifted(x[own - HALO :], "ctx", 1)
     part = call(sums_kernel, shape((1, own), f32), [], 1 << 20, 1 << 20)(x)
-    total = part + turned(part, "tp", 3) + turned(part, "tp", 1) + turned(part, "tp", 2)
+    total = part + turned(part, "tp", 3) + turned(part, "tp", 2) + turned(part, "tp", 1)
     before = shifted(total, "ctx", 1)
     ext = HALO + own
     off, fexp = call(
@@ -375,7 +372,7 @@
     gain = gain_se.reshape(1, width)
     mid, part_two = se_own_call(x, total, off, gain, feat_se, fexp)
     early, part_two = se_halo_call(x, halo, total, before, part_two, off, gain, feat_se, fexp)
-    sums_two = [part_two] + [turned(part_two, "tp", by) for by in (3, 1, 2)]
+    sums_two = [part_two] + [turned(part_two, "tp", by) for by in (3, 2, 1)]
     return mr_call(early, mid, *sums_two, off, gain_mr.reshape(1, width), feat_mr, base, keep)[None]
 
 

time: 44.2 us -> 44.1 us (level)
  starting transfers between devices: 22.7 us -> 23.6 us
  waiting for transfers between devices: 5.11 us -> 4.25 us
    ppermute x6, waiting for transfers between devices: 4.08 us -> 3.18 us  [turned(): return lax.ppermute(x, axis, [(i, (i + by) % peers) for i in range(peers)])]
    ppermute x6, starting transfers between devices: 17.1 us -> 17.9 us  [turned(): return lax.ppermute(x, axis, [(i, (i + by) % peers) for i in range(peers)])]
  transfers between devices with their start and end apart: 8 -> 8, of which waited for: 5 -> 4; matrix products, arithmetic and copies ran while one was open for 0% -> 0% of each run, Pallas kernels for 14% -> 14%
where the time goes in v7:
time: 44.1 us; the launch traced here: 43.9 us
  starting transfers between devices  23.6 us (54%)
  Pallas kernels  14.5 us (33%)
  waiting for transfers between devices  4.25 us (10%)
  local copies, waits for them, and re-layouts  1.35 us (3%)
    ppermute x6, starting transfers between devices, turned(): return lax.ppermute(x, axis, [(i, (i + by) % peers) for i in range(peers)])  17.9 us
    pallas_call x6, Pallas kernels, run(): pl.pallas_call(kernel, out_shape=out_shape, in_specs=specs, out_specs=jax...  14.5 us
    ppermute x2, starting transfers between devices, shifted(): return lax.ppermute(x, axis, pairs)  5.66 us
    ppermute x6, waiting for transfers between devices, turned(): return lax.ppermute(x, axis, [(i, (i + by) % peers) for i in range(peers)])  3.18 us
    slice x1, local copies, waits for them, and re-layouts, shards(): halo = shifted(x[own - HALO:], 'ctx', 1)  1.19 us
    ppermute x2, waiting for transfers between devices, shifted(): return lax.ppermute(x, axis, pairs)  1.07 us
  transfers between devices with their start and end apart: 8, of which 4 were waited for; matrix products, arithmetic and copies ran while one was open for 0% of the time, Pallas kernels for 14%

profile of v7, /device:TPU:2, one launch (start us, length us, event | category | flops | bytes accessed | tf_op | source)
XLA Modules:
  0.0 43.9 jit_solution(6896668712137977022)
XLA Ops:
  0.0 0.0 copy-start
  0.0 1.2 %slice_bitcast_fusion = bf16[144,2048]{1,0:T(8,128)(2,1)S(1)} fusion(bf16[1,256,2048]{2,1,0:T(8,128)(2,1)} %param.8), kind=kLoop, calls=%fused_computation | loop fusion | bytes 1179648 | tf_op jit(solution)/shard_map/slice | solution.py:357
  1.2 1.9 %collective-permute-start = (bf16[144,2048]{1,0:T(8,128)(2,1)S(1)}, bf16[144,2048]{1,0:T(8,128)(2,1)S(1)}, u32[]{:S(2)}, u32[]{:S(2)}) collective-permute-start(bf16[144,2048]{1,0:T(8,128)(2,1)S(1)} %slice_bitcast_fusion), channel_id=1, source_target_pairs={{0,4},{4,8},{8,12},{12,16},{16,20},{20,24},{24,28},{28,32},{32,36}... | collective-permute-start | bytes 1769480 | tf_op jit(solution)/shard_map/ppermute | solution.py:25
  3.1 0.0 copy-done
  3.1 0.0 copy-start.7
  3.1 0.0 copy-start.4
  3.2 0.3 shard_map.82
  3.4 0.0 copy-start.1
  3.5 3.3 %collective-permute-start.3 = (f32[1,256]{1,0:T(1,128)S(1)}, f32[1,256]{1,0:T(1,128)S(1)}, u32[]{:S(2)}, u32[]{:S(2)}) collective-permute-start(f32[1,256]{1,0:T(1,128)S(1)} %shard_map.82), channel_id=1, source_target_pairs={{0,1},{1,2},{2,3},{3,0},{4,5},{5,6},{6,7},{7,4},{8,9},{9,10},{10,1... | collective-permute-start | bytes 3080 | tf_op jit(solution)/shard_map/ppermute | solution.py:30
  6.8 5.4 %collective-permute-start.2 = (f32[1,256]{1,0:T(1,128)S(1)}, f32[1,256]{1,0:T(1,128)S(1)}, u32[]{:S(2)}, u32[]{:S(2)}) collective-permute-start(f32[1,256]{1,0:T(1,128)S(1)} %shard_map.82), channel_id=1, source_target_pairs={{0,2},{1,3},{2,0},{3,1},{4,6},{5,7},{6,4},{7,5},{8,10},{9,11},{10,... | collective-permute-start | bytes 3080 | tf_op jit(solution)/shard_map/ppermute | solution.py:30
  12.2 2.7 %collective-permute-start.1 = (f32[1,256]{1,0:T(1,128)S(1)}, f32[1,256]{1,0:T(1,128)S(1)}, u32[]{:S(2)}, u32[]{:S(2)}) collective-permute-start(f32[1,256]{1,0:T(1,128)S(1)} %shard_map.82), channel_id=1, source_target_pairs={{0,3},{1,0},{2,1},{3,2},{4,7},{5,4},{6,5},{7,6},{8,11},{9,8},{10,9... | collective-permute-start | bytes 3080 | tf_op jit(solution)/shard_map/ppermute | solution.py:30
  14.9 0.0 copy-done.7
  14.9 0.1 copy.9.fse_ref
  15.0 0.0 copy-done.4
  15.0 0.7 %shard_map.83 = (f32[400,128]{1,0:T(8,128)S(1)}, f32[8,2048]{1,0:T(8,128)S(1)}) custom-call(s32[1]{0:T(128)} %bitcast.2.first_ref, s32[1,128]{1,0:T(1,128)S(1)} %copy-done.4, f32[128,7]{1,0:T(8,128)S(1)} %copy.9.fse_ref), custom_call_target="tpu_custom_call" | custom-call | flops 16777216 | bytes 1048576 | tf_op jit(solution)/shard_map/pallas_call | solution.py:297
  15.7 0.0 copy-start.2
  15.7 0.0 collective-permute-done.3
  15.7 0.0 collective-permute-done.2
  15.7 1.0 %collective-permute-done.1 = f32[1,256]{1,0:T(1,128)S(1)} collective-permute-done((f32[1,256]{1,0:T(1,128)S(1)}, f32[1,256]{1,0:T(1,128)S(1)}, u32[]{:S(2)}, u32[]{:S(2)}) %collective-permute-start.1) | collective-permute-done | bytes 1056 | tf_op jit(solution)/shard_map/ppermute | solution.py:30
  16.7 3.7 %collective-permute-start.4 = (f32[1,256]{1,0:T(1,128)S(1)}, f32[1,256]{1,0:T(1,128)S(1)}, u32[]{:S(2)}, u32[]{:S(2)}) collective-permute-start(f32[1,256]{1,0:T(1,128)S(1)} %add_add_fusion.total_ref.after_ref), channel_id=1, source_target_pairs={{0,4},{4,8},{8,12},{12,16},{16,20},{20,24},{24,28},{28,32},{32,36}... | collective-permute-start | bytes 3080 | tf_op jit(solution)/shard_map/ppermute | solution.py:25
  20.4 0.0 copy-done.1
  20.4 0.0 copy-done.2
  20.4 3.7 %shard_map.84 = (bf16[256,2048]{1,0:T(8,128)(2,1)S(1)}, f32[1,256]{1,0:T(1,128)S(1)}) custom-call(bf16[256,2048]{1,0:T(8,128)(2,1)S(1)} %bitcast.8, f32[1,256]{1,0:T(1,128)S(1)} %add_add_fusion.total_ref.after_ref, f32[400,128]{1,0:T(8,128)S(1)} %get-tuple-element.13.off_ref, f32[1,2048]{1,0:T(1,128)S(1)} %bitcast.10, f32[3,3,2048]{2,1,0:T(4,128)S(1)} %copy-done.1, ...), custom_call_target="tpu_custom_call" | custom-call | flops 26214400 | bytes 2097152 | tf_op jit(solution)/shard_map/pallas_call | solution.py:297
  24.2 1.1 %collective-permute-done.4.before_ref = f32[1,256]{1,0:T(1,128)S(1)} collective-permute-done((f32[1,256]{1,0:T(1,128)S(1)}, f32[1,256]{1,0:T(1,128)S(1)}, u32[]{:S(2)}, u32[]{:S(2)}) %collective-permute-start.4) | collective-permute-done | bytes 1056 | tf_op jit(solution)/shard_map/ppermute | solution.py:25
  25.2 0.0 collective-permute-done.halo_ref
  25.3 0.0 copy-start.3
  25.3 2.6 %shard_map.85 = (bf16[160,2048]{1,0:T(8,128)(2,1)S(1)}, f32[1,512]{1,0:T(1,128)S(1)}) custom-call(bf16[256,2048]{1,0:T(8,128)(2,1)S(1)} %bitcast.9, bf16[144,2048]{1,0:T(8,128)(2,1)S(1)} %collective-permute-done.halo_ref, f32[1,256]{1,0:T(1,128)S(1)} %add_add_fusion.total_ref.after_ref, f32[1,256]{1,0:T(1,128)S(1)} %collective-permute-done.4.before_ref, ...), custom_call_target="tpu_custom_call" | custom-call | flops 26214400 | bytes 2097152 | tf_op jit(solution)/shard_map/pallas_call | solution.py:297
  27.9 0.0 copy-start.5
  27.9 1.6 %collective-permute-start.7 = (f32[1,512]{1,0:T(1,128)S(1)}, f32[1,512]{1,0:T(1,128)S(1)}, u32[]{:S(2)}, u32[]{:S(2)}) collective-permute-start(f32[1,512]{1,0:T(1,128)S(1)} %get-tuple-element.18.sums0_ref), channel_id=1, source_target_pairs={{0,1},{1,2},{2,3},{3,0},{4,5},{5,6},{6,7},{7,4},{8,9},{9,10},{10,1... | collective-permute-start | bytes 6152 | tf_op jit(solution)/shard_map/ppermute | solution.py:30
  29.5 4.0 %collective-permute-start.6 = (f32[1,512]{1,0:T(1,128)S(1)}, f32[1,512]{1,0:T(1,128)S(1)}, u32[]{:S(2)}, u32[]{:S(2)}) collective-permute-start(f32[1,512]{1,0:T(1,128)S(1)} %get-tuple-element.18.sums0_ref), channel_id=1, source_target_pairs={{0,2},{1,3},{2,0},{3,1},{4,6},{5,7},{6,4},{7,5},{8,10},{9,11},{10,... | collective-permute-start | bytes 6152 | tf_op jit(solution)/shard_map/ppermute | solution.py:30
  33.5 0.9 %collective-permute-start.5 = (f32[1,512]{1,0:T(1,128)S(1)}, f32[1,512]{1,0:T(1,128)S(1)}, u32[]{:S(2)}, u32[]{:S(2)}) collective-permute-start(f32[1,512]{1,0:T(1,128)S(1)} %get-tuple-element.18.sums0_ref), channel_id=1, source_target_pairs={{0,3},{1,0},{2,1},{3,2},{4,7},{5,4},{6,5},{7,6},{8,11},{9,8},{10,9... | collective-permute-start | bytes 6152 | tf_op jit(solution)/shard_map/ppermute | solution.py:30
  34.4 0.0 copy-done.3
  34.4 1.3 %shard_map.86 = (bf16[128,16,128]{2,1,0:T(8,128)(2,1)S(1)}, bf16[256,256]{1,0:T(8,128)(2,1)S(1)}) custom-call(f32[1,256]{1,0:T(1,128)S(1)} %add_add_fusion.total_ref.after_ref, bf16[128,128]{1,0:T(8,128)(2,1)S(1)} %copy-done.3, f32[400,128]{1,0:T(8,128)S(1)} %get-tuple-element.13.off_ref), custom_call_target="tpu_custom_call" | custom-call | flops 16777216 | bytes 1048576 | tf_op jit(solution)/shard_map/pallas_call | solution.py:297
  35.7 0.0 copy-start.6
  35.8 0.0 collective-permute-done.7.sums3_ref
  35.8 1.2 %collective-permute-done.6.sums2_ref = f32[1,512]{1,0:T(1,128)S(1)} collective-permute-done((f32[1,512]{1,0:T(1,128)S(1)}, f32[1,512]{1,0:T(1,128)S(1)}, u32[]{:S(2)}, u32[]{:S(2)}) %collective-permute-start.6) | collective-permute-done | bytes 2080 | tf_op jit(solution)/shard_map/ppermute | solution.py:30
  36.9 1.0 %collective-permute-done.5.sums1_ref = f32[1,512]{1,0:T(1,128)S(1)} collective-permute-done((f32[1,512]{1,0:T(1,128)S(1)}, f32[1,512]{1,0:T(1,128)S(1)}, u32[]{:S(2)}, u32[]{:S(2)}) %collective-permute-start.5) | collective-permute-done | bytes 2080 | tf_op jit(solution)/shard_map/ppermute | solution.py:30
  38.0 0.0 copy-done.5
  38.0 0.0 copy-done.6
  38.0 5.9 %shard_map.87 = bf16[256,2048]{1,0:T(8,128)(2,1)} custom-call(bf16[160,2048]{1,0:T(8,128)(2,1)S(1)} %get-tuple-element.16.early_ref, bf16[256,2048]{1,0:T(8,128)(2,1)S(1)} %get-tuple-element.17.mid_ref, f32[1,512]{1,0:T(1,128)S(1)} %get-tuple-element.18.sums0_ref, f32[1,512]{1,0:T(1,128)S(1)} %collective-permute-done.5.sums1_ref, ...), custom_call_target="tpu_custom_call" | custom-call | flops 1073741824 | bytes 4194304 | tf_op jit(solution)/shard_map/pallas_call | solution.py:297
  (1 shorter events, 0.0 us)
Async XLA Ops:
  0.0 3.1 %copy-start = (bf16[1,256,2048]{2,1,0:T(8,128)(2,1)S(1)}, bf16[1,256,2048]{2,1,0:T(8,128)(2,1)}, u32[]{:S(2)}) copy-start(bf16[1,256,2048]{2,1,0:T(8,128)(2,1)} %param.8) | copy-start | bytes 3145732
  1.2 24.1 %collective-permute-start = (bf16[144,2048]{1,0:T(8,128)(2,1)S(1)}, bf16[144,2048]{1,0:T(8,128)(2,1)S(1)}, u32[]{:S(2)}, u32[]{:S(2)}) collective-permute-start(bf16[144,2048]{1,0:T(8,128)(2,1)S(1)} %slice_bitcast_fusion), channel_id=1, source_target_pairs={{0,4},{4,8},{8,12},{12,16},{16,20},{20,24},{24,28},{28,32},{32,36}... | collective-permute-start | bytes 1769480 | tf_op jit(solution)/shard_map/ppermute | solution.py:25
  3.1 11.7 %copy-start.7 = (f32[128,7]{0,1:T(8,128)S(1)}, f32[128,7]{0,1:T(8,128)}, u32[]{:S(2)}) copy-start(f32[128,7]{0,1:T(8,128)} %param.14) | copy-start | bytes 10756
  3.1 11.8 %copy-start.4 = (s32[1,128]{1,0:T(1,128)S(1)}, s32[1,128]{1,0:T(1,128)}, u32[]{:S(2)}) copy-start(s32[1,128]{1,0:T(1,128)} %len_ref.1) | copy-start | bytes 1540
  3.4 17.0 %copy-start.1 = (f32[3,3,2048]{2,1,0:T(4,128)S(1)}, f32[3,3,2048]{2,1,0:T(4,128)}, u32[]{:S(2)}) copy-start(f32[3,3,2048]{2,1,0:T(4,128)} %feat_ref.4) | copy-start | bytes 221188
  3.5 12.2 %collective-permute-start.3 = (f32[1,256]{1,0:T(1,128)S(1)}, f32[1,256]{1,0:T(1,128)S(1)}, u32[]{:S(2)}, u32[]{:S(2)}) collective-permute-start(f32[1,256]{1,0:T(1,128)S(1)} %shard_map.82), channel_id=1, source_target_pairs={{0,1},{1,2},{2,3},{3,0},{4,5},{5,6},{6,7},{7,4},{8,9},{9,10},{10,1... | collective-permute-start | bytes 3080 | tf_op jit(solution)/shard_map/ppermute | solution.py:30
  6.8 8.9 %collective-permute-start.2 = (f32[1,256]{1,0:T(1,128)S(1)}, f32[1,256]{1,0:T(1,128)S(1)}, u32[]{:S(2)}, u32[]{:S(2)}) collective-permute-start(f32[1,256]{1,0:T(1,128)S(1)} %shard_map.82), channel_id=1, source_target_pairs={{0,2},{1,3},{2,0},{3,1},{4,6},{5,7},{6,4},{7,5},{8,10},{9,11},{10,... | collective-permute-start | bytes 3080 | tf_op jit(solution)/shard_map/ppermute | solution.py:30
  12.2 4.5 %collective-permute-start.1 = (f32[1,256]{1,0:T(1,128)S(1)}, f32[1,256]{1,0:T(1,128)S(1)}, u32[]{:S(2)}, u32[]{:S(2)}) collective-permute-start(f32[1,256]{1,0:T(1,128)S(1)} %shard_map.82), channel_id=1, source_target_pairs={{0,3},{1,0},{2,1},{3,2},{4,7},{5,4},{6,5},{7,6},{8,11},{9,8},{10,9... | collective-permute-start | bytes 3080 | tf_op jit(solution)/shard_map/ppermute | solution.py:30
  15.7 4.7 %copy-start.2 = (f32[2048]{0:T(1024)S(1)}, f32[2048]{0:T(1024)}, u32[]{:S(2)}) copy-start(f32[2048]{0:T(1024)} %param.10) | copy-start | bytes 24580
  16.7 8.6 %collective-permute-start.4 = (f32[1,256]{1,0:T(1,128)S(1)}, f32[1,256]{1,0:T(1,128)S(1)}, u32[]{:S(2)}, u32[]{:S(2)}) collective-permute-start(f32[1,256]{1,0:T(1,128)S(1)} %add_add_fusion.total_ref.after_ref), channel_id=1, source_target_pairs={{0,4},{4,8},{8,12},{12,16},{16,20},{20,24},{24,28},{28,32},{32,36}... | collective-permute-start | bytes 3080 | tf_op jit(solution)/shard_map/ppermute | solution.py:25
  25.3 9.2 %copy-start.3 = (bf16[128,128]{1,0:T(8,128)(2,1)S(1)}, bf16[128,128]{1,0:T(8,128)(2,1)}, u32[]{:S(2)}) copy-start(bf16[128,128]{1,0:T(8,128)(2,1)} %fmr_ref.1) | copy-start | bytes 98308
  27.9 10.1 %copy-start.5 = (f32[3,3,2048]{2,1,0:T(4,128)S(1)}, f32[3,3,2048]{2,1,0:T(4,128)}, u32[]{:S(2)}) copy-start(f32[3,3,2048]{2,1,0:T(4,128)} %feat_ref.5) | copy-start | bytes 221188
  27.9 7.9 %collective-permute-start.7 = (f32[1,512]{1,0:T(1,128)S(1)}, f32[1,512]{1,0:T(1,128)S(1)}, u32[]{:S(2)}, u32[]{:S(2)}) collective-permute-start(f32[1,512]{1,0:T(1,128)S(1)} %get-tuple-element.18.sums0_ref), channel_id=1, source_target_pairs={{0,1},{1,2},{2,3},{3,0},{4,5},{5,6},{6,7},{7,4},{8,9},{9,10},{10,1... | collective-permute-start | bytes 6152 | tf_op jit(solution)/shard_map/ppermute | solution.py:30
  29.5 7.5 %collective-permute-start.6 = (f32[1,512]{1,0:T(1,128)S(1)}, f32[1,512]{1,0:T(1,128)S(1)}, u32[]{:S(2)}, u32[]{:S(2)}) collective-permute-start(f32[1,512]{1,0:T(1,128)S(1)} %get-tuple-element.18.sums0_ref), channel_id=1, source_target_pairs={{0,2},{1,3},{2,0},{3,1},{4,6},{5,7},{6,4},{7,5},{8,10},{9,11},{10,... | collective-permute-start | bytes 6152 | tf_op jit(solution)/shard_map/ppermute | solution.py:30
  33.5 4.5 %collective-permute-start.5 = (f32[1,512]{1,0:T(1,128)S(1)}, f32[1,512]{1,0:T(1,128)S(1)}, u32[]{:S(2)}, u32[]{:S(2)}) collective-permute-start(f32[1,512]{1,0:T(1,128)S(1)} %get-tuple-element.18.sums0_ref), channel_id=1, source_target_pairs={{0,3},{1,0},{2,1},{3,2},{4,7},{5,4},{6,5},{7,6},{8,11},{9,8},{10,9... | collective-permute-start | bytes 6152 | tf_op jit(solution)/shard_map/ppermute | solution.py:30
  35.7 2.2 %copy-start.6 = (f32[2048]{0:T(1024)S(1)}, f32[2048]{0:T(1024)}, u32[]{:S(2)}) copy-start(f32[2048]{0:T(1024)} %param.11) | copy-start | bytes 24580
